TPU v7x, 512 devices: a whole 4x4x16 slice. The times are simulated.
512 devices in a mesh: seq: 64 (over x, z_hi, y), head: 8 (over z_lo, core).
Axes of the slice: x: 4, y: 4, z: 16 (z_hi: 4, z_lo: 4; z = z_hi * 4 + z_lo), core: 2. Of those that a mesh axis runs over, the one named last changes fastest.
Arguments:
- tokens: bfloat16 [16384, 2048], P('seq'), may hold values from -16 to 16
- latents: bfloat16 [512, 2048], P(None, 'seq'), may hold values from -6 to 6
- w_query: bfloat16 [2048, 2048], P('seq', 'head'), may hold values from -0.125 to 0.125
- w_key: bfloat16 [2048, 2048], P(None, 'head'), may hold values from -0.125 to 0.125
- w_value: bfloat16 [2048, 2048], P(None, 'head'), may hold values from -0.125 to 0.125
- cotangent: bfloat16 [512, 2048], P(None, 'head'), may hold values from -384 to 384
Outputs:
- token_grad: bfloat16 [16384, 2048], P('seq', 'head')
- latent_grad: float32 [512, 2048], P(None, 'seq')
- query_weight_grad: float32 [2048, 2048], P('seq', 'head')
- key_weight_grad: float32 [2048, 2048], P('seq', 'head')
- value_weight_grad: float32 [2048, 2048], P('seq', 'head')
All inputs are finite; a program needn't handle non-finite values.
Results may differ from a plain program's by a relative error of at most 0.015.
The roundings to bfloat16 on the way count: a program that leaves them out, or rounds other values in their place, can miss the bound.
Values may be sent and summed in bfloat16 or wider, within the bound.
No kernel may reach another device: no remote copies, remote signals or barrier semaphores. Data moves between devices by JAX's collectives and lax.ppermute only.
A program may use at most 64 MiB of HBM per device.

v0:
```python
import jax
import jax.numpy as jnp
from jax import lax
from jax.sharding import PartitionSpec as P

HEAD_DIM = 128


def on_device(tokens, latents, w_query, w_key, w_value, cotangent):
    rows = tokens.shape[0]
    lat_rows = latents.shape[0]
    width = w_key.shape[1]
    local_heads = width // HEAD_DIM
    scale = HEAD_DIM ** (-0.5)
    query_part = jnp.dot(latents, w_query, preferred_element_type=jnp.float32)
    query = lax.psum(query_part, "seq").astype(jnp.bfloat16)
    keys = jnp.dot(tokens, w_key, preferred_element_type=jnp.float32).astype(jnp.bfloat16)
    values = jnp.dot(tokens, w_value, preferred_element_type=jnp.float32).astype(jnp.bfloat16)
    query_3d = query.reshape(lat_rows, local_heads, HEAD_DIM)
    keys_3d = keys.reshape(rows, local_heads, HEAD_DIM)
    values_3d = values.reshape(rows, local_heads, HEAD_DIM)
    cot_3d = cotangent.reshape(lat_rows, local_heads, HEAD_DIM)
    total_rows = rows * lax.axis_size("seq")
    pos_t = lax.axis_index("seq") * rows + jnp.arange(rows, dtype=jnp.int32)
    pos_q = total_rows - lat_rows + jnp.arange(lat_rows, dtype=jnp.int32)
    visible = pos_t[None, :] <= pos_q[:, None]
    scores = (
        jnp.einsum("ihd,thd->hit", query_3d, keys_3d, preferred_element_type=jnp.float32) * scale
    )
    expo = jnp.where(visible[None], jnp.exp(scores), jnp.float32(0.0))
    dprob = jnp.einsum("ihd,thd->hit", cot_3d, values_3d, preferred_element_type=jnp.float32)
    denom, numer = lax.psum((jnp.sum(expo, axis=2), jnp.sum(expo * dprob, axis=2)), "seq")
    probs = expo / denom[:, :, None]
    delta = numer / denom
    score_grad = (probs * (dprob - delta[:, :, None]) * scale).astype(jnp.bfloat16)
    query_grad_part = jnp.einsum(
        "hit,thd->ihd", score_grad, keys_3d, preferred_element_type=jnp.float32
    ).reshape(lat_rows, width)
    query_grad = lax.psum(query_grad_part, "seq").astype(jnp.bfloat16)
    key_grad = (
        jnp.einsum("hit,ihd->thd", score_grad, query_3d, preferred_element_type=jnp.float32)
        .astype(jnp.bfloat16)
        .reshape(rows, width)
    )
    value_grad = (
        jnp.einsum(
            "hit,ihd->thd", probs.astype(jnp.bfloat16), cot_3d, preferred_element_type=jnp.float32
        )
        .astype(jnp.bfloat16)
        .reshape(rows, width)
    )
    both_grads = jnp.concatenate([key_grad, value_grad], axis=1)
    weight_grads = lax.psum_scatter(
        lax.dot_general(
            tokens, both_grads, (((0,), (0,)), ((), ())), preferred_element_type=jnp.float32
        ),
        "seq",
        scatter_dimension=0,
        tiled=True,
    )
    key_weight_grad = weight_grads[:, :width]
    value_weight_grad = weight_grads[:, width:]
    query_weight_grad = lax.dot_general(
        latents, query_grad, (((0,), (0,)), ((), ())), preferred_element_type=jnp.float32
    )
    latent_part = lax.dot_general(
        query_grad, w_query, (((1,), (1,)), ((), ())), preferred_element_type=jnp.float32
    )
    latent_grad = lax.psum(latent_part.astype(jnp.bfloat16), "head").astype(jnp.float32)
    joined_weights = jnp.concatenate([w_key, w_value], axis=1)
    token_part = lax.dot_general(
        both_grads, joined_weights, (((1,), (1,)), ((), ())), preferred_element_type=jnp.float32
    )
    received = lax.all_to_all(
        token_part[None].astype(jnp.bfloat16), "head", split_axis=2, concat_axis=0, tiled=True
    ).astype(jnp.float32)
    token_grad = jnp.sum(received, axis=0)
    return (
        token_grad.astype(jnp.bfloat16),
        latent_grad,
        query_weight_grad,
        key_weight_grad,
        value_weight_grad,
    )


def solution(mesh):
    placed = (
        P("seq", None),
        P(None, "seq"),
        P("seq", "head"),
        P(None, "head"),
        P(None, "head"),
        P(None, "head"),
    )
    return jax.shard_map(
        on_device,
        mesh=mesh,
        in_specs=placed,
        out_specs=(
            P("seq", "head"),
            P(None, "seq"),
            P("seq", "head"),
            P("seq", "head"),
            P("seq", "head"),
        ),
        check_vma=False,
    )
```

profile of v0, /device:TPU:1, one launch (start us, length us, event | category | flops | bytes accessed | tf_op | source)
XLA Modules:
  0.0 1231.8 jit_solution(18198518346624488725)
XLA Ops:
  7.2 0.0 copy-start
  7.2 0.0 copy-start.3
  7.2 0.0 reduce-scatter.4.cloned.1.call-start
  7.3 1.1 copy-done
  8.4 0.0 copy-start.7
  8.4 0.0 copy-start.8
  8.4 0.0 copy-start.12
  8.4 1.8 convolution_convert_fusion.4
  10.2 0.0 copy-done.3
  10.2 0.5 convolution_convert_fusion.3
  10.7 0.0 copy-done.7
  10.7 0.1 copy.70
  10.9 0.0 copy-done.8
  10.9 0.0 copy-done.12
  10.9 0.0 copy-start.6
  10.9 0.2 fusion.12
  11.2 392.7 %all-reduce.3 = bf16[512,256]{1,0:T(8,128)(2,1)S(1)} all-reduce(f32[512,256]{1,0:T(8,128)S(1)} %fusion.12), channel_id=1, replica_groups=mesh['seq'=64,'head'=8] {'seq'}, use_global_device_ids=true, to_apply=%region_0.0 | all-reduce | flops 131072 | bytes 786432 | tf_op jit(solution)/shard_map/psum | solution.py:16
  403.8 0.1 copy.69
  404.0 0.1 broadcast_compare_fusion
  404.1 0.3 convolution_bitcast_fusion.1
  404.5 0.0 copy-done.6
  404.5 1.2 multiply_reduce_fusion
  405.6 191.3 %all-reduce = (f32[2,512]{1,0:T(2,128)}, f32[2,512]{1,0:T(2,128)}) all-reduce(f32[2,512]{1,0:T(2,128)} %get-tuple-element.26, f32[2,512]{1,0:T(2,128)} %get-tuple-element.25), channel_id=1, replica_groups=mesh['seq'=64,'head'=8] {'seq'}, use_global_device_ids=true, to_apply=%region_2.3 | all-reduce | flops 2048 | bytes 16384 | tf_op jit(solution)/shard_map/psum | solution.py:32
  596.9 0.0 copy-start.13
  596.9 0.0 copy-start.14
  596.9 1.3 convolution_convert_fusion.1
  598.2 0.0 copy-start.10
  598.2 0.0 copy-done.13
  598.3 0.0 copy-done.14
  598.3 0.2 multiply_convert_fusion
  598.5 0.0 copy-start.1
  598.5 0.8 copy-done.1
  599.4 0.3 convolution_convert_fusion.2
  599.7 0.0 copy-done.10
  599.7 2.7 convolution_bitcast_fusion
  602.4 5.3 copy.64
  607.7 0.0 copy-start.4
  607.7 0.0 copy-start.5
  607.7 0.0 copy-start.11
  607.8 0.0 reduce-scatter.4.cloned.1.call-update
  607.8 1.2 copy-done.4
  609.0 0.3 copy-done.5
  609.3 0.0 copy-done.11
  609.3 1.7 fusion
  611.0 4.6 copy.54
  615.6 0.5 broadcast.34
  616.1 11.6 reduce.4
  627.8 0.0 copy-start.2
  627.8 2.2 reshape.79
  630.0 86.7 %all-to-all-start = ((bf16[8,2,32768]{2,1,0:T(2,128)(2,1)}), bf16[8,2,32768]{2,1,0:T(2,128)(2,1)}, u32[]{:S(2)}, u32[]{:S(2)}) async-start(bf16[8,2,32768]{2,1,0:T(2,128)(2,1)} %reshape.79), calls=%async_computation | async-start | bytes 2097152 | tf_op jit(solution)/shard_map/all_to_all | solution.py:74
  716.7 0.0 copy-done.2
  716.7 0.2 fusion.13
  716.9 410.1 %all-reduce.4 = bf16[512,256]{0,1:T(8,128)(2,1)S(1)} all-reduce(f32[512,256]{0,1:T(8,128)S(1)} %bitcast.50), channel_id=1, replica_groups=mesh['seq'=64,'head'=8] {'seq'}, use_global_device_ids=true, to_apply=%region_6.7 | all-reduce | flops 131072 | bytes 786432 | tf_op jit(solution)/shard_map/psum | solution.py:39
  1127.0 0.1 convolution_convert_fusion.5
  1127.1 87.4 %psum.39 = bf16[512,32]{0,1:T(8,128)(2,1)S(1)} all-reduce(bf16[512,32]{0,1:T(8,128)(2,1)S(1)} %convolution_convert_fusion.5), channel_id=1, replica_groups=mesh['seq'=64,'head'=8] {'head'}, use_global_device_ids=true, to_apply=%region_7.8 | all-reduce | flops 16384 | bytes 65536 | tf_op jit(solution)/shard_map/psum | solution.py:69
  1214.5 0.6 convert_element_type.57
  1215.1 0.0 copy-done.9
  1215.1 0.8 convolution_bitcast_fusion.2
  1216.0 0.0 all-to-all-done
  1216.0 4.3 reshape.80
  1220.3 1.1 copy.66
  1221.4 1.4 reduce_sum.32
  1222.8 0.8 copy.56
  1223.5 1.4 fusion.11
  (5 shorter events, 0.0 us)
Async XLA Ops:
  7.2 1.2 copy-start
  7.2 3.0 copy-start.3
  7.2 1216.4 %reduce-scatter.4.cloned.1.call-start = ((), (), s32[]{:S(2)}) async-start(), calls=%async_computation.2 | async-start | bytes 4259840
  8.4 2.3 copy-start.7
  8.4 2.5 copy-start.8
  8.4 2.5 copy-start.12
  10.9 393.6 %copy-start.6 = (bf16[512,256]{0,1:T(8,128)(2,1)}, bf16[512,256]{0,1:T(8,128)(2,1)S(1)}, u32[]{:S(2)}) copy-start(bf16[512,256]{0,1:T(8,128)(2,1)S(1)} %copy.70) | copy-start | bytes 786436
  596.9 1.3 copy-start.13
  596.9 1.3 copy-start.14
  598.2 1.5 copy-start.10
  598.5 0.8 copy-start.1
  607.7 1.2 copy-start.4
  607.7 1.5 copy-start.5
  607.7 1.5 copy-start.11
  627.8 88.9 %copy-start.2 = (bf16[2,512,256]{1,2,0:T(8,128)(2,1)S(1)}, bf16[2,512,256]{1,2,0:T(8,128)(2,1)}, u32[]{:S(2)}) copy-start(bf16[2,512,256]{1,2,0:T(8,128)(2,1)} %copy-done.1) | copy-start | bytes 1572868
  630.0 585.2 %copy-start.9 = (bf16[512,32]{0,1:T(8,128)(2,1)S(1)}, bf16[512,32]{0,1:T(8,128)(2,1)}, u32[]{:S(2)}) copy-start(bf16[512,32]{0,1:T(8,128)(2,1)} %param.7) | copy-start | bytes 98308
  630.0 586.0 %all-to-all-start = ((bf16[8,2,32768]{2,1,0:T(2,128)(2,1)}), bf16[8,2,32768]{2,1,0:T(2,128)(2,1)}, u32[]{:S(2)}, u32[]{:S(2)}) async-start(bf16[8,2,32768]{2,1,0:T(2,128)(2,1)} %reshape.79), calls=%async_computation | async-start | bytes 2097152 | tf_op jit(solution)/shard_map/all_to_all | solution.py:74
Sparse Core Ops, SparseCore 0:
  607.9 485.4 reduce-scatter.3
where the time goes:
time: 1230 us
  blocking collectives  1080 us (88%)
  starting transfers between devices  86.7 us (7%)
  local copies, waits for them, and re-layouts  24.1 us (2%)
  between operations  14.3 us (1%)
  other arithmetic  14 us (1%)
    psum x1, blocking collectives, on_device(): query_grad = lax.psum(query_grad_part, 'seq').astype(jnp.bfloat16)  410 us
    psum x1, blocking collectives, on_device(): query = lax.psum(query_part, 'seq').astype(jnp.bfloat16)  393 us
    psum x1, blocking collectives, on_device(): lax.psum((jnp.sum(expo, axis=2), jnp.sum(expo * dprob, axis=2)), 'seq')  191 us
    psum x1, blocking collectives, on_device(): lax.psum(latent_part.astype(jnp.bfloat16), 'head').astype(jnp.float32)  87.4 us
    all_to_all x1, starting transfers between devices, on_device(): lax.all_to_all(token_part[None].astype(jnp.bfloat16), 'head', split_axis=...  86.7 us
  transfers between devices with their start and end apart: 2, of which 0 were waited for; matrix products, arithmetic and copies ran while one was open for 2% of the time, Pallas kernels for 0%

commit v1 on v0

v1 whole, which is shorter than its diff:
```python
import jax
import jax.numpy as jnp
from jax import lax
from jax.experimental import pallas as pl
from jax.experimental.pallas import tpu as pltpu
from jax.sharding import Mesh
from jax.sharding import PartitionSpec as P

HEAD_DIM = 128
SCALE = HEAD_DIM ** (-0.5)
SEQ = ("x", "w", "y")
HEAD = ("z", "c")
NEAR = ("x", "y")
F32 = jnp.float32
BF16 = jnp.bfloat16
SMEM = pl.BlockSpec(memory_space=pltpu.SMEM)
HBM = pl.BlockSpec(memory_space=pl.ANY)
NT = (((1,), (1,)), ((), ()))
MIB = 1024 * 1024
SHRINK = 2.0**-12


def dot(a, b):
    return jnp.dot(a, b, preferred_element_type=F32)


def dot_nt(a, b):
    return lax.dot_general(a, b, NT, preferred_element_type=F32)


def shape(dims, dtype):
    return jax.ShapeDtypeStruct(dims, dtype)


def whole(array):
    rank = len(array.shape)
    return pl.BlockSpec(array.shape, lambda i: (0,) * rank)


def local(body, outs, args, flops=0, specs=None, grid=1, out_specs=None, scratch=(), limit=16):
    specs = specs or {}
    moved = sum(a.size * a.dtype.itemsize for a in list(args) + list(outs))
    return pl.pallas_call(
        body,
        out_shape=outs,
        grid=(grid,),
        in_specs=[specs.get(i) or whole(a) for i, a in enumerate(args)],
        out_specs=out_specs or [whole(o) for o in outs],
        scratch_shapes=list(scratch),
        compiler_params=pltpu.CompilerParams(vmem_limit_bytes=limit * MIB),
        cost_estimate=pl.CostEstimate(flops=flops, bytes_accessed=moved, transcendentals=0),
    )(*args)


def exchange(blocks, axes):
    return lax.all_to_all(blocks, axes, split_axis=0, concat_axis=0, tiled=True)


def partner(value, axis, flip):
    size = lax.axis_size(axis)
    return lax.ppermute(value, axis, [(i, i ^ flip) for i in range(size)])


def summed(blocks):
    acc = blocks[0].astype(F32)
    for j in range(1, blocks.shape[0]):
        acc = acc + blocks[j].astype(F32)
    return acc


def sum_kernel(blocks, out):
    acc = summed(blocks).astype(out.dtype)
    for j in range(out.shape[0]):
        out[j] = acc


def sum_copies(blocks, count, dtype):
    (out,) = local(sum_kernel, [shape((count,) + blocks.shape[1:], dtype)], [blocks])
    return out


def total_kernel(blocks, out):
    out[...] = summed(blocks)


def query_kernel(w_query, latents_t, out):
    part = lax.dot_general(
        w_query[...], latents_t[...], (((0,), (0,)), ((), ())), preferred_element_type=F32
    )
    n, each, _ = out.shape
    for j in range(n):
        out[j] = part[j * each : (j + 1) * each]


def prepare_kernel(place, tokens, w_key, w_value, keys, keys_t, values, tokens_t, other_t, own_t):
    key = dot(tokens[...], w_key[...])
    keys[...] = key.astype(BF16)
    keys_t[...] = key.T.astype(BF16)
    values[...] = dot(tokens[...], w_value[...]).astype(BF16)
    for x in range(4):
        for w in range(4):
            at = (x * 4 + w) * 128
            slab = tokens[:, at : at + 128].T
            for y in range(4):
                tokens_t[x * 4 + y, w * 32 : (w + 1) * 32, :] = slab[y * 32 : (y + 1) * 32, :]
    z, c = place[2], place[3]
    hops, depth, cols = own_t.shape
    half = depth // 2
    for k in range(hops):
        for core, out in ((c, own_t), (1 - c, other_t)):
            rows = pl.ds(pl.multiple_of(((z ^ k) * 2 + core) * cols, cols), cols)
            out[k, :half, :] = w_key[rows, :].T
            out[k, half:, :] = w_value[rows, :].T


def expo_of(place, h, query_t, keys):
    rows, lats = keys.shape[0], query_t.shape[1]
    cols = slice(h * HEAD_DIM, (h + 1) * HEAD_DIM)
    pos_t = place[0] * rows + lax.broadcasted_iota(jnp.int32, (rows, lats), 0)
    pos_q = place[1] + lax.broadcasted_iota(jnp.int32, (rows, lats), 1)
    scores = dot(keys[:, cols], query_t[cols, :]) * SCALE
    return jnp.where(pos_t <= pos_q, jnp.exp(scores), 0.0)


def dprob_of(h, values, cot):
    cols = slice(h * HEAD_DIM, (h + 1) * HEAD_DIM)
    return dot_nt(values[:, cols], cot[:, cols])


def split(value):
    high = value.astype(BF16)
    return high, (value - high.astype(F32)).astype(BF16)


def dot_split(a, value):
    high, low = split(value)
    return dot(a, high) + dot(a, low)


def expo_kernel(place, query_t, keys, keys_t, values, cot, spread):
    heads = keys.shape[1] // HEAD_DIM
    n = spread.shape[0]
    each = keys.shape[1] // n
    per_head = n // heads
    sums = []
    for h in range(heads):
        cols = slice(h * HEAD_DIM, (h + 1) * HEAD_DIM)
        expo = expo_of(place, h, query_t, keys)
        weighted = expo * (dprob_of(h, values, cot) * SHRINK)
        sums.append(jnp.sum(expo, axis=0, keepdims=True))
        sums.append(jnp.sum(weighted, axis=0, keepdims=True))
        first = dot_split(keys_t[cols, :], weighted)
        second = dot_split(keys_t[cols, :], expo)
        for j in range(per_head):
            rows = slice(j * each, (j + 1) * each)
            spread[h * per_head + j, :each, :] = first[rows, :]
            spread[h * per_head + j, each : 2 * each, :] = second[rows, :]
    packed = jnp.concatenate(sums + sums, axis=0)
    for j in range(n):
        spread[j, 2 * each :, :] = packed


def grad_kernel(place, sums4, query_t, keys, values, cot, tokens_hbm, blocks, both, tokens_t, sem):
    fetch = pltpu.make_async_copy(tokens_hbm, tokens_t, sem)
    fetch.start()
    heads = keys.shape[1] // HEAD_DIM
    sums = summed(sums4)
    n, held, _ = blocks.shape
    depth = tokens_t.shape[1]
    each = held - depth
    denoms, deltas = [], []
    for h in range(heads):
        cols = slice(h * HEAD_DIM, (h + 1) * HEAD_DIM)
        at = 2 * each + 2 * h
        denom = sums[at : at + 1, :]
        shrunk = sums[at + 1 : at + 2, :] / denom
        delta = shrunk * (1.0 / SHRINK)
        denoms.append(denom)
        deltas.append(shrunk)
        probs = expo_of(place, h, query_t, keys) / denom
        grad = (probs * (dprob_of(h, values, cot) - delta) * SCALE).astype(BF16)
        both[:, cols] = dot_nt(grad, query_t[cols, :]).astype(BF16)
        value_cols = slice((heads + h) * HEAD_DIM, (heads + h + 1) * HEAD_DIM)
        both[:, value_cols] = dot(probs.astype(BF16), cot[:, cols]).astype(BF16)
    first_head = place[4] * heads < n
    denom = jnp.where(first_head, denoms[0], denoms[1])
    shrunk = jnp.where(first_head, deltas[0], deltas[1])
    query_grad = (sums[:each] - shrunk * sums[each : 2 * each]) / denom * (SCALE / SHRINK)
    query_grad = query_grad.astype(BF16)
    fetch.wait()
    tall = 4
    for j in range(0, n, tall):
        part = dot(tokens_t[j : j + tall].reshape(tall * depth, -1), both[...]).astype(BF16)
        for i in range(tall):
            blocks[j + i, :depth, :] = part[i * depth : (i + 1) * depth]
            blocks[j + i, depth:, :] = query_grad


def other_kernel(both, weights, other):
    for k in range(other.shape[0]):
        other[k] = dot(both[...], weights[k]).astype(BF16)


def pair_kernel(both, weights, other, here, *away):
    here[...] = dot(both[...], weights[0]) + other[0].astype(F32)
    for k, out in enumerate(away):
        out[...] = (dot(both[...], weights[k + 1]) + other[k + 1].astype(F32)).astype(BF16)


def token_sum_kernel(here, one, two, three, out):
    total = here[...] + one[...].astype(F32) + two[...].astype(F32) + three[...].astype(F32)
    out[...] = total.astype(BF16)


def near_sum_kernel(arrived, out):
    acc = summed(arrived)
    share = out.shape[1]
    for w in range(out.shape[0]):
        out[w] = acc[w * share : (w + 1) * share].astype(BF16)


def far_sum_kernel(arrived, key_weight, value_weight):
    width = key_weight.shape[1]
    acc = summed(arrived)
    key_weight[...] = acc[:, :width]
    value_weight[...] = acc[:, width:]


def on_device(tokens, latents, w_query, w_key, w_value, cotangent):
    rows, depth = tokens.shape
    lats = latents.shape[0]
    width = w_key.shape[1]
    heads = width // HEAD_DIM
    near, far = lax.axis_size(NEAR), lax.axis_size("w")
    n_seq = lax.axis_size(SEQ)
    n_head = lax.axis_size(HEAD)
    share = depth // n_seq
    each = width // near
    z, c = lax.axis_index("z"), lax.axis_index("c")
    place = jnp.stack([lax.axis_index(SEQ), rows * n_seq - lats, z, c, lax.axis_index(NEAR)])
    place = place.astype(jnp.int32)
    scalars = {0: SMEM}

    (query_part,) = local(
        query_kernel, [shape((near, each, lats), F32)], [w_query, latents.T], 2 * share * width * lats
    )
    query_part = exchange(query_part, NEAR)
    query_part = exchange(sum_copies(query_part, far, F32), "w")
    query_t = exchange(sum_copies(query_part, near, BF16), NEAR).reshape(width, lats)

    block = depth // n_head
    hops = n_head // 2
    keys, keys_t, values, tokens_t, other_t, own_t = local(
        prepare_kernel,
        [
            shape((rows, width), BF16),
            shape((width, rows), BF16),
            shape((rows, width), BF16),
            shape((near, depth // near, rows), BF16),
            shape((hops, 2 * width, block), BF16),
            shape((hops, 2 * width, block), BF16),
        ],
        [place, tokens, w_key, w_value],
        2 * rows * depth * 2 * width,
        specs=scalars,
        limit=60,
    )

    (spread,) = local(
        expo_kernel,
        [shape((near, 2 * each + 4 * heads, lats), F32)],
        [place, query_t, keys, keys_t, values, cotangent],
        12 * rows * width * lats,
        specs=scalars,
        limit=60,
    )
    sums = exchange(sum_copies(exchange(spread, NEAR), far, F32), "w")

    blocks, both = local(
        grad_kernel,
        [shape((near, depth // near + each, 2 * width), BF16), shape((rows, 2 * width), BF16)],
        [place, sums, query_t, keys, values, cotangent, tokens_t],
        8 * rows * width * lats + 2 * rows * depth * 2 * width,
        specs={0: SMEM, 6: HBM},
        scratch=[pltpu.VMEM(tokens_t.shape, BF16), pltpu.SemaphoreType.DMA(())],
        limit=60,
    )
    arrived = exchange(blocks, NEAR)

    (other,) = local(
        other_kernel,
        [shape((hops, rows, block), BF16)],
        [both, other_t],
        rows * depth * 2 * width,
        limit=60,
    )
    here, *away = local(
        pair_kernel,
        [shape((rows, block), F32)] + [shape((rows, block), BF16)] * (hops - 1),
        [both, own_t, partner(other, "c", 1)],
        rows * depth * 2 * width,
        limit=60,
    )
    parts = [partner(part, "z", k + 1) for k, part in enumerate(away)]
    arrived, here, *parts = lax.optimization_barrier((arrived, here, *parts))
    (token_grad,) = local(token_sum_kernel, [shape((rows, block), BF16)], [here, *parts], limit=60)

    query_grad_t = arrived[:, depth // near :, :].reshape(width, lats)
    latent_grad_t = dot(w_query, query_grad_t)
    query_weight_grad = lax.dot_general(
        latents, query_grad_t, (((0,), (1,)), ((), ())), preferred_element_type=F32
    )
    (sent,) = local(
        near_sum_kernel,
        [shape((far, share, 2 * width), BF16)],
        [arrived],
        specs={0: pl.BlockSpec((near, depth // near, 2 * width), lambda i: (0, 0, 0))},
    )
    key_weight_grad, value_weight_grad = local(
        far_sum_kernel, [shape((share, width), F32)] * 2, [exchange(sent, "w")]
    )
    for axis, flip in (("c", 1), ("z", 1), ("z", 2)):
        latent_grad_t = latent_grad_t + partner(latent_grad_t, axis, flip)
    return (
        token_grad,
        latent_grad_t.T,
        query_weight_grad,
        key_weight_grad,
        value_weight_grad,
    )


def solution(mesh):
    fine = Mesh(mesh.devices.reshape(4, 4, 4, 4, 2), ("x", "w", "y", "z", "c"))
    placed = (
        P(SEQ, None),
        P(None, SEQ),
        P(SEQ, HEAD),
        P(None, HEAD),
        P(None, HEAD),
        P(None, HEAD),
    )
    return jax.shard_map(
        on_device,
        mesh=fine,
        in_specs=placed,
        out_specs=(
            P(SEQ, HEAD),
            P(None, SEQ),
            P(SEQ, HEAD),
            P(SEQ, HEAD),
            P(SEQ, HEAD),
        ),
        check_vma=False,
    )
```

time: 1230 us -> 176 us (0.14)
  the two profiles are of different devices: /device:TPU:1 before, /device:TPU:8 now
where the time goes in v1:
time: 176 us; the launch traced here: 175 us
  blocking collectives  85.7 us (49%)
  starting transfers between devices  38.5 us (22%)
  waiting for transfers between devices  22.6 us (13%)
  Pallas kernels  21.9 us (12%)
  local copies, waits for them, and re-layouts  3.66 us (2%)
    all_to_all x4, blocking collectives, exchange(): return lax.all_to_all(blocks, axes, split_axis=0, concat_axis=0, tiled=True)  85.7 us
    ppermute x7, starting transfers between devices, partner(): return lax.ppermute(value, axis, [(i, i ^ flip) for i in range(size)])  22.9 us
    pallas_call x12, Pallas kernels, local(): pl.pallas_call(body, out_shape=outs, grid=(grid,), in_specs=[specs.get(i)...  21.9 us
    ppermute x7, waiting for transfers between devices, partner(): return lax.ppermute(value, axis, [(i, i ^ flip) for i in range(size)])  16.3 us
    all_to_all x3, starting transfers between devices, exchange(): return lax.all_to_all(blocks, axes, split_axis=0, concat_axis=0, tiled=True)  15.7 us
    all_to_all x3, waiting for transfers between devices, exchange(): return lax.all_to_all(blocks, axes, split_axis=0, concat_axis=0, tiled=True)  6.33 us
  transfers between devices with their start and end apart: 10, of which 6 were waited for; matrix products, arithmetic and copies ran while one was open for 1% of the time, Pallas kernels for 7%

profile of v1, /device:TPU:8, one launch (start us, length us, event | category | flops | bytes accessed | tf_op | source)
XLA Modules:
  0.0 174.8 jit_solution(17678951798380774232)
XLA Ops:
  0.6 0.0 copy-start
  0.6 0.7 copy-done
  1.4 0.0 copy-start.2
  1.4 0.7 copy-done.2
  2.1 0.2 shard_map.101
  2.4 17.3 %all_to_all.35.blocks = f32[16,16,512]{2,1,0:T(8,128)S(1)} all-to-all(f32[16,16,512]{2,1,0:T(8,128)S(1)} %shard_map.101), channel_id=1, replica_groups=mesh['x'=4,'w'=4,'y'=4,'z'=4,'c'=2] {'x','y'}, dimensions={0} | all-to-all | bytes 1048576 | tf_op jit(solution)/shard_map/all_to_all | solution.py:56
  19.7 29.5 %all_to_all.36.blocks = f32[4,16,512]{2,1,0:T(8,128)S(1)} all-to-all(f32[4,16,512]{2,1,0:T(8,128)S(1)} %shard_map.102), channel_id=1, replica_groups=mesh['x'=4,'w'=4,'y'=4,'z'=4,'c'=2] {'w'}, dimensions={0} | all-to-all | bytes 262144 | tf_op jit(solution)/shard_map/all_to_all | solution.py:56
  49.2 0.7 shard_map.103
  50.0 4.9 %all-to-all-start.2 = ((bf16[16,16,512]{2,1,0:T(8,128)(2,1)}), bf16[16,16,512]{2,1,0:T(8,128)(2,1)S(1)}, u32[]{:S(2)}, u32[]{:S(2)}) async-start(bf16[16,16,512]{2,1,0:T(8,128)(2,1)} %shard_map.103), calls=%async_computation.2 | async-start | bytes 524288 | tf_op jit(solution)/shard_map/all_to_all | solution.py:56
  54.9 0.7 stack.19.place
  55.5 4.3 %shard_map.104 = (bf16[256,256]{1,0:T(8,128)(2,1)}, bf16[256,256]{1,0:T(8,128)(2,1)}, bf16[256,256]{1,0:T(8,128)(2,1)}, bf16[16,128,256]{2,1,0:T(8,128)(2,1)}, b...) custom-call(s32[5]{0:T(128)} %stack.19.place, bf16[256,2048]{1,0:T(8,128)(2,1)} %tokens.1, ...), custom_call_target="tpu_custom_call" | custom-call | flops 536870912 | bytes 6684692 | tf_op jit(solution)/shard_map/pallas_call | solution.py:43
  59.8 2.1 %all-to-all-done.2 = bf16[16,16,512]{2,1,0:T(8,128)(2,1)S(1)} async-done(((bf16[16,16,512]{2,1,0:T(8,128)(2,1)}), bf16[16,16,512]{2,1,0:T(8,128)(2,1)S(1)}, u32[]{:S(2)}, u32[]{:S(2)}) %all-to-all-start.2) | async-done | bytes 262176 | tf_op jit(solution)/shard_map/all_to_all | solution.py:56
  61.8 0.0 copy-start.4
  61.8 0.7 copy-done.4
  62.5 3.4 %shard_map.105 = f32[16,40,512]{2,1,0:T(8,128)} custom-call(s32[5]{0:T(128)} %stack.19.place, bf16[256,512]{1,0:T(8,128)(2,1)} %bitcast.20, bf16[256,256]{1,0:T(8,128)(2,1)} %get-tuple-element.24.keys, bf16[256,256]{1,0:T(8,128)(2,1)} %get-tuple-element.25.keys_t, bf16[256,256]{1,0:T(8,128)(2,1)} %get-tuple-element.26.values, bf16[512,256]{1,0:T(8,128)(2,1)} %cot.3), custom_call_target="tpu_custom_call" | custom-call | flops 402653184 | bytes 2228244 | tf_op jit(solution)/shard_map/pallas_call | solution.py:43
  66.0 18.9 %all_to_all.37.blocks = f32[16,40,512]{2,1,0:T(8,128)S(1)} all-to-all(f32[16,40,512]{2,1,0:T(8,128)} %shard_map.105), channel_id=1, replica_groups=mesh['x'=4,'w'=4,'y'=4,'z'=4,'c'=2] {'x','y'}, dimensions={0} | all-to-all | bytes 2621440 | tf_op jit(solution)/shard_map/all_to_all | solution.py:56
  84.8 0.1 shard_map.106
  84.9 20.0 %all_to_all.38.sums4 = f32[4,40,512]{2,1,0:T(8,128)} all-to-all(f32[4,40,512]{2,1,0:T(8,128)S(1)} %shard_map.106), channel_id=1, replica_groups=mesh['x'=4,'w'=4,'y'=4,'z'=4,'c'=2] {'w'}, dimensions={0} | all-to-all | bytes 655360 | tf_op jit(solution)/shard_map/all_to_all | solution.py:56
  104.9 4.6 %shard_map.107 = (bf16[16,144,512]{2,1,0:T(8,128)(2,1)}, bf16[256,512]{1,0:T(8,128)(2,1)}) custom-call(s32[5]{0:T(128)} %stack.19.place, f32[4,40,512]{2,1,0:T(8,128)} %all_to_all.38.sums4, bf16[256,512]{1,0:T(8,128)(2,1)} %bitcast.21, bf16[256,256]{1,0:T(8,128)(2,1)} %get-tuple-element.24.keys, bf16[256,256]{1,0:T(8,128)(2,1)} %get-tuple-element.26.values, ...), custom_call_target="tpu_custom_call" | custom-call | flops 805306368 | bytes 4784148 | tf_op jit(solution)/shard_map/pallas_call | solution.py:43
  109.5 7.4 %all-to-all-start.5 = ((bf16[16,144,512]{2,1,0:T(8,128)(2,1)}), bf16[16,144,512]{2,1,0:T(8,128)(2,1)S(1)}, u32[]{:S(2)}, u32[]{:S(2)}) async-start(bf16[16,144,512]{2,1,0:T(8,128)(2,1)} %get-tuple-element.28), calls=%async_computation.5 | async-start | bytes 4718592 | tf_op jit(solution)/shard_map/all_to_all | solution.py:56
  117.0 0.0 copy-start.3
  117.0 2.6 %shard_map.108 = bf16[4,256,256]{2,1,0:T(8,128)(2,1)} custom-call(bf16[256,512]{1,0:T(8,128)(2,1)} %get-tuple-element.29.both, bf16[4,512,256]{2,1,0:T(8,128)(2,1)} %get-tuple-element.31.weights), custom_call_target="tpu_custom_call" | custom-call | flops 268435456 | bytes 1835008 | tf_op jit(solution)/shard_map/pallas_call | solution.py:43
  119.5 1.9 %collective-permute-start = (bf16[4,256,256]{2,1,0:T(8,128)(2,1)}, bf16[4,256,256]{2,1,0:T(8,128)(2,1)S(1)}, u32[]{:S(2)}, u32[]{:S(2)}) collective-permute-start(bf16[4,256,256]{2,1,0:T(8,128)(2,1)} %shard_map.108), channel_id=1, source_target_pairs={{0,1},{1,0},{2,3},{3,2},{4,5},{5,4},{6,7},{7,6},{8,9},{9,8},{10,11... | collective-permute-start | bytes 1572872 | tf_op jit(solution)/shard_map/ppermute | solution.py:61
  121.4 2.1 %collective-permute-done.other = bf16[4,256,256]{2,1,0:T(8,128)(2,1)S(1)} collective-permute-done((bf16[4,256,256]{2,1,0:T(8,128)(2,1)}, bf16[4,256,256]{2,1,0:T(8,128)(2,1)S(1)}, u32[]{:S(2)}, u32[]{:S(2)}) %collective-permute-start) | collective-permute-done | bytes 524320 | tf_op jit(solution)/shard_map/ppermute | solution.py:61
  123.5 0.0 copy-start.5
  123.5 0.8 copy-done.5
  124.3 2.6 %shard_map.109 = (f32[256,256]{1,0:T(8,128)}, bf16[256,256]{1,0:T(8,128)(2,1)}, bf16[256,256]{1,0:T(8,128)(2,1)}, bf16[256,256]{1,0:T(8,128)(2,1)}) custom-call(bf16[256,512]{1,0:T(8,128)(2,1)} %get-tuple-element.29.both, bf16[4,512,256]{2,1,0:T(8,128)(2,1)} %get-tuple-element.30.weights, bf16[4,256,256]{2,1,0:T(8,128)(2,1)} %copy-done.5), custom_call_target="tpu_custom_call" | custom-call | flops 268435456 | bytes 2490368 | tf_op jit(solution)/shard_map/pallas_call | solution.py:43
  126.9 0.0 copy-start.1
  126.9 5.2 %collective-permute-start.1 = (bf16[256,256]{1,0:T(8,128)(2,1)}, bf16[256,256]{1,0:T(8,128)(2,1)S(1)}, u32[]{:S(2)}, u32[]{:S(2)}) collective-permute-start(bf16[256,256]{1,0:T(8,128)(2,1)} %get-tuple-element.33), channel_id=1, source_target_pairs={{0,2},{2,0},{4,6},{6,4},{1,3},{3,1},{5,7},{7,5},{8,10},{10,8},{12,... | collective-permute-start | bytes 393224 | tf_op jit(solution)/shard_map/ppermute | solution.py:61
  132.1 1.9 %collective-permute-start.2 = (bf16[256,256]{1,0:T(8,128)(2,1)}, bf16[256,256]{1,0:T(8,128)(2,1)S(1)}, u32[]{:S(2)}, u32[]{:S(2)}) collective-permute-start(bf16[256,256]{1,0:T(8,128)(2,1)} %get-tuple-element.34), channel_id=1, source_target_pairs={{0,4},{2,6},{4,0},{6,2},{1,5},{3,7},{5,1},{7,3},{8,12},{10,14},{12... | collective-permute-start | bytes 393224 | tf_op jit(solution)/shard_map/ppermute | solution.py:61
  134.0 4.3 %collective-permute-start.3 = (bf16[256,256]{1,0:T(8,128)(2,1)}, bf16[256,256]{1,0:T(8,128)(2,1)S(1)}, u32[]{:S(2)}, u32[]{:S(2)}) collective-permute-start(bf16[256,256]{1,0:T(8,128)(2,1)} %get-tuple-element.35), channel_id=1, source_target_pairs={{0,6},{2,4},{4,2},{6,0},{1,7},{3,5},{5,3},{7,1},{8,14},{10,12},{12... | collective-permute-start | bytes 393224 | tf_op jit(solution)/shard_map/ppermute | solution.py:61
  138.3 0.0 collective-permute-done.1.one
  138.3 0.0 copy-start.6
  138.3 7.5 %collective-permute-done.2.two = bf16[256,256]{1,0:T(8,128)(2,1)S(1)} collective-permute-done((bf16[256,256]{1,0:T(8,128)(2,1)}, bf16[256,256]{1,0:T(8,128)(2,1)S(1)}, u32[]{:S(2)}, u32[]{:S(2)}) %collective-permute-start.2) | collective-permute-done | bytes 131104 | tf_op jit(solution)/shard_map/ppermute | solution.py:61
  145.8 0.0 copy-start.7
  145.8 0.0 collective-permute-done.3.three
  145.8 0.0 copy-start.8
  145.8 0.0 all-to-all-done.5.arrived
  145.9 0.0 copy-done.3
  145.9 0.1 convolution_bitcast_fusion
  146.0 1.9 %collective-permute-start.4 = (f32[32,512]{1,0:T(8,128)S(1)}, f32[32,512]{1,0:T(8,128)S(1)}, u32[]{:S(2)}, u32[]{:S(2)}) collective-permute-start(f32[32,512]{1,0:T(8,128)S(1)} %convolution_bitcast_fusion), channel_id=1, source_target_pairs={{0,1},{1,0},{2,3},{3,2},{4,5},{5,4},{6,7},{7,6},{8,9},{9,8},{10,11... | collective-permute-start | bytes 196616 | tf_op jit(solution)/shard_map/ppermute | solution.py:61
  147.9 1.2 collective-permute-done.4
  149.2 5.2 %collective-permute-start.5 = (f32[32,512]{1,0:T(8,128)S(1)}, f32[32,512]{1,0:T(8,128)S(1)}, u32[]{:S(2)}, u32[]{:S(2)}) collective-permute-start(f32[32,512]{1,0:T(8,128)S(1)} %add.21), channel_id=1, source_target_pairs={{0,2},{2,0},{4,6},{6,4},{1,3},{3,1},{5,7},{7,5},{8,10},{10,8},{12,... | collective-permute-start | bytes 196616 | tf_op jit(solution)/shard_map/ppermute | solution.py:61
  154.4 0.9 shard_map.111
  155.3 3.3 %all-to-all-start.6 = ((bf16[4,32,512]{2,1,0:T(8,128)(2,1)}), bf16[4,32,512]{2,1,0:T(8,128)(2,1)S(1)}, u32[]{:S(2)}, u32[]{:S(2)}) async-start(bf16[4,32,512]{2,1,0:T(8,128)(2,1)} %shard_map.111), calls=%async_computation.6 | async-start | bytes 262144 | tf_op jit(solution)/shard_map/all_to_all | solution.py:56
  158.6 0.0 collective-permute-done.5
  158.6 2.4 %collective-permute-start.6 = (f32[32,512]{1,0:T(8,128)S(1)}, f32[32,512]{1,0:T(8,128)S(1)}, u32[]{:S(2)}, u32[]{:S(2)}) collective-permute-start(f32[32,512]{1,0:T(8,128)S(1)} %add.22), channel_id=1, source_target_pairs={{0,4},{2,6},{4,0},{6,2},{1,5},{3,7},{5,1},{7,3},{8,12},{10,14},{12... | collective-permute-start | bytes 196616 | tf_op jit(solution)/shard_map/ppermute | solution.py:61
  161.1 0.0 copy-done.1
  161.1 0.8 convolution_bitcast_fusion.1
  161.9 0.0 copy-done.6
  161.9 0.0 copy-done.7
  161.9 0.0 copy-done.8
  161.9 1.8 %shard_map.110 = bf16[256,256]{1,0:T(8,128)(2,1)} custom-call(f32[256,256]{1,0:T(8,128)} %get-tuple-element.36.here, bf16[256,256]{1,0:T(8,128)(2,1)} %copy-done.6, bf16[256,256]{1,0:T(8,128)(2,1)} %copy-done.7, bf16[256,256]{1,0:T(8,128)(2,1)} %copy-done.8), custom_call_target="tpu_custom_call" | custom-call | bytes 786432 | tf_op jit(solution)/shard_map/pallas_call | solution.py:43
  163.7 5.5 %collective-permute-done.6 = f32[32,512]{1,0:T(8,128)S(1)} collective-permute-done((f32[32,512]{1,0:T(8,128)S(1)}, f32[32,512]{1,0:T(8,128)S(1)}, u32[]{:S(2)}, u32[]{:S(2)}) %collective-permute-start.6) | collective-permute-done | bytes 65568 | tf_op jit(solution)/shard_map/ppermute | solution.py:61
  169.3 0.6 add_bitcast_fusion
  169.9 4.3 %all-to-all-done.6.arrived = bf16[4,32,512]{2,1,0:T(8,128)(2,1)S(1)} async-done(((bf16[4,32,512]{2,1,0:T(8,128)(2,1)}), bf16[4,32,512]{2,1,0:T(8,128)(2,1)S(1)}, u32[]{:S(2)}, u32[]{:S(2)}) %all-to-all-start.6) | async-done | bytes 131104 | tf_op jit(solution)/shard_map/all_to_all | solution.py:56
  174.2 0.6 shard_map.112
  (4 shorter events, 0.1 us)
Async XLA Ops:
  0.6 0.8 copy-start
  1.4 0.7 copy-start.2
  50.0 11.9 %all-to-all-start.2 = ((bf16[16,16,512]{2,1,0:T(8,128)(2,1)}), bf16[16,16,512]{2,1,0:T(8,128)(2,1)S(1)}, u32[]{:S(2)}, u32[]{:S(2)}) async-start(bf16[16,16,512]{2,1,0:T(8,128)(2,1)} %shard_map.103), calls=%async_computation.2 | async-start | bytes 524288 | tf_op jit(solution)/shard_map/all_to_all | solution.py:56
  61.8 0.7 copy-start.4
  109.5 36.3 %all-to-all-start.5 = ((bf16[16,144,512]{2,1,0:T(8,128)(2,1)}), bf16[16,144,512]{2,1,0:T(8,128)(2,1)S(1)}, u32[]{:S(2)}, u32[]{:S(2)}) async-start(bf16[16,144,512]{2,1,0:T(8,128)(2,1)} %get-tuple-element.28), calls=%async_computation.5 | async-start | bytes 4718592 | tf_op jit(solution)/shard_map/all_to_all | solution.py:56
  117.0 28.9 %copy-start.3 = (bf16[32,256]{1,0:T(8,128)(2,1)S(1)}, bf16[32,256]{1,0:T(8,128)(2,1)}, u32[]{:S(2)}) copy-start(bf16[32,256]{1,0:T(8,128)(2,1)} %w_query.1) | copy-start | bytes 49156
  119.5 4.0 %collective-permute-start = (bf16[4,256,256]{2,1,0:T(8,128)(2,1)}, bf16[4,256,256]{2,1,0:T(8,128)(2,1)S(1)}, u32[]{:S(2)}, u32[]{:S(2)}) collective-permute-start(bf16[4,256,256]{2,1,0:T(8,128)(2,1)} %shard_map.108), channel_id=1, source_target_pairs={{0,1},{1,0},{2,3},{3,2},{4,5},{5,4},{6,7},{7,6},{8,9},{9,8},{10,11... | collective-permute-start | bytes 1572872 | tf_op jit(solution)/shard_map/ppermute | solution.py:61
  123.5 0.8 copy-start.5
  126.9 34.2 %copy-start.1 = (bf16[512,32]{0,1:T(8,128)(2,1)S(1)}, bf16[512,32]{0,1:T(8,128)(2,1)}, u32[]{:S(2)}) copy-start(bf16[512,32]{0,1:T(8,128)(2,1)} %param.7) | copy-start | bytes 98308
  126.9 11.4 %collective-permute-start.1 = (bf16[256,256]{1,0:T(8,128)(2,1)}, bf16[256,256]{1,0:T(8,128)(2,1)S(1)}, u32[]{:S(2)}, u32[]{:S(2)}) collective-permute-start(bf16[256,256]{1,0:T(8,128)(2,1)} %get-tuple-element.33), channel_id=1, source_target_pairs={{0,2},{2,0},{4,6},{6,4},{1,3},{3,1},{5,7},{7,5},{8,10},{10,8},{12,... | collective-permute-start | bytes 393224 | tf_op jit(solution)/shard_map/ppermute | solution.py:61
  132.1 13.7 %collective-permute-start.2 = (bf16[256,256]{1,0:T(8,128)(2,1)}, bf16[256,256]{1,0:T(8,128)(2,1)S(1)}, u32[]{:S(2)}, u32[]{:S(2)}) collective-permute-start(bf16[256,256]{1,0:T(8,128)(2,1)} %get-tuple-element.34), channel_id=1, source_target_pairs={{0,4},{2,6},{4,0},{6,2},{1,5},{3,7},{5,1},{7,3},{8,12},{10,14},{12... | collective-permute-start | bytes 393224 | tf_op jit(solution)/shard_map/ppermute | solution.py:61
  134.0 11.8 %collective-permute-start.3 = (bf16[256,256]{1,0:T(8,128)(2,1)}, bf16[256,256]{1,0:T(8,128)(2,1)S(1)}, u32[]{:S(2)}, u32[]{:S(2)}) collective-permute-start(bf16[256,256]{1,0:T(8,128)(2,1)} %get-tuple-element.35), channel_id=1, source_target_pairs={{0,6},{2,4},{4,2},{6,0},{1,7},{3,5},{5,3},{7,1},{8,14},{10,12},{12... | collective-permute-start | bytes 393224 | tf_op jit(solution)/shard_map/ppermute | solution.py:61
  138.3 23.6 %copy-start.6 = (bf16[256,256]{1,0:T(8,128)(2,1)}, bf16[256,256]{1,0:T(8,128)(2,1)S(1)}, u32[]{:S(2)}) copy-start(bf16[256,256]{1,0:T(8,128)(2,1)S(1)} %collective-permute-done.1.one) | copy-start | bytes 393220
  145.8 16.1 %copy-start.7 = (bf16[256,256]{1,0:T(8,128)(2,1)}, bf16[256,256]{1,0:T(8,128)(2,1)S(1)}, u32[]{:S(2)}) copy-start(bf16[256,256]{1,0:T(8,128)(2,1)S(1)} %collective-permute-done.2.two) | copy-start | bytes 393220
  145.8 16.1 %copy-start.8 = (bf16[256,256]{1,0:T(8,128)(2,1)}, bf16[256,256]{1,0:T(8,128)(2,1)S(1)}, u32[]{:S(2)}) copy-start(bf16[256,256]{1,0:T(8,128)(2,1)S(1)} %collective-permute-done.3.three) | copy-start | bytes 393220
  146.0 3.2 %collective-permute-start.4 = (f32[32,512]{1,0:T(8,128)S(1)}, f32[32,512]{1,0:T(8,128)S(1)}, u32[]{:S(2)}, u32[]{:S(2)}) collective-permute-start(f32[32,512]{1,0:T(8,128)S(1)} %convolution_bitcast_fusion), channel_id=1, source_target_pairs={{0,1},{1,0},{2,3},{3,2},{4,5},{5,4},{6,7},{7,6},{8,9},{9,8},{10,11... | collective-permute-start | bytes 196616 | tf_op jit(solution)/shard_map/ppermute | solution.py:61
  149.2 9.4 %collective-permute-start.5 = (f32[32,512]{1,0:T(8,128)S(1)}, f32[32,512]{1,0:T(8,128)S(1)}, u32[]{:S(2)}, u32[]{:S(2)}) collective-permute-start(f32[32,512]{1,0:T(8,128)S(1)} %add.21), channel_id=1, source_target_pairs={{0,2},{2,0},{4,6},{6,4},{1,3},{3,1},{5,7},{7,5},{8,10},{10,8},{12,... | collective-permute-start | bytes 196616 | tf_op jit(solution)/shard_map/ppermute | solution.py:61
  155.3 18.9 %all-to-all-start.6 = ((bf16[4,32,512]{2,1,0:T(8,128)(2,1)}), bf16[4,32,512]{2,1,0:T(8,128)(2,1)S(1)}, u32[]{:S(2)}, u32[]{:S(2)}) async-start(bf16[4,32,512]{2,1,0:T(8,128)(2,1)} %shard_map.111), calls=%async_computation.6 | async-start | bytes 262144 | tf_op jit(solution)/shard_map/all_to_all | solution.py:56
  158.6 10.6 %collective-permute-start.6 = (f32[32,512]{1,0:T(8,128)S(1)}, f32[32,512]{1,0:T(8,128)S(1)}, u32[]{:S(2)}, u32[]{:S(2)}) collective-permute-start(f32[32,512]{1,0:T(8,128)S(1)} %add.22), channel_id=1, source_target_pairs={{0,4},{2,6},{4,0},{6,2},{1,5},{3,7},{5,1},{7,3},{8,12},{10,14},{12... | collective-permute-start | bytes 196616 | tf_op jit(solution)/shard_map/ppermute | solution.py:61

commit v2 on v1

--- a/solution.py
+++ b/solution.py
@@ -160,9 +160,13 @@
         spread[j, 2 * each :, :] = packed
 
 
-def grad_kernel(place, sums4, query_t, keys, values, cot, tokens_hbm, blocks, both, tokens_t, sem):
-    fetch = pltpu.make_async_copy(tokens_hbm, tokens_t, sem)
+def grad_kernel(
+    place, sums4, query_t, keys, values, cot, tokens_hbm, other_hbm, blocks, both, other, tokens_t, other_t, sems
+):
+    fetch = pltpu.make_async_copy(tokens_hbm, tokens_t, sems.at[0])
+    fetch_other = pltpu.make_async_copy(other_hbm, other_t, sems.at[1])
     fetch.start()
+    fetch_other.start()
     heads = keys.shape[1] // HEAD_DIM
     sums = summed(sums4)
     n, held, _ = blocks.shape
@@ -194,11 +198,9 @@
         for i in range(tall):
             blocks[j + i, :depth, :] = part[i * depth : (i + 1) * depth]
             blocks[j + i, depth:, :] = query_grad
-
-
-def other_kernel(both, weights, other):
+    fetch_other.wait()
     for k in range(other.shape[0]):
-        other[k] = dot(both[...], weights[k]).astype(BF16)
+        other[k] = dot(both[...], other_t[k]).astype(BF16)
 
 
 def pair_kernel(both, weights, other, here, *away):
@@ -242,7 +244,7 @@
     scalars = {0: SMEM}
 
     (query_part,) = local(
-        query_kernel, [shape((near, each, lats), F32)], [w_query, latents.T], 2 * share * width * lats
+        query_kernel, [shape((near, each, lats), F32)], [w_query, latents.T], 2 * share * width * lats, limit=60
     )
     query_part = exchange(query_part, NEAR)
     query_part = exchange(sum_copies(query_part, far, F32), "w")
@@ -276,24 +278,25 @@
     )
     sums = exchange(sum_copies(exchange(spread, NEAR), far, F32), "w")
 
-    blocks, both = local(
+    blocks, both, other = local(
         grad_kernel,
-        [shape((near, depth // near + each, 2 * width), BF16), shape((rows, 2 * width), BF16)],
-        [place, sums, query_t, keys, values, cotangent, tokens_t],
-        8 * rows * width * lats + 2 * rows * depth * 2 * width,
-        specs={0: SMEM, 6: HBM},
-        scratch=[pltpu.VMEM(tokens_t.shape, BF16), pltpu.SemaphoreType.DMA(())],
+        [
+            shape((near, depth // near + each, 2 * width), BF16),
+            shape((rows, 2 * width), BF16),
+            shape((hops, rows, block), BF16),
+        ],
+        [place, sums, query_t, keys, values, cotangent, tokens_t, other_t],
+        8 * rows * width * lats + 3 * rows * depth * 2 * width,
+        specs={0: SMEM, 6: HBM, 7: HBM},
+        scratch=[
+            pltpu.VMEM(tokens_t.shape, BF16),
+            pltpu.VMEM(other_t.shape, BF16),
+            pltpu.SemaphoreType.DMA((2,)),
+        ],
         limit=60,
     )
     arrived = exchange(blocks, NEAR)
 
-    (other,) = local(
-        other_kernel,
-        [shape((hops, rows, block), BF16)],
-        [both, other_t],
-        rows * depth * 2 * width,
-        limit=60,
-    )
     here, *away = local(
         pair_kernel,
         [shape((rows, block), F32)] + [shape((rows, block), BF16)] * (hops - 1),
@@ -301,26 +304,28 @@
         rows * depth * 2 * width,
         limit=60,
     )
-    parts = [partner(part, "z", k + 1) for k, part in enumerate(away)]
+    parts = [partner(away[k - 1], "z", k) for k in (2, 3, 1)]
     arrived, here, *parts = lax.optimization_barrier((arrived, here, *parts))
     (token_grad,) = local(token_sum_kernel, [shape((rows, block), BF16)], [here, *parts], limit=60)
 
-    query_grad_t = arrived[:, depth // near :, :].reshape(width, lats)
-    latent_grad_t = dot(w_query, query_grad_t)
-    query_weight_grad = lax.dot_general(
-        latents, query_grad_t, (((0,), (1,)), ((), ())), preferred_element_type=F32
-    )
     (sent,) = local(
         near_sum_kernel,
         [shape((far, share, 2 * width), BF16)],
         [arrived],
         specs={0: pl.BlockSpec((near, depth // near, 2 * width), lambda i: (0, 0, 0))},
     )
+    query_grad_t = arrived[:, depth // near :, :].reshape(width, lats)
+    sent, query_grad_t = lax.optimization_barrier((sent, query_grad_t))
     key_weight_grad, value_weight_grad = local(
         far_sum_kernel, [shape((share, width), F32)] * 2, [exchange(sent, "w")]
     )
+    latent_grad_t = dot(w_query, query_grad_t)
+    query_weight_grad = lax.dot_general(
+        latents, query_grad_t, (((0,), (1,)), ((), ())), preferred_element_type=F32
+    )
     for axis, flip in (("c", 1), ("z", 1), ("z", 2)):
-        latent_grad_t = latent_grad_t + partner(latent_grad_t, axis, flip)
+        held = latent_grad_t.astype(BF16)
+        latent_grad_t = held.astype(F32) + partner(held, axis, flip).astype(F32)
     return (
         token_grad,
         latent_grad_t.T,

time: 176 us -> 176 us (level)
  starting transfers between devices: 38.5 us -> 41.6 us
    ppermute x7, waiting for transfers between devices: 16.3 us -> 9.14 us  [partner(): return lax.ppermute(value, axis, [(i, i ^ flip) for i in range(size)])]
    all_to_all x3, waiting for transfers between devices: 6.33 us -> 12.3 us  [exchange(): return lax.all_to_all(blocks, axes, split_axis=0, concat_axis=0, tiled=True)]
    all_to_all x3, starting transfers between devices: 15.7 us -> 19.8 us  [exchange(): return lax.all_to_all(blocks, axes, split_axis=0, concat_axis=0, tiled=True)]
    pallas_call x12 -> x11, Pallas kernels: 21.9 us -> 21.2 us  [local(): pl.pallas_call(body, out_shape=outs, grid=(grid,), in_specs=[specs.get(i)...]
  transfers between devices with their start and end apart: 10 -> 10, of which waited for: 6 -> 8; matrix products, arithmetic and copies ran while one was open for 1% -> 1% of each run, Pallas kernels for 7% -> 5%
where the time goes in v2:
time: 176 us; the launch traced here: 175 us
  blocking collectives  85.8 us (49%)
  starting transfers between devices  41.6 us (24%)
  waiting for transfers between devices  21.5 us (12%)
  Pallas kernels  21.2 us (12%)
  local copies, waits for them, and re-layouts  2.16 us (1%)
    all_to_all x4, blocking collectives, exchange(): return lax.all_to_all(blocks, axes, split_axis=0, concat_axis=0, tiled=True)  85.8 us
    ppermute x7, starting transfers between devices, partner(): return lax.ppermute(value, axis, [(i, i ^ flip) for i in range(size)])  21.8 us
    pallas_call x11, Pallas kernels, local(): pl.pallas_call(body, out_shape=outs, grid=(grid,), in_specs=[specs.get(i)...  21.2 us
    all_to_all x3, starting transfers between devices, exchange(): return lax.all_to_all(blocks, axes, split_axis=0, concat_axis=0, tiled=True)  19.8 us
    all_to_all x3, waiting for transfers between devices, exchange(): return lax.all_to_all(blocks, axes, split_axis=0, concat_axis=0, tiled=True)  12.3 us
    ppermute x7, waiting for transfers between devices, partner(): return lax.ppermute(value, axis, [(i, i ^ flip) for i in range(size)])  9.14 us
  transfers between devices with their start and end apart: 10, of which 8 were waited for; matrix products, arithmetic and copies ran while one was open for 1% of the time, Pallas kernels for 5%

profile of v2, /device:TPU:8, one launch (start us, length us, event | category | flops | bytes accessed | tf_op | source)
XLA Modules:
  0.0 174.6 jit_solution(635999545272927423)
XLA Ops:
  0.6 1.8 %shard_map.101 = f32[16,16,512]{2,1,0:T(8,128)} custom-call(bf16[32,256]{1,0:T(8,128)(2,1)} %w_query.1, bf16[32,512]{1,0:T(8,128)(2,1)} %bitcast.21), custom_call_target="tpu_custom_call" | custom-call | flops 8388608 | bytes 573440 | tf_op jit(solution)/shard_map/pallas_call | solution.py:43
  2.5 18.0 %all_to_all.35.blocks = f32[16,16,512]{2,1,0:T(8,128)S(1)} all-to-all(f32[16,16,512]{2,1,0:T(8,128)} %shard_map.101), channel_id=1, replica_groups=mesh['x'=4,'w'=4,'y'=4,'z'=4,'c'=2] {'x','y'}, dimensions={0} | all-to-all | bytes 1048576 | tf_op jit(solution)/shard_map/all_to_all | solution.py:56
  20.5 29.0 %all_to_all.36.blocks = f32[4,16,512]{2,1,0:T(8,128)S(1)} all-to-all(f32[4,16,512]{2,1,0:T(8,128)S(1)} %shard_map.102), channel_id=1, replica_groups=mesh['x'=4,'w'=4,'y'=4,'z'=4,'c'=2] {'w'}, dimensions={0} | all-to-all | bytes 262144 | tf_op jit(solution)/shard_map/all_to_all | solution.py:56
  49.5 0.7 shard_map.103
  50.3 4.9 %all-to-all-start.2 = ((bf16[16,16,512]{2,1,0:T(8,128)(2,1)}), bf16[16,16,512]{2,1,0:T(8,128)(2,1)S(1)}, u32[]{:S(2)}, u32[]{:S(2)}) async-start(bf16[16,16,512]{2,1,0:T(8,128)(2,1)} %shard_map.103), calls=%async_computation.2 | async-start | bytes 524288 | tf_op jit(solution)/shard_map/all_to_all | solution.py:56
  55.2 0.6 stack.19.place
  55.8 4.3 %shard_map.104 = (bf16[256,256]{1,0:T(8,128)(2,1)}, bf16[256,256]{1,0:T(8,128)(2,1)}, bf16[256,256]{1,0:T(8,128)(2,1)}, bf16[16,128,256]{2,1,0:T(8,128)(2,1)}, b...) custom-call(s32[5]{0:T(128)} %stack.19.place, bf16[256,2048]{1,0:T(8,128)(2,1)} %tokens.1, ...), custom_call_target="tpu_custom_call" | custom-call | flops 536870912 | bytes 6684692 | tf_op jit(solution)/shard_map/pallas_call | solution.py:43
  60.1 2.1 %all-to-all-done.2 = bf16[16,16,512]{2,1,0:T(8,128)(2,1)S(1)} async-done(((bf16[16,16,512]{2,1,0:T(8,128)(2,1)}), bf16[16,16,512]{2,1,0:T(8,128)(2,1)S(1)}, u32[]{:S(2)}, u32[]{:S(2)}) %all-to-all-start.2) | async-done | bytes 262176 | tf_op jit(solution)/shard_map/all_to_all | solution.py:56
  62.2 0.0 copy-start
  62.2 0.7 copy-done
  62.9 3.4 %shard_map.105 = f32[16,40,512]{2,1,0:T(8,128)} custom-call(s32[5]{0:T(128)} %stack.19.place, bf16[256,512]{1,0:T(8,128)(2,1)} %bitcast.19, bf16[256,256]{1,0:T(8,128)(2,1)} %get-tuple-element.27.keys, bf16[256,256]{1,0:T(8,128)(2,1)} %get-tuple-element.28.keys_t, bf16[256,256]{1,0:T(8,128)(2,1)} %get-tuple-element.29.values, bf16[512,256]{1,0:T(8,128)(2,1)} %cot.3), custom_call_target="tpu_custom_call" | custom-call | flops 402653184 | bytes 2228244 | tf_op jit(solution)/shard_map/pallas_call | solution.py:43
  66.3 18.8 %all_to_all.37.blocks = f32[16,40,512]{2,1,0:T(8,128)S(1)} all-to-all(f32[16,40,512]{2,1,0:T(8,128)} %shard_map.105), channel_id=1, replica_groups=mesh['x'=4,'w'=4,'y'=4,'z'=4,'c'=2] {'x','y'}, dimensions={0} | all-to-all | bytes 2621440 | tf_op jit(solution)/shard_map/all_to_all | solution.py:56
  85.2 0.1 shard_map.106
  85.2 19.9 %all_to_all.38.sums4 = f32[4,40,512]{2,1,0:T(8,128)} all-to-all(f32[4,40,512]{2,1,0:T(8,128)S(1)} %shard_map.106), channel_id=1, replica_groups=mesh['x'=4,'w'=4,'y'=4,'z'=4,'c'=2] {'w'}, dimensions={0} | all-to-all | bytes 655360 | tf_op jit(solution)/shard_map/all_to_all | solution.py:56
  105.2 4.9 %shard_map.107 = (bf16[16,144,512]{2,1,0:T(8,128)(2,1)}, bf16[256,512]{1,0:T(8,128)(2,1)}, bf16[4,256,256]{2,1,0:T(8,128)(2,1)}) custom-call(s32[5]{0:T(128)} %stack.19.place, f32[4,40,512]{2,1,0:T(8,128)} %all_to_all.38.sums4, bf16[256,512]{1,0:T(8,128)(2,1)} %bitcast.20, bf16[256,256]{1,0:T(8,128)(2,1)} %get-tuple-element.27.keys, ...), custom_call_target="tpu_custom_call" | custom-call | flops 1073741824 | bytes 6357012 | tf_op jit(solution)/shard_map/pallas_call | solution.py:43
  110.0 0.0 copy-start.7
  110.1 7.6 %all-to-all-start.5 = ((bf16[16,144,512]{2,1,0:T(8,128)(2,1)}), bf16[16,144,512]{2,1,0:T(8,128)(2,1)S(1)}, u32[]{:S(2)}, u32[]{:S(2)}) async-start(bf16[16,144,512]{2,1,0:T(8,128)(2,1)} %get-tuple-element.32), calls=%async_computation.5 | async-start | bytes 4718592 | tf_op jit(solution)/shard_map/all_to_all | solution.py:56
  117.6 0.0 copy-done.7
  117.6 1.9 %collective-permute-start = (bf16[4,256,256]{2,1,0:T(8,128)(2,1)S(1)}, bf16[4,256,256]{2,1,0:T(8,128)(2,1)S(1)}, u32[]{:S(2)}, u32[]{:S(2)}) collective-permute-start(bf16[4,256,256]{2,1,0:T(8,128)(2,1)S(1)} %copy-done.7), channel_id=1, source_target_pairs={{0,1},{1,0},{2,3},{3,2},{4,5},{5,4},{6,7},{7,6},{8,9},{9,8},{10,11... | collective-permute-start | bytes 1572872 | tf_op jit(solution)/shard_map/ppermute | solution.py:61
  119.6 1.9 %collective-permute-done.other = bf16[4,256,256]{2,1,0:T(8,128)(2,1)S(1)} collective-permute-done((bf16[4,256,256]{2,1,0:T(8,128)(2,1)S(1)}, bf16[4,256,256]{2,1,0:T(8,128)(2,1)S(1)}, u32[]{:S(2)}, u32[]{:S(2)}) %collective-permute-start) | collective-permute-done | bytes 524320 | tf_op jit(solution)/shard_map/ppermute | solution.py:61
  121.4 0.0 copy-start.1
  121.5 0.8 copy-done.1
  122.2 0.0 copy-start.6
  122.2 0.0 copy-start.2
  122.2 2.6 %shard_map.108 = (f32[256,256]{1,0:T(8,128)}, bf16[256,256]{1,0:T(8,128)(2,1)}, bf16[256,256]{1,0:T(8,128)(2,1)}, bf16[256,256]{1,0:T(8,128)(2,1)}) custom-call(bf16[256,512]{1,0:T(8,128)(2,1)} %get-tuple-element.33.both, bf16[4,512,256]{2,1,0:T(8,128)(2,1)} %get-tuple-element.34.weights, bf16[4,256,256]{2,1,0:T(8,128)(2,1)} %copy-done.1), custom_call_target="tpu_custom_call" | custom-call | flops 268435456 | bytes 2490368 | tf_op jit(solution)/shard_map/pallas_call | solution.py:43
  124.8 4.9 %collective-permute-start.1 = (bf16[256,256]{1,0:T(8,128)(2,1)}, bf16[256,256]{1,0:T(8,128)(2,1)S(1)}, u32[]{:S(2)}, u32[]{:S(2)}) collective-permute-start(bf16[256,256]{1,0:T(8,128)(2,1)} %get-tuple-element.37), channel_id=1, source_target_pairs={{0,4},{2,6},{4,0},{6,2},{1,5},{3,7},{5,1},{7,3},{8,12},{10,14},{12... | collective-permute-start | bytes 393224 | tf_op jit(solution)/shard_map/ppermute | solution.py:61
  129.7 4.5 %collective-permute-start.2 = (bf16[256,256]{1,0:T(8,128)(2,1)}, bf16[256,256]{1,0:T(8,128)(2,1)S(1)}, u32[]{:S(2)}, u32[]{:S(2)}) collective-permute-start(bf16[256,256]{1,0:T(8,128)(2,1)} %get-tuple-element.38), channel_id=1, source_target_pairs={{0,6},{2,4},{4,2},{6,0},{1,7},{3,5},{5,3},{7,1},{8,14},{10,12},{12... | collective-permute-start | bytes 393224 | tf_op jit(solution)/shard_map/ppermute | solution.py:61
  134.2 1.9 %collective-permute-start.3 = (bf16[256,256]{1,0:T(8,128)(2,1)}, bf16[256,256]{1,0:T(8,128)(2,1)S(1)}, u32[]{:S(2)}, u32[]{:S(2)}) collective-permute-start(bf16[256,256]{1,0:T(8,128)(2,1)} %get-tuple-element.39), channel_id=1, source_target_pairs={{0,2},{2,0},{4,6},{6,4},{1,3},{3,1},{5,7},{7,5},{8,10},{10,8},{12,... | collective-permute-start | bytes 393224 | tf_op jit(solution)/shard_map/ppermute | solution.py:61
  136.1 3.5 %collective-permute-done.1.one = bf16[256,256]{1,0:T(8,128)(2,1)S(1)} collective-permute-done((bf16[256,256]{1,0:T(8,128)(2,1)}, bf16[256,256]{1,0:T(8,128)(2,1)S(1)}, u32[]{:S(2)}, u32[]{:S(2)}) %collective-permute-start.1) | collective-permute-done | bytes 131104 | tf_op jit(solution)/shard_map/ppermute | solution.py:61
  139.6 0.0 copy-start.3
  139.6 0.2 collective-permute-done.2.two
  139.8 0.0 copy-start.4
  139.8 2.4 %collective-permute-done.3.three = bf16[256,256]{1,0:T(8,128)(2,1)S(1)} collective-permute-done((bf16[256,256]{1,0:T(8,128)(2,1)}, bf16[256,256]{1,0:T(8,128)(2,1)S(1)}, u32[]{:S(2)}, u32[]{:S(2)}) %collective-permute-start.3) | collective-permute-done | bytes 131104 | tf_op jit(solution)/shard_map/ppermute | solution.py:61
  142.2 0.0 copy-start.5
  142.2 1.2 all-to-all-done.5.arrived
  143.5 0.9 shard_map.110
  144.4 0.0 copy-done.6
  144.4 0.1 fusion
  144.5 1.9 %collective-permute-start.4 = (bf16[32,512]{1,0:T(8,128)(2,1)S(1)}, bf16[32,512]{1,0:T(8,128)(2,1)S(1)}, u32[]{:S(2)}, u32[]{:S(2)}) collective-permute-start(bf16[32,512]{1,0:T(8,128)(2,1)S(1)} %fusion), channel_id=1, source_target_pairs={{0,1},{1,0},{2,3},{3,2},{4,5},{5,4},{6,7},{7,6},{8,9},{9,8},{10,11... | collective-permute-start | bytes 98312 | tf_op jit(solution)/shard_map/ppermute | solution.py:61
  146.5 1.2 collective-permute-done.4
  147.7 1.9 %collective-permute-start.5 = (bf16[32,512]{1,0:T(8,128)(2,1)S(1)}, bf16[32,512]{1,0:T(8,128)(2,1)S(1)}, u32[]{:S(2)}, u32[]{:S(2)}) collective-permute-start(bf16[32,512]{1,0:T(8,128)(2,1)S(1)} %add_convert_fusion.1), channel_id=1, source_target_pairs={{0,2},{2,0},{4,6},{6,4},{1,3},{3,1},{5,7},{7,5},{8,10},{10,8},{12,... | collective-permute-start | bytes 98312 | tf_op jit(solution)/shard_map/ppermute | solution.py:61
  149.6 7.3 %all-to-all-start.6 = ((bf16[4,32,512]{2,1,0:T(8,128)(2,1)}), bf16[4,32,512]{2,1,0:T(8,128)(2,1)S(1)}, u32[]{:S(2)}, u32[]{:S(2)}) async-start(bf16[4,32,512]{2,1,0:T(8,128)(2,1)} %shard_map.110), calls=%async_computation.6 | async-start | bytes 262144 | tf_op jit(solution)/shard_map/all_to_all | solution.py:56
  156.9 0.0 collective-permute-done.5
  156.9 4.8 %collective-permute-start.6 = (bf16[32,512]{1,0:T(8,128)(2,1)S(1)}, bf16[32,512]{1,0:T(8,128)(2,1)S(1)}, u32[]{:S(2)}, u32[]{:S(2)}) collective-permute-start(bf16[32,512]{1,0:T(8,128)(2,1)S(1)} %add_convert_fusion), channel_id=1, source_target_pairs={{0,4},{2,6},{4,0},{6,2},{1,5},{3,7},{5,1},{7,3},{8,12},{10,14},{12... | collective-permute-start | bytes 98312 | tf_op jit(solution)/shard_map/ppermute | solution.py:61
  161.7 0.0 copy-done.2
  161.7 0.8 convolution_bitcast_fusion
  162.5 0.0 copy-done.3
  162.5 0.0 copy-done.4
  162.5 0.0 copy-done.5
  162.5 1.8 %shard_map.109 = bf16[256,256]{1,0:T(8,128)(2,1)} custom-call(f32[256,256]{1,0:T(8,128)} %get-tuple-element.40.here, bf16[256,256]{1,0:T(8,128)(2,1)} %copy-done.3, bf16[256,256]{1,0:T(8,128)(2,1)} %copy-done.4, bf16[256,256]{1,0:T(8,128)(2,1)} %copy-done.5), custom_call_target="tpu_custom_call" | custom-call | bytes 786432 | tf_op jit(solution)/shard_map/pallas_call | solution.py:43
  164.3 0.0 collective-permute-done.6
  164.4 0.6 add_bitcast_fusion
  165.0 9.0 %all-to-all-done.6.arrived = bf16[4,32,512]{2,1,0:T(8,128)(2,1)S(1)} async-done(((bf16[4,32,512]{2,1,0:T(8,128)(2,1)}), bf16[4,32,512]{2,1,0:T(8,128)(2,1)S(1)}, u32[]{:S(2)}, u32[]{:S(2)}) %all-to-all-start.6) | async-done | bytes 131104 | tf_op jit(solution)/shard_map/all_to_all | solution.py:56
  174.0 0.6 shard_map.111
  (4 shorter events, 0.1 us)
Async XLA Ops:
  50.3 11.9 %all-to-all-start.2 = ((bf16[16,16,512]{2,1,0:T(8,128)(2,1)}), bf16[16,16,512]{2,1,0:T(8,128)(2,1)S(1)}, u32[]{:S(2)}, u32[]{:S(2)}) async-start(bf16[16,16,512]{2,1,0:T(8,128)(2,1)} %shard_map.103), calls=%async_computation.2 | async-start | bytes 524288 | tf_op jit(solution)/shard_map/all_to_all | solution.py:56
  62.2 0.7 copy-start
  110.0 7.6 %copy-start.7 = (bf16[4,256,256]{2,1,0:T(8,128)(2,1)S(1)}, bf16[4,256,256]{2,1,0:T(8,128)(2,1)}, u32[]{:S(2)}) copy-start(bf16[4,256,256]{2,1,0:T(8,128)(2,1)} %get-tuple-element.35) | copy-start | bytes 1572868
  110.1 33.4 %all-to-all-start.5 = ((bf16[16,144,512]{2,1,0:T(8,128)(2,1)}), bf16[16,144,512]{2,1,0:T(8,128)(2,1)S(1)}, u32[]{:S(2)}, u32[]{:S(2)}) async-start(bf16[16,144,512]{2,1,0:T(8,128)(2,1)} %get-tuple-element.32), calls=%async_computation.5 | async-start | bytes 4718592 | tf_op jit(solution)/shard_map/all_to_all | solution.py:56
  117.6 3.8 %collective-permute-start = (bf16[4,256,256]{2,1,0:T(8,128)(2,1)S(1)}, bf16[4,256,256]{2,1,0:T(8,128)(2,1)S(1)}, u32[]{:S(2)}, u32[]{:S(2)}) collective-permute-start(bf16[4,256,256]{2,1,0:T(8,128)(2,1)S(1)} %copy-done.7), channel_id=1, source_target_pairs={{0,1},{1,0},{2,3},{3,2},{4,5},{5,4},{6,7},{7,6},{8,9},{9,8},{10,11... | collective-permute-start | bytes 1572872 | tf_op jit(solution)/shard_map/ppermute | solution.py:61
  121.4 0.8 copy-start.1
  122.2 22.2 %copy-start.6 = (bf16[32,256]{1,0:T(8,128)(2,1)S(1)}, bf16[32,256]{1,0:T(8,128)(2,1)}, u32[]{:S(2)}) copy-start(bf16[32,256]{1,0:T(8,128)(2,1)} %w_query.1) | copy-start | bytes 49156
  122.2 39.5 %copy-start.2 = (bf16[512,32]{0,1:T(8,128)(2,1)S(1)}, bf16[512,32]{0,1:T(8,128)(2,1)}, u32[]{:S(2)}) copy-start(bf16[512,32]{0,1:T(8,128)(2,1)} %param.7) | copy-start | bytes 98308
  124.8 14.7 %collective-permute-start.1 = (bf16[256,256]{1,0:T(8,128)(2,1)}, bf16[256,256]{1,0:T(8,128)(2,1)S(1)}, u32[]{:S(2)}, u32[]{:S(2)}) collective-permute-start(bf16[256,256]{1,0:T(8,128)(2,1)} %get-tuple-element.37), channel_id=1, source_target_pairs={{0,4},{2,6},{4,0},{6,2},{1,5},{3,7},{5,1},{7,3},{8,12},{10,14},{12... | collective-permute-start | bytes 393224 | tf_op jit(solution)/shard_map/ppermute | solution.py:61
  129.7 10.1 %collective-permute-start.2 = (bf16[256,256]{1,0:T(8,128)(2,1)}, bf16[256,256]{1,0:T(8,128)(2,1)S(1)}, u32[]{:S(2)}, u32[]{:S(2)}) collective-permute-start(bf16[256,256]{1,0:T(8,128)(2,1)} %get-tuple-element.38), channel_id=1, source_target_pairs={{0,6},{2,4},{4,2},{6,0},{1,7},{3,5},{5,3},{7,1},{8,14},{10,12},{12... | collective-permute-start | bytes 393224 | tf_op jit(solution)/shard_map/ppermute | solution.py:61
  134.2 8.0 %collective-permute-start.3 = (bf16[256,256]{1,0:T(8,128)(2,1)}, bf16[256,256]{1,0:T(8,128)(2,1)S(1)}, u32[]{:S(2)}, u32[]{:S(2)}) collective-permute-start(bf16[256,256]{1,0:T(8,128)(2,1)} %get-tuple-element.39), channel_id=1, source_target_pairs={{0,2},{2,0},{4,6},{6,4},{1,3},{3,1},{5,7},{7,5},{8,10},{10,8},{12,... | collective-permute-start | bytes 393224 | tf_op jit(solution)/shard_map/ppermute | solution.py:61
  139.6 22.9 %copy-start.3 = (bf16[256,256]{1,0:T(8,128)(2,1)}, bf16[256,256]{1,0:T(8,128)(2,1)S(1)}, u32[]{:S(2)}) copy-start(bf16[256,256]{1,0:T(8,128)(2,1)S(1)} %collective-permute-done.1.one) | copy-start | bytes 393220
  139.8 22.7 %copy-start.4 = (bf16[256,256]{1,0:T(8,128)(2,1)}, bf16[256,256]{1,0:T(8,128)(2,1)S(1)}, u32[]{:S(2)}) copy-start(bf16[256,256]{1,0:T(8,128)(2,1)S(1)} %collective-permute-done.2.two) | copy-start | bytes 393220
  142.2 20.3 %copy-start.5 = (bf16[256,256]{1,0:T(8,128)(2,1)}, bf16[256,256]{1,0:T(8,128)(2,1)S(1)}, u32[]{:S(2)}) copy-start(bf16[256,256]{1,0:T(8,128)(2,1)S(1)} %collective-permute-done.3.three) | copy-start | bytes 393220
  144.5 3.1 %collective-permute-start.4 = (bf16[32,512]{1,0:T(8,128)(2,1)S(1)}, bf16[32,512]{1,0:T(8,128)(2,1)S(1)}, u32[]{:S(2)}, u32[]{:S(2)}) collective-permute-start(bf16[32,512]{1,0:T(8,128)(2,1)S(1)} %fusion), channel_id=1, source_target_pairs={{0,1},{1,0},{2,3},{3,2},{4,5},{5,4},{6,7},{7,6},{8,9},{9,8},{10,11... | collective-permute-start | bytes 98312 | tf_op jit(solution)/shard_map/ppermute | solution.py:61
  147.7 9.2 %collective-permute-start.5 = (bf16[32,512]{1,0:T(8,128)(2,1)S(1)}, bf16[32,512]{1,0:T(8,128)(2,1)S(1)}, u32[]{:S(2)}, u32[]{:S(2)}) collective-permute-start(bf16[32,512]{1,0:T(8,128)(2,1)S(1)} %add_convert_fusion.1), channel_id=1, source_target_pairs={{0,2},{2,0},{4,6},{6,4},{1,3},{3,1},{5,7},{7,5},{8,10},{10,8},{12,... | collective-permute-start | bytes 98312 | tf_op jit(solution)/shard_map/ppermute | solution.py:61
  149.6 24.4 %all-to-all-start.6 = ((bf16[4,32,512]{2,1,0:T(8,128)(2,1)}), bf16[4,32,512]{2,1,0:T(8,128)(2,1)S(1)}, u32[]{:S(2)}, u32[]{:S(2)}) async-start(bf16[4,32,512]{2,1,0:T(8,128)(2,1)} %shard_map.110), calls=%async_computation.6 | async-start | bytes 262144 | tf_op jit(solution)/shard_map/all_to_all | solution.py:56
  156.9 7.4 %collective-permute-start.6 = (bf16[32,512]{1,0:T(8,128)(2,1)S(1)}, bf16[32,512]{1,0:T(8,128)(2,1)S(1)}, u32[]{:S(2)}, u32[]{:S(2)}) collective-permute-start(bf16[32,512]{1,0:T(8,128)(2,1)S(1)} %add_convert_fusion), channel_id=1, source_target_pairs={{0,4},{2,6},{4,0},{6,2},{1,5},{3,7},{5,1},{7,3},{8,12},{10,14},{12... | collective-permute-start | bytes 98312 | tf_op jit(solution)/shard_map/ppermute | solution.py:61

commit v3 on v2

--- a/solution.py
+++ b/solution.py
@@ -161,17 +161,18 @@
 
 
 def grad_kernel(
-    place, sums4, query_t, keys, values, cot, tokens_hbm, other_hbm, blocks, both, other, tokens_t, other_t, sems
+    place, sums4, query_t, keys, values, cot, tokens_hbm, other_hbm, blocks_hbm, both, other_out, *scratch
 ):
+    tokens_t, other_t, blocks, other, sems = scratch
     fetch = pltpu.make_async_copy(tokens_hbm, tokens_t, sems.at[0])
     fetch_other = pltpu.make_async_copy(other_hbm, other_t, sems.at[1])
     fetch.start()
     fetch_other.start()
     heads = keys.shape[1] // HEAD_DIM
     sums = summed(sums4)
-    n, held, _ = blocks.shape
+    n, rows, _ = blocks.shape
     depth = tokens_t.shape[1]
-    each = held - depth
+    each = rows - depth
     denoms, deltas = [], []
     for h in range(heads):
         cols = slice(h * HEAD_DIM, (h + 1) * HEAD_DIM)
@@ -193,14 +194,24 @@
     query_grad = query_grad.astype(BF16)
     fetch.wait()
     tall = 4
+    leaving = []
     for j in range(0, n, tall):
         part = dot(tokens_t[j : j + tall].reshape(tall * depth, -1), both[...]).astype(BF16)
         for i in range(tall):
             blocks[j + i, :depth, :] = part[i * depth : (i + 1) * depth]
             blocks[j + i, depth:, :] = query_grad
+        group = pl.ds(j, tall)
+        leaving.append(
+            pltpu.make_async_copy(blocks.at[group], blocks_hbm.at[group], sems.at[2 + j // tall])
+        )
+        leaving[-1].start()
     fetch_other.wait()
     for k in range(other.shape[0]):
         other[k] = dot(both[...], other_t[k]).astype(BF16)
+    leaving.append(pltpu.make_async_copy(other, other_out, sems.at[2 + n // tall]))
+    leaving[-1].start()
+    for copy in leaving:
+        copy.wait()
 
 
 def pair_kernel(both, weights, other, here, *away):
@@ -291,8 +302,11 @@
         scratch=[
             pltpu.VMEM(tokens_t.shape, BF16),
             pltpu.VMEM(other_t.shape, BF16),
-            pltpu.SemaphoreType.DMA((2,)),
+            pltpu.VMEM((near, depth // near + each, 2 * width), BF16),
+            pltpu.VMEM((hops, rows, block), BF16),
+            pltpu.SemaphoreType.DMA((7,)),
         ],
+        out_specs=[HBM, whole(shape((rows, 2 * width), BF16)), HBM],
         limit=60,
     )
     arrived = exchange(blocks, NEAR)
@@ -305,8 +319,8 @@
         limit=60,
     )
     parts = [partner(away[k - 1], "z", k) for k in (2, 3, 1)]
-    arrived, here, *parts = lax.optimization_barrier((arrived, here, *parts))
     (token_grad,) = local(token_sum_kernel, [shape((rows, block), BF16)], [here, *parts], limit=60)
+    arrived, token_grad = lax.optimization_barrier((arrived, token_grad))
 
     (sent,) = local(
         near_sum_kernel,

time: 176 us -> 176 us (level)
    all_to_all x3, starting transfers between devices: 19.8 us -> 17.9 us  [exchange(): return lax.all_to_all(blocks, axes, split_axis=0, concat_axis=0, tiled=True)]
    ppermute x7, waiting for transfers between devices: 9.14 us -> 11 us  [partner(): return lax.ppermute(value, axis, [(i, i ^ flip) for i in range(size)])]
where the time goes in v3:
time: 176 us; the launch traced here: 175 us
  blocking collectives  85.8 us (49%)
  starting transfers between devices  40.4 us (23%)
  waiting for transfers between devices  22.1 us (13%)
  Pallas kernels  21.5 us (12%)
  local copies, waits for them, and re-layouts  2.82 us (2%)
    all_to_all x4, blocking collectives, exchange(): return lax.all_to_all(blocks, axes, split_axis=0, concat_axis=0, tiled=True)  85.8 us
    ppermute x7, starting transfers between devices, partner(): return lax.ppermute(value, axis, [(i, i ^ flip) for i in range(size)])  22.5 us
    pallas_call x11, Pallas kernels, local(): pl.pallas_call(body, out_shape=outs, grid=(grid,), in_specs=[specs.get(i)...  21.5 us
    all_to_all x3, starting transfers between devices, exchange(): return lax.all_to_all(blocks, axes, split_axis=0, concat_axis=0, tiled=True)  17.9 us
    all_to_all x3, waiting for transfers between devices, exchange(): return lax.all_to_all(blocks, axes, split_axis=0, concat_axis=0, tiled=True)  11.1 us
    ppermute x7, waiting for transfers between devices, partner(): return lax.ppermute(value, axis, [(i, i ^ flip) for i in range(size)])  11 us
  transfers between devices with their start and end apart: 10, of which 8 were waited for; matrix products, arithmetic and copies ran while one was open for 1% of the time, Pallas kernels for 5%

profile of v3, /device:TPU:8, one launch (start us, length us, event | category | flops | bytes accessed | tf_op | source)
XLA Modules:
  0.0 174.9 jit_solution(2945852359248106957)
XLA Ops:
  0.6 1.8 %shard_map.101 = f32[16,16,512]{2,1,0:T(8,128)} custom-call(bf16[32,256]{1,0:T(8,128)(2,1)} %w_query.1, bf16[32,512]{1,0:T(8,128)(2,1)} %bitcast.21), custom_call_target="tpu_custom_call" | custom-call | flops 8388608 | bytes 573440 | tf_op jit(solution)/shard_map/pallas_call | solution.py:43
  2.5 18.0 %all_to_all.35.blocks = f32[16,16,512]{2,1,0:T(8,128)S(1)} all-to-all(f32[16,16,512]{2,1,0:T(8,128)} %shard_map.101), channel_id=1, replica_groups=mesh['x'=4,'w'=4,'y'=4,'z'=4,'c'=2] {'x','y'}, dimensions={0} | all-to-all | bytes 1048576 | tf_op jit(solution)/shard_map/all_to_all | solution.py:56
  20.5 29.0 %all_to_all.36.blocks = f32[4,16,512]{2,1,0:T(8,128)S(1)} all-to-all(f32[4,16,512]{2,1,0:T(8,128)S(1)} %shard_map.102), channel_id=1, replica_groups=mesh['x'=4,'w'=4,'y'=4,'z'=4,'c'=2] {'w'}, dimensions={0} | all-to-all | bytes 262144 | tf_op jit(solution)/shard_map/all_to_all | solution.py:56
  49.5 0.7 shard_map.103
  50.3 4.9 %all-to-all-start.2 = ((bf16[16,16,512]{2,1,0:T(8,128)(2,1)}), bf16[16,16,512]{2,1,0:T(8,128)(2,1)S(1)}, u32[]{:S(2)}, u32[]{:S(2)}) async-start(bf16[16,16,512]{2,1,0:T(8,128)(2,1)} %shard_map.103), calls=%async_computation.2 | async-start | bytes 524288 | tf_op jit(solution)/shard_map/all_to_all | solution.py:56
  55.2 0.6 stack.19.place
  55.8 4.3 %shard_map.104 = (bf16[256,256]{1,0:T(8,128)(2,1)}, bf16[256,256]{1,0:T(8,128)(2,1)}, bf16[256,256]{1,0:T(8,128)(2,1)}, bf16[16,128,256]{2,1,0:T(8,128)(2,1)}, b...) custom-call(s32[5]{0:T(128)} %stack.19.place, bf16[256,2048]{1,0:T(8,128)(2,1)} %tokens.1, ...), custom_call_target="tpu_custom_call" | custom-call | flops 536870912 | bytes 6684692 | tf_op jit(solution)/shard_map/pallas_call | solution.py:43
  60.1 2.1 %all-to-all-done.2 = bf16[16,16,512]{2,1,0:T(8,128)(2,1)S(1)} async-done(((bf16[16,16,512]{2,1,0:T(8,128)(2,1)}), bf16[16,16,512]{2,1,0:T(8,128)(2,1)S(1)}, u32[]{:S(2)}, u32[]{:S(2)}) %all-to-all-start.2) | async-done | bytes 262176 | tf_op jit(solution)/shard_map/all_to_all | solution.py:56
  62.2 0.0 copy-start
  62.2 0.7 copy-done
  62.9 3.4 %shard_map.105 = f32[16,40,512]{2,1,0:T(8,128)} custom-call(s32[5]{0:T(128)} %stack.19.place, bf16[256,512]{1,0:T(8,128)(2,1)} %bitcast.19, bf16[256,256]{1,0:T(8,128)(2,1)} %get-tuple-element.24.keys, bf16[256,256]{1,0:T(8,128)(2,1)} %get-tuple-element.25.keys_t, bf16[256,256]{1,0:T(8,128)(2,1)} %get-tuple-element.26.values, bf16[512,256]{1,0:T(8,128)(2,1)} %cot.3), custom_call_target="tpu_custom_call" | custom-call | flops 402653184 | bytes 2228244 | tf_op jit(solution)/shard_map/pallas_call | solution.py:43
  66.3 18.8 %all_to_all.37.blocks = f32[16,40,512]{2,1,0:T(8,128)S(1)} all-to-all(f32[16,40,512]{2,1,0:T(8,128)} %shard_map.105), channel_id=1, replica_groups=mesh['x'=4,'w'=4,'y'=4,'z'=4,'c'=2] {'x','y'}, dimensions={0} | all-to-all | bytes 2621440 | tf_op jit(solution)/shard_map/all_to_all | solution.py:56
  85.2 0.1 shard_map.106
  85.2 19.9 %all_to_all.38.sums4 = f32[4,40,512]{2,1,0:T(8,128)} all-to-all(f32[4,40,512]{2,1,0:T(8,128)S(1)} %shard_map.106), channel_id=1, replica_groups=mesh['x'=4,'w'=4,'y'=4,'z'=4,'c'=2] {'w'}, dimensions={0} | all-to-all | bytes 655360 | tf_op jit(solution)/shard_map/all_to_all | solution.py:56
  105.2 5.2 %shard_map.107 = (bf16[16,144,512]{2,1,0:T(8,128)(2,1)}, bf16[256,512]{1,0:T(8,128)(2,1)}, bf16[4,256,256]{2,1,0:T(8,128)(2,1)}) custom-call(s32[5]{0:T(128)} %stack.19.place, f32[4,40,512]{2,1,0:T(8,128)} %all_to_all.38.sums4, bf16[256,512]{1,0:T(8,128)(2,1)} %bitcast.20, bf16[256,256]{1,0:T(8,128)(2,1)} %get-tuple-element.24.keys, ...), custom_call_target="tpu_custom_call" | custom-call | flops 1073741824 | bytes 6357012 | tf_op jit(solution)/shard_map/pallas_call | solution.py:43
  110.3 0.0 copy-start.7
  110.4 7.6 %all-to-all-start.5 = ((bf16[16,144,512]{2,1,0:T(8,128)(2,1)}), bf16[16,144,512]{2,1,0:T(8,128)(2,1)S(1)}, u32[]{:S(2)}, u32[]{:S(2)}) async-start(bf16[16,144,512]{2,1,0:T(8,128)(2,1)} %get-tuple-element.29), calls=%async_computation.5 | async-start | bytes 4718592 | tf_op jit(solution)/shard_map/all_to_all | solution.py:56
  117.9 0.0 copy-done.7
  117.9 1.9 %collective-permute-start = (bf16[4,256,256]{2,1,0:T(8,128)(2,1)S(1)}, bf16[4,256,256]{2,1,0:T(8,128)(2,1)S(1)}, u32[]{:S(2)}, u32[]{:S(2)}) collective-permute-start(bf16[4,256,256]{2,1,0:T(8,128)(2,1)S(1)} %copy-done.7), channel_id=1, source_target_pairs={{0,1},{1,0},{2,3},{3,2},{4,5},{5,4},{6,7},{7,6},{8,9},{9,8},{10,11... | collective-permute-start | bytes 1572872 | tf_op jit(solution)/shard_map/ppermute | solution.py:61
  119.9 1.9 %collective-permute-done.other = bf16[4,256,256]{2,1,0:T(8,128)(2,1)S(1)} collective-permute-done((bf16[4,256,256]{2,1,0:T(8,128)(2,1)S(1)}, bf16[4,256,256]{2,1,0:T(8,128)(2,1)S(1)}, u32[]{:S(2)}, u32[]{:S(2)}) %collective-permute-start) | collective-permute-done | bytes 524320 | tf_op jit(solution)/shard_map/ppermute | solution.py:61
  121.7 0.0 copy-start.1
  121.7 0.8 copy-done.1
  122.5 2.6 %shard_map.108 = (f32[256,256]{1,0:T(8,128)}, bf16[256,256]{1,0:T(8,128)(2,1)}, bf16[256,256]{1,0:T(8,128)(2,1)}, bf16[256,256]{1,0:T(8,128)(2,1)}) custom-call(bf16[256,512]{1,0:T(8,128)(2,1)} %get-tuple-element.30.both, bf16[4,512,256]{2,1,0:T(8,128)(2,1)} %get-tuple-element.31.weights, bf16[4,256,256]{2,1,0:T(8,128)(2,1)} %copy-done.1), custom_call_target="tpu_custom_call" | custom-call | flops 268435456 | bytes 2490368 | tf_op jit(solution)/shard_map/pallas_call | solution.py:43
  125.1 0.0 copy-start.6
  125.1 0.0 copy-start.2
  125.1 5.0 %collective-permute-start.1 = (bf16[256,256]{1,0:T(8,128)(2,1)}, bf16[256,256]{1,0:T(8,128)(2,1)S(1)}, u32[]{:S(2)}, u32[]{:S(2)}) collective-permute-start(bf16[256,256]{1,0:T(8,128)(2,1)} %get-tuple-element.34), channel_id=1, source_target_pairs={{0,4},{2,6},{4,0},{6,2},{1,5},{3,7},{5,1},{7,3},{8,12},{10,14},{12... | collective-permute-start | bytes 393224 | tf_op jit(solution)/shard_map/ppermute | solution.py:61
  130.1 4.5 %collective-permute-start.2 = (bf16[256,256]{1,0:T(8,128)(2,1)}, bf16[256,256]{1,0:T(8,128)(2,1)S(1)}, u32[]{:S(2)}, u32[]{:S(2)}) collective-permute-start(bf16[256,256]{1,0:T(8,128)(2,1)} %get-tuple-element.35), channel_id=1, source_target_pairs={{0,6},{2,4},{4,2},{6,0},{1,7},{3,5},{5,3},{7,1},{8,14},{10,12},{12... | collective-permute-start | bytes 393224 | tf_op jit(solution)/shard_map/ppermute | solution.py:61
  134.6 1.9 %collective-permute-start.3 = (bf16[256,256]{1,0:T(8,128)(2,1)}, bf16[256,256]{1,0:T(8,128)(2,1)S(1)}, u32[]{:S(2)}, u32[]{:S(2)}) collective-permute-start(bf16[256,256]{1,0:T(8,128)(2,1)} %get-tuple-element.36), channel_id=1, source_target_pairs={{0,2},{2,0},{4,6},{6,4},{1,3},{3,1},{5,7},{7,5},{8,10},{10,8},{12,... | collective-permute-start | bytes 393224 | tf_op jit(solution)/shard_map/ppermute | solution.py:61
  136.5 3.5 %collective-permute-done.1.one = bf16[256,256]{1,0:T(8,128)(2,1)S(1)} collective-permute-done((bf16[256,256]{1,0:T(8,128)(2,1)}, bf16[256,256]{1,0:T(8,128)(2,1)S(1)}, u32[]{:S(2)}, u32[]{:S(2)}) %collective-permute-start.1) | collective-permute-done | bytes 131104 | tf_op jit(solution)/shard_map/ppermute | solution.py:61
  140.0 0.0 copy-start.3
  140.0 0.2 collective-permute-done.2.two
  140.2 0.0 copy-start.4
  140.2 2.4 %collective-permute-done.3.three = bf16[256,256]{1,0:T(8,128)(2,1)S(1)} collective-permute-done((bf16[256,256]{1,0:T(8,128)(2,1)}, bf16[256,256]{1,0:T(8,128)(2,1)S(1)}, u32[]{:S(2)}, u32[]{:S(2)}) %collective-permute-start.3) | collective-permute-done | bytes 131104 | tf_op jit(solution)/shard_map/ppermute | solution.py:61
  142.6 0.0 copy-start.5
  142.6 0.0 copy-done.3
  142.6 0.0 copy-done.4
  142.6 0.7 copy-done.5
  143.3 1.8 %shard_map.109 = bf16[256,256]{1,0:T(8,128)(2,1)} custom-call(f32[256,256]{1,0:T(8,128)} %get-tuple-element.33.here, bf16[256,256]{1,0:T(8,128)(2,1)} %copy-done.3, bf16[256,256]{1,0:T(8,128)(2,1)} %copy-done.4, bf16[256,256]{1,0:T(8,128)(2,1)} %copy-done.5), custom_call_target="tpu_custom_call" | custom-call | bytes 786432 | tf_op jit(solution)/shard_map/pallas_call | solution.py:43
  145.1 0.0 all-to-all-done.5.arrived
  145.1 0.9 shard_map.110
  146.1 0.0 copy-done.6
  146.1 0.1 fusion
  146.2 1.9 %collective-permute-start.4 = (bf16[32,512]{1,0:T(8,128)(2,1)S(1)}, bf16[32,512]{1,0:T(8,128)(2,1)S(1)}, u32[]{:S(2)}, u32[]{:S(2)}) collective-permute-start(bf16[32,512]{1,0:T(8,128)(2,1)S(1)} %fusion), channel_id=1, source_target_pairs={{0,1},{1,0},{2,3},{3,2},{4,5},{5,4},{6,7},{7,6},{8,9},{9,8},{10,11... | collective-permute-start | bytes 98312 | tf_op jit(solution)/shard_map/ppermute | solution.py:61
  148.1 1.2 collective-permute-done.4
  149.3 2.5 %collective-permute-start.5 = (bf16[32,512]{1,0:T(8,128)(2,1)S(1)}, bf16[32,512]{1,0:T(8,128)(2,1)S(1)}, u32[]{:S(2)}, u32[]{:S(2)}) collective-permute-start(bf16[32,512]{1,0:T(8,128)(2,1)S(1)} %add_convert_fusion.1), channel_id=1, source_target_pairs={{0,2},{2,0},{4,6},{6,4},{1,3},{3,1},{5,7},{7,5},{8,10},{10,8},{12,... | collective-permute-start | bytes 98312 | tf_op jit(solution)/shard_map/ppermute | solution.py:61
  151.8 5.4 %all-to-all-start.6 = ((bf16[4,32,512]{2,1,0:T(8,128)(2,1)}), bf16[4,32,512]{2,1,0:T(8,128)(2,1)S(1)}, u32[]{:S(2)}, u32[]{:S(2)}) async-start(bf16[4,32,512]{2,1,0:T(8,128)(2,1)} %shard_map.110), calls=%async_computation.6 | async-start | bytes 262144 | tf_op jit(solution)/shard_map/all_to_all | solution.py:56
  157.2 0.0 collective-permute-done.5
  157.2 4.8 %collective-permute-start.6 = (bf16[32,512]{1,0:T(8,128)(2,1)S(1)}, bf16[32,512]{1,0:T(8,128)(2,1)S(1)}, u32[]{:S(2)}, u32[]{:S(2)}) collective-permute-start(bf16[32,512]{1,0:T(8,128)(2,1)S(1)} %add_convert_fusion), channel_id=1, source_target_pairs={{0,4},{2,6},{4,0},{6,2},{1,5},{3,7},{5,1},{7,3},{8,12},{10,14},{12... | collective-permute-start | bytes 98312 | tf_op jit(solution)/shard_map/ppermute | solution.py:61
  162.0 0.0 copy-done.2
  162.0 0.8 convolution_bitcast_fusion
  162.8 1.8 %collective-permute-done.6 = bf16[32,512]{1,0:T(8,128)(2,1)S(1)} collective-permute-done((bf16[32,512]{1,0:T(8,128)(2,1)S(1)}, bf16[32,512]{1,0:T(8,128)(2,1)S(1)}, u32[]{:S(2)}, u32[]{:S(2)}) %collective-permute-start.6) | collective-permute-done | bytes 32800 | tf_op jit(solution)/shard_map/ppermute | solution.py:61
  164.6 0.6 add_bitcast_fusion
  165.3 9.0 %all-to-all-done.6.arrived = bf16[4,32,512]{2,1,0:T(8,128)(2,1)S(1)} async-done(((bf16[4,32,512]{2,1,0:T(8,128)(2,1)}), bf16[4,32,512]{2,1,0:T(8,128)(2,1)S(1)}, u32[]{:S(2)}, u32[]{:S(2)}) %all-to-all-start.6) | async-done | bytes 131104 | tf_op jit(solution)/shard_map/all_to_all | solution.py:56
  174.3 0.6 shard_map.111
  (4 shorter events, 0.1 us)
Async XLA Ops:
  50.3 11.9 %all-to-all-start.2 = ((bf16[16,16,512]{2,1,0:T(8,128)(2,1)}), bf16[16,16,512]{2,1,0:T(8,128)(2,1)S(1)}, u32[]{:S(2)}, u32[]{:S(2)}) async-start(bf16[16,16,512]{2,1,0:T(8,128)(2,1)} %shard_map.103), calls=%async_computation.2 | async-start | bytes 524288 | tf_op jit(solution)/shard_map/all_to_all | solution.py:56
  62.2 0.7 copy-start
  110.3 7.6 %copy-start.7 = (bf16[4,256,256]{2,1,0:T(8,128)(2,1)S(1)}, bf16[4,256,256]{2,1,0:T(8,128)(2,1)}, u32[]{:S(2)}) copy-start(bf16[4,256,256]{2,1,0:T(8,128)(2,1)} %get-tuple-element.32) | copy-start | bytes 1572868
  110.4 34.8 %all-to-all-start.5 = ((bf16[16,144,512]{2,1,0:T(8,128)(2,1)}), bf16[16,144,512]{2,1,0:T(8,128)(2,1)S(1)}, u32[]{:S(2)}, u32[]{:S(2)}) async-start(bf16[16,144,512]{2,1,0:T(8,128)(2,1)} %get-tuple-element.29), calls=%async_computation.5 | async-start | bytes 4718592 | tf_op jit(solution)/shard_map/all_to_all | solution.py:56
  117.9 3.8 %collective-permute-start = (bf16[4,256,256]{2,1,0:T(8,128)(2,1)S(1)}, bf16[4,256,256]{2,1,0:T(8,128)(2,1)S(1)}, u32[]{:S(2)}, u32[]{:S(2)}) collective-permute-start(bf16[4,256,256]{2,1,0:T(8,128)(2,1)S(1)} %copy-done.7), channel_id=1, source_target_pairs={{0,1},{1,0},{2,3},{3,2},{4,5},{5,4},{6,7},{7,6},{8,9},{9,8},{10,11... | collective-permute-start | bytes 1572872 | tf_op jit(solution)/shard_map/ppermute | solution.py:61
  121.7 0.8 copy-start.1
  125.1 20.9 %copy-start.6 = (bf16[32,256]{1,0:T(8,128)(2,1)S(1)}, bf16[32,256]{1,0:T(8,128)(2,1)}, u32[]{:S(2)}) copy-start(bf16[32,256]{1,0:T(8,128)(2,1)} %w_query.1) | copy-start | bytes 49156
  125.1 36.9 %copy-start.2 = (bf16[512,32]{0,1:T(8,128)(2,1)S(1)}, bf16[512,32]{0,1:T(8,128)(2,1)}, u32[]{:S(2)}) copy-start(bf16[512,32]{0,1:T(8,128)(2,1)} %param.7) | copy-start | bytes 98308
  125.1 14.9 %collective-permute-start.1 = (bf16[256,256]{1,0:T(8,128)(2,1)}, bf16[256,256]{1,0:T(8,128)(2,1)S(1)}, u32[]{:S(2)}, u32[]{:S(2)}) collective-permute-start(bf16[256,256]{1,0:T(8,128)(2,1)} %get-tuple-element.34), channel_id=1, source_target_pairs={{0,4},{2,6},{4,0},{6,2},{1,5},{3,7},{5,1},{7,3},{8,12},{10,14},{12... | collective-permute-start | bytes 393224 | tf_op jit(solution)/shard_map/ppermute | solution.py:61
  130.1 10.1 %collective-permute-start.2 = (bf16[256,256]{1,0:T(8,128)(2,1)}, bf16[256,256]{1,0:T(8,128)(2,1)S(1)}, u32[]{:S(2)}, u32[]{:S(2)}) collective-permute-start(bf16[256,256]{1,0:T(8,128)(2,1)} %get-tuple-element.35), channel_id=1, source_target_pairs={{0,6},{2,4},{4,2},{6,0},{1,7},{3,5},{5,3},{7,1},{8,14},{10,12},{12... | collective-permute-start | bytes 393224 | tf_op jit(solution)/shard_map/ppermute | solution.py:61
  134.6 8.0 %collective-permute-start.3 = (bf16[256,256]{1,0:T(8,128)(2,1)}, bf16[256,256]{1,0:T(8,128)(2,1)S(1)}, u32[]{:S(2)}, u32[]{:S(2)}) collective-permute-start(bf16[256,256]{1,0:T(8,128)(2,1)} %get-tuple-element.36), channel_id=1, source_target_pairs={{0,2},{2,0},{4,6},{6,4},{1,3},{3,1},{5,7},{7,5},{8,10},{10,8},{12,... | collective-permute-start | bytes 393224 | tf_op jit(solution)/shard_map/ppermute | solution.py:61
  140.0 2.6 %copy-start.3 = (bf16[256,256]{1,0:T(8,128)(2,1)}, bf16[256,256]{1,0:T(8,128)(2,1)S(1)}, u32[]{:S(2)}) copy-start(bf16[256,256]{1,0:T(8,128)(2,1)S(1)} %collective-permute-done.1.one) | copy-start | bytes 393220
  140.2 2.4 %copy-start.4 = (bf16[256,256]{1,0:T(8,128)(2,1)}, bf16[256,256]{1,0:T(8,128)(2,1)S(1)}, u32[]{:S(2)}) copy-start(bf16[256,256]{1,0:T(8,128)(2,1)S(1)} %collective-permute-done.2.two) | copy-start | bytes 393220
  142.6 0.7 copy-start.5
  146.2 3.1 %collective-permute-start.4 = (bf16[32,512]{1,0:T(8,128)(2,1)S(1)}, bf16[32,512]{1,0:T(8,128)(2,1)S(1)}, u32[]{:S(2)}, u32[]{:S(2)}) collective-permute-start(bf16[32,512]{1,0:T(8,128)(2,1)S(1)} %fusion), channel_id=1, source_target_pairs={{0,1},{1,0},{2,3},{3,2},{4,5},{5,4},{6,7},{7,6},{8,9},{9,8},{10,11... | collective-permute-start | bytes 98312 | tf_op jit(solution)/shard_map/ppermute | solution.py:61
  149.3 7.9 %collective-permute-start.5 = (bf16[32,512]{1,0:T(8,128)(2,1)S(1)}, bf16[32,512]{1,0:T(8,128)(2,1)S(1)}, u32[]{:S(2)}, u32[]{:S(2)}) collective-permute-start(bf16[32,512]{1,0:T(8,128)(2,1)S(1)} %add_convert_fusion.1), channel_id=1, source_target_pairs={{0,2},{2,0},{4,6},{6,4},{1,3},{3,1},{5,7},{7,5},{8,10},{10,8},{12,... | collective-permute-start | bytes 98312 | tf_op jit(solution)/shard_map/ppermute | solution.py:61
  151.8 22.5 %all-to-all-start.6 = ((bf16[4,32,512]{2,1,0:T(8,128)(2,1)}), bf16[4,32,512]{2,1,0:T(8,128)(2,1)S(1)}, u32[]{:S(2)}, u32[]{:S(2)}) async-start(bf16[4,32,512]{2,1,0:T(8,128)(2,1)} %shard_map.110), calls=%async_computation.6 | async-start | bytes 262144 | tf_op jit(solution)/shard_map/all_to_all | solution.py:56
  157.2 7.4 %collective-permute-start.6 = (bf16[32,512]{1,0:T(8,128)(2,1)S(1)}, bf16[32,512]{1,0:T(8,128)(2,1)S(1)}, u32[]{:S(2)}, u32[]{:S(2)}) collective-permute-start(bf16[32,512]{1,0:T(8,128)(2,1)S(1)} %add_convert_fusion), channel_id=1, source_target_pairs={{0,4},{2,6},{4,0},{6,2},{1,5},{3,7},{5,1},{7,3},{8,12},{10,14},{12... | collective-permute-start | bytes 98312 | tf_op jit(solution)/shard_map/ppermute | solution.py:61

commit v4 on v2

--- a/solution.py
+++ b/solution.py
@@ -214,6 +214,13 @@
     out[...] = total.astype(BF16)
 
 
+def latent_sum_kernel(place, own, two, three, one, out, terms):
+    for k, term in enumerate((own, one, two, three)):
+        terms[k] = term[...].astype(F32)
+    z = place[2]
+    out[...] = ((terms[z] + terms[z ^ 1]) + terms[z ^ 2]) + terms[z ^ 3]
+
+
 def near_sum_kernel(arrived, out):
     acc = summed(arrived)
     share = out.shape[1]
@@ -247,9 +254,6 @@
         query_kernel, [shape((near, each, lats), F32)], [w_query, latents.T], 2 * share * width * lats, limit=60
     )
     query_part = exchange(query_part, NEAR)
-    query_part = exchange(sum_copies(query_part, far, F32), "w")
-    query_t = exchange(sum_copies(query_part, near, BF16), NEAR).reshape(width, lats)
-
     block = depth // n_head
     hops = n_head // 2
     keys, keys_t, values, tokens_t, other_t, own_t = local(
@@ -268,6 +272,12 @@
         limit=60,
     )
 
+    query_part = exchange(sum_copies(query_part, far, F32), "w")
+    query_part, keys, keys_t, values, tokens_t, other_t, own_t = lax.optimization_barrier(
+        (query_part, keys, keys_t, values, tokens_t, other_t, own_t)
+    )
+    query_t = exchange(sum_copies(query_part, near, BF16), NEAR).reshape(width, lats)
+
     (spread,) = local(
         expo_kernel,
         [shape((near, 2 * each + 4 * heads, lats), F32)],
@@ -305,8 +315,8 @@
         limit=60,
     )
     parts = [partner(away[k - 1], "z", k) for k in (2, 3, 1)]
-    arrived, here, *parts = lax.optimization_barrier((arrived, here, *parts))
     (token_grad,) = local(token_sum_kernel, [shape((rows, block), BF16)], [here, *parts], limit=60)
+    arrived, token_grad = lax.optimization_barrier((arrived, token_grad))
 
     (sent,) = local(
         near_sum_kernel,
@@ -323,9 +333,15 @@
     query_weight_grad = lax.dot_general(
         latents, query_grad_t, (((0,), (1,)), ((), ())), preferred_element_type=F32
     )
-    for axis, flip in (("c", 1), ("z", 1), ("z", 2)):
-        held = latent_grad_t.astype(BF16)
-        latent_grad_t = held.astype(F32) + partner(held, axis, flip).astype(F32)
+    held = latent_grad_t.astype(BF16)
+    held = (held.astype(F32) + partner(held, "c", 1).astype(F32)).astype(BF16)
+    (latent_grad_t,) = local(
+        latent_sum_kernel,
+        [shape((share, lats), F32)],
+        [place, held] + [partner(held, "z", k) for k in (2, 3, 1)],
+        specs=scalars,
+        scratch=[pltpu.VMEM((hops, share, lats), F32)],
+    )
     return (
         token_grad,
         latent_grad_t.T,

time: 176 us -> 173 us (0.983)
  the two profiles are of different devices: /device:TPU:8 before, /device:TPU:1 now
where the time goes in v4:
time: 173 us; the launch traced here: 171 us
  blocking collectives  67.8 us (39%)
  starting transfers between devices  57.8 us (33%)
  Pallas kernels  22.3 us (13%)
  waiting for transfers between devices  19.2 us (11%)
  local copies, waits for them, and re-layouts  2.15 us (1%)
    all_to_all x4, blocking collectives, exchange(): return lax.all_to_all(blocks, axes, split_axis=0, concat_axis=0, tiled=True)  67.8 us
    ppermute x8, starting transfers between devices, partner(): return lax.ppermute(value, axis, [(i, i ^ flip) for i in range(size)])  29.5 us
    all_to_all x3, starting transfers between devices, exchange(): return lax.all_to_all(blocks, axes, split_axis=0, concat_axis=0, tiled=True)  28.3 us
    pallas_call x12, Pallas kernels, local(): pl.pallas_call(body, out_shape=outs, grid=(grid,), in_specs=[specs.get(i)...  22.3 us
    ppermute x8, waiting for transfers between devices, partner(): return lax.ppermute(value, axis, [(i, i ^ flip) for i in range(size)])  11.9 us
    all_to_all x3, waiting for transfers between devices, exchange(): return lax.all_to_all(blocks, axes, split_axis=0, concat_axis=0, tiled=True)  7.27 us
  transfers between devices with their start and end apart: 11, of which 6 were waited for; matrix products, arithmetic and copies ran while one was open for 1% of the time, Pallas kernels for 6%

profile of v4, /device:TPU:1, one launch (start us, length us, event | category | flops | bytes accessed | tf_op | source)
XLA Modules:
  0.0 170.9 jit_solution(8606382133099235208)
XLA Ops:
  0.6 1.8 %shard_map.101 = f32[16,16,512]{2,1,0:T(8,128)} custom-call(bf16[32,256]{1,0:T(8,128)(2,1)} %w_query.1, bf16[32,512]{1,0:T(8,128)(2,1)} %bitcast.20), custom_call_target="tpu_custom_call" | custom-call | flops 8388608 | bytes 573440 | tf_op jit(solution)/shard_map/pallas_call | solution.py:43
  2.5 16.7 %all_to_all.35.blocks = f32[16,16,512]{2,1,0:T(8,128)S(1)} all-to-all(f32[16,16,512]{2,1,0:T(8,128)} %shard_map.101), channel_id=1, replica_groups=mesh['x'=4,'w'=4,'y'=4,'z'=4,'c'=2] {'x','y'}, dimensions={0} | all-to-all | bytes 1048576 | tf_op jit(solution)/shard_map/all_to_all | solution.py:56
  19.1 0.7 shard_map.102
  19.8 16.0 %all-to-all-start.1 = ((f32[4,16,512]{2,1,0:T(8,128)}), f32[4,16,512]{2,1,0:T(8,128)S(1)}, u32[]{:S(2)}, u32[]{:S(2)}) async-start(f32[4,16,512]{2,1,0:T(8,128)} %shard_map.102), calls=%async_computation.1 | async-start | bytes 262144 | tf_op jit(solution)/shard_map/all_to_all | solution.py:56
  35.8 0.7 stack.19.place
  36.5 4.3 %shard_map.103 = (bf16[256,256]{1,0:T(8,128)(2,1)}, bf16[256,256]{1,0:T(8,128)(2,1)}, bf16[256,256]{1,0:T(8,128)(2,1)}, bf16[16,128,256]{2,1,0:T(8,128)(2,1)}, b...) custom-call(s32[5]{0:T(128)} %stack.19.place, bf16[256,2048]{1,0:T(8,128)(2,1)} %tokens.1, ...), custom_call_target="tpu_custom_call" | custom-call | flops 536870912 | bytes 6684692 | tf_op jit(solution)/shard_map/pallas_call | solution.py:43
  40.8 7.3 %all-to-all-done.1.blocks = f32[4,16,512]{2,1,0:T(8,128)S(1)} async-done(((f32[4,16,512]{2,1,0:T(8,128)}), f32[4,16,512]{2,1,0:T(8,128)S(1)}, u32[]{:S(2)}, u32[]{:S(2)}) %all-to-all-start.1) | async-done | bytes 131104 | tf_op jit(solution)/shard_map/all_to_all | solution.py:56
  48.1 10.7 %all_to_all.36 = bf16[16,16,512]{2,1,0:T(8,128)(2,1)} all-to-all(bf16[16,16,512]{2,1,0:T(8,128)(2,1)S(1)} %shard_map.104), channel_id=1, replica_groups=mesh['x'=4,'w'=4,'y'=4,'z'=4,'c'=2] {'x','y'}, dimensions={0} | all-to-all | bytes 524288 | tf_op jit(solution)/shard_map/all_to_all | solution.py:56
  58.8 3.5 %shard_map.105 = f32[16,40,512]{2,1,0:T(8,128)} custom-call(s32[5]{0:T(128)} %stack.19.place, bf16[256,512]{1,0:T(8,128)(2,1)} %bitcast.18, bf16[256,256]{1,0:T(8,128)(2,1)} %get-tuple-element.38.keys, bf16[256,256]{1,0:T(8,128)(2,1)} %get-tuple-element.39.keys_t, bf16[256,256]{1,0:T(8,128)(2,1)} %get-tuple-element.40.values, bf16[512,256]{1,0:T(8,128)(2,1)} %cot.3), custom_call_target="tpu_custom_call" | custom-call | flops 402653184 | bytes 2228244 | tf_op jit(solution)/shard_map/pallas_call | solution.py:43
  62.2 16.9 %all_to_all.37.blocks = f32[16,40,512]{2,1,0:T(8,128)S(1)} all-to-all(f32[16,40,512]{2,1,0:T(8,128)} %shard_map.105), channel_id=1, replica_groups=mesh['x'=4,'w'=4,'y'=4,'z'=4,'c'=2] {'x','y'}, dimensions={0} | all-to-all | bytes 2621440 | tf_op jit(solution)/shard_map/all_to_all | solution.py:56
  79.1 0.1 shard_map.106
  79.2 23.5 %all_to_all.38.sums4 = f32[4,40,512]{2,1,0:T(8,128)} all-to-all(f32[4,40,512]{2,1,0:T(8,128)S(1)} %shard_map.106), channel_id=1, replica_groups=mesh['x'=4,'w'=4,'y'=4,'z'=4,'c'=2] {'w'}, dimensions={0} | all-to-all | bytes 655360 | tf_op jit(solution)/shard_map/all_to_all | solution.py:56
  102.7 4.9 %shard_map.107 = (bf16[16,144,512]{2,1,0:T(8,128)(2,1)}, bf16[256,512]{1,0:T(8,128)(2,1)}, bf16[4,256,256]{2,1,0:T(8,128)(2,1)}) custom-call(s32[5]{0:T(128)} %stack.19.place, f32[4,40,512]{2,1,0:T(8,128)} %all_to_all.38.sums4, bf16[256,512]{1,0:T(8,128)(2,1)} %bitcast.19, bf16[256,256]{1,0:T(8,128)(2,1)} %get-tuple-element.38.keys, ...), custom_call_target="tpu_custom_call" | custom-call | flops 1073741824 | bytes 6357012 | tf_op jit(solution)/shard_map/pallas_call | solution.py:43
  107.6 0.0 copy-start.7
  107.6 5.3 %all-to-all-start.5 = ((bf16[16,144,512]{2,1,0:T(8,128)(2,1)}), bf16[16,144,512]{2,1,0:T(8,128)(2,1)S(1)}, u32[]{:S(2)}, u32[]{:S(2)}) async-start(bf16[16,144,512]{2,1,0:T(8,128)(2,1)} %get-tuple-element.43), calls=%async_computation.5 | async-start | bytes 4718592 | tf_op jit(solution)/shard_map/all_to_all | solution.py:56
  112.9 0.0 copy-done.7
  112.9 8.2 %collective-permute-start = (bf16[4,256,256]{2,1,0:T(8,128)(2,1)S(1)}, bf16[4,256,256]{2,1,0:T(8,128)(2,1)S(1)}, u32[]{:S(2)}, u32[]{:S(2)}) collective-permute-start(bf16[4,256,256]{2,1,0:T(8,128)(2,1)S(1)} %copy-done.7), channel_id=1, source_target_pairs={{0,1},{1,0},{2,3},{3,2},{4,5},{5,4},{6,7},{7,6},{8,9},{9,8},{10,11... | collective-permute-start | bytes 1572872 | tf_op jit(solution)/shard_map/ppermute | solution.py:61
  121.1 1.5 collective-permute-done.other
  122.7 0.0 copy-start.1
  122.7 0.8 copy-done.1
  123.4 2.6 %shard_map.108 = (f32[256,256]{1,0:T(8,128)}, bf16[256,256]{1,0:T(8,128)(2,1)}, bf16[256,256]{1,0:T(8,128)(2,1)}, bf16[256,256]{1,0:T(8,128)(2,1)}) custom-call(bf16[256,512]{1,0:T(8,128)(2,1)} %get-tuple-element.44.both, bf16[4,512,256]{2,1,0:T(8,128)(2,1)} %get-tuple-element.45.weights, bf16[4,256,256]{2,1,0:T(8,128)(2,1)} %copy-done.1), custom_call_target="tpu_custom_call" | custom-call | flops 268435456 | bytes 2490368 | tf_op jit(solution)/shard_map/pallas_call | solution.py:43
  126.0 0.0 copy-start.6
  126.0 0.0 copy-start.2
  126.0 4.2 %collective-permute-start.1 = (bf16[256,256]{1,0:T(8,128)(2,1)}, bf16[256,256]{1,0:T(8,128)(2,1)S(1)}, u32[]{:S(2)}, u32[]{:S(2)}) collective-permute-start(bf16[256,256]{1,0:T(8,128)(2,1)} %get-tuple-element.48), channel_id=1, source_target_pairs={{0,4},{2,6},{4,0},{6,2},{1,5},{3,7},{5,1},{7,3},{8,12},{10,14},{12... | collective-permute-start | bytes 393224 | tf_op jit(solution)/shard_map/ppermute | solution.py:61
  130.2 4.0 %collective-permute-start.2 = (bf16[256,256]{1,0:T(8,128)(2,1)}, bf16[256,256]{1,0:T(8,128)(2,1)S(1)}, u32[]{:S(2)}, u32[]{:S(2)}) collective-permute-start(bf16[256,256]{1,0:T(8,128)(2,1)} %get-tuple-element.49), channel_id=1, source_target_pairs={{0,6},{2,4},{4,2},{6,0},{1,7},{3,5},{5,3},{7,1},{8,14},{10,12},{12... | collective-permute-start | bytes 393224 | tf_op jit(solution)/shard_map/ppermute | solution.py:61
  134.3 1.9 %collective-permute-start.3 = (bf16[256,256]{1,0:T(8,128)(2,1)}, bf16[256,256]{1,0:T(8,128)(2,1)S(1)}, u32[]{:S(2)}, u32[]{:S(2)}) collective-permute-start(bf16[256,256]{1,0:T(8,128)(2,1)} %get-tuple-element.50), channel_id=1, source_target_pairs={{0,2},{2,0},{4,6},{6,4},{1,3},{3,1},{5,7},{7,5},{8,10},{10,8},{12,... | collective-permute-start | bytes 393224 | tf_op jit(solution)/shard_map/ppermute | solution.py:61
  136.2 0.0 collective-permute-done.1.one
  136.2 0.0 copy-start.3
  136.2 2.3 %collective-permute-done.2.two = bf16[256,256]{1,0:T(8,128)(2,1)S(1)} collective-permute-done((bf16[256,256]{1,0:T(8,128)(2,1)}, bf16[256,256]{1,0:T(8,128)(2,1)S(1)}, u32[]{:S(2)}, u32[]{:S(2)}) %collective-permute-start.2) | collective-permute-done | bytes 131104 | tf_op jit(solution)/shard_map/ppermute | solution.py:61
  138.5 0.0 copy-start.4
  138.5 4.3 %collective-permute-done.3.three = bf16[256,256]{1,0:T(8,128)(2,1)S(1)} collective-permute-done((bf16[256,256]{1,0:T(8,128)(2,1)}, bf16[256,256]{1,0:T(8,128)(2,1)S(1)}, u32[]{:S(2)}, u32[]{:S(2)}) %collective-permute-start.3) | collective-permute-done | bytes 131104 | tf_op jit(solution)/shard_map/ppermute | solution.py:61
  142.8 0.0 copy-start.5
  142.8 0.0 copy-done.3
  142.8 0.0 copy-done.4
  142.8 0.6 copy-done.5
  143.5 0.0 copy-start
  143.5 1.8 %shard_map.109 = bf16[256,256]{1,0:T(8,128)(2,1)} custom-call(f32[256,256]{1,0:T(8,128)} %get-tuple-element.47.here, bf16[256,256]{1,0:T(8,128)(2,1)} %copy-done.3, bf16[256,256]{1,0:T(8,128)(2,1)} %copy-done.4, bf16[256,256]{1,0:T(8,128)(2,1)} %copy-done.5), custom_call_target="tpu_custom_call" | custom-call | bytes 786432 | tf_op jit(solution)/shard_map/pallas_call | solution.py:43
  145.3 0.0 all-to-all-done.5.arrived
  145.3 0.9 shard_map.110
  146.2 0.0 copy-done.6
  146.2 0.1 fusion
  146.4 2.7 %collective-permute-start.4 = (bf16[32,512]{1,0:T(8,128)(2,1)S(1)}, bf16[32,512]{1,0:T(8,128)(2,1)S(1)}, u32[]{:S(2)}, u32[]{:S(2)}) collective-permute-start(bf16[32,512]{1,0:T(8,128)(2,1)S(1)} %fusion), channel_id=1, source_target_pairs={{0,1},{1,0},{2,3},{3,2},{4,5},{5,4},{6,7},{7,6},{8,9},{9,8},{10,11... | collective-permute-start | bytes 98312 | tf_op jit(solution)/shard_map/ppermute | solution.py:61
  149.1 7.0 %all-to-all-start.6 = ((bf16[4,32,512]{2,1,0:T(8,128)(2,1)}), bf16[4,32,512]{2,1,0:T(8,128)(2,1)S(1)}, u32[]{:S(2)}, u32[]{:S(2)}) async-start(bf16[4,32,512]{2,1,0:T(8,128)(2,1)} %shard_map.110), calls=%async_computation.6 | async-start | bytes 262144 | tf_op jit(solution)/shard_map/all_to_all | solution.py:56
  156.1 0.0 collective-permute-done.4
  156.1 2.2 %collective-permute-start.7 = (bf16[32,512]{1,0:T(8,128)(2,1)S(1)}, bf16[32,512]{1,0:T(8,128)(2,1)S(1)}, u32[]{:S(2)}, u32[]{:S(2)}) collective-permute-start(bf16[32,512]{1,0:T(8,128)(2,1)S(1)} %add_convert_fusion.own), channel_id=1, source_target_pairs={{0,2},{2,0},{4,6},{6,4},{1,3},{3,1},{5,7},{7,5},{8,10},{10,8},{12,... | collective-permute-start | bytes 98312 | tf_op jit(solution)/shard_map/ppermute | solution.py:61
  158.3 3.5 %collective-permute-start.6 = (bf16[32,512]{1,0:T(8,128)(2,1)S(1)}, bf16[32,512]{1,0:T(8,128)(2,1)S(1)}, u32[]{:S(2)}, u32[]{:S(2)}) collective-permute-start(bf16[32,512]{1,0:T(8,128)(2,1)S(1)} %add_convert_fusion.own), channel_id=1, source_target_pairs={{0,6},{2,4},{4,2},{6,0},{1,7},{3,5},{5,3},{7,1},{8,14},{10,12},{12... | collective-permute-start | bytes 98312 | tf_op jit(solution)/shard_map/ppermute | solution.py:61
  161.8 2.7 %collective-permute-start.5 = (bf16[32,512]{1,0:T(8,128)(2,1)S(1)}, bf16[32,512]{1,0:T(8,128)(2,1)S(1)}, u32[]{:S(2)}, u32[]{:S(2)}) collective-permute-start(bf16[32,512]{1,0:T(8,128)(2,1)S(1)} %add_convert_fusion.own), channel_id=1, source_target_pairs={{0,4},{2,6},{4,0},{6,2},{1,5},{3,7},{5,1},{7,3},{8,12},{10,14},{12... | collective-permute-start | bytes 98312 | tf_op jit(solution)/shard_map/ppermute | solution.py:61
  164.5 0.0 copy-done.2
  164.5 0.8 convolution_bitcast_fusion
  165.3 0.0 collective-permute-done.7.one
  165.3 2.3 %collective-permute-done.6.three = bf16[32,512]{1,0:T(8,128)(2,1)S(1)} collective-permute-done((bf16[32,512]{1,0:T(8,128)(2,1)S(1)}, bf16[32,512]{1,0:T(8,128)(2,1)S(1)}, u32[]{:S(2)}, u32[]{:S(2)}) %collective-permute-start.6) | collective-permute-done | bytes 32800 | tf_op jit(solution)/shard_map/ppermute | solution.py:61
  167.6 1.5 collective-permute-done.5.two
  169.1 0.0 copy-done
  169.1 1.2 shard_map.111
  170.3 0.0 all-to-all-done.6.arrived
  170.3 0.6 shard_map.112
  (3 shorter events, 0.1 us)
Async XLA Ops:
  19.8 28.2 %all-to-all-start.1 = ((f32[4,16,512]{2,1,0:T(8,128)}), f32[4,16,512]{2,1,0:T(8,128)S(1)}, u32[]{:S(2)}, u32[]{:S(2)}) async-start(f32[4,16,512]{2,1,0:T(8,128)} %shard_map.102), calls=%async_computation.1 | async-start | bytes 262144 | tf_op jit(solution)/shard_map/all_to_all | solution.py:56
  107.6 5.3 %copy-start.7 = (bf16[4,256,256]{2,1,0:T(8,128)(2,1)S(1)}, bf16[4,256,256]{2,1,0:T(8,128)(2,1)}, u32[]{:S(2)}) copy-start(bf16[4,256,256]{2,1,0:T(8,128)(2,1)} %get-tuple-element.46) | copy-start | bytes 1572868
  107.6 37.7 %all-to-all-start.5 = ((bf16[16,144,512]{2,1,0:T(8,128)(2,1)}), bf16[16,144,512]{2,1,0:T(8,128)(2,1)S(1)}, u32[]{:S(2)}, u32[]{:S(2)}) async-start(bf16[16,144,512]{2,1,0:T(8,128)(2,1)} %get-tuple-element.43), calls=%async_computation.5 | async-start | bytes 4718592 | tf_op jit(solution)/shard_map/all_to_all | solution.py:56
  112.9 9.8 %collective-permute-start = (bf16[4,256,256]{2,1,0:T(8,128)(2,1)S(1)}, bf16[4,256,256]{2,1,0:T(8,128)(2,1)S(1)}, u32[]{:S(2)}, u32[]{:S(2)}) collective-permute-start(bf16[4,256,256]{2,1,0:T(8,128)(2,1)S(1)} %copy-done.7), channel_id=1, source_target_pairs={{0,1},{1,0},{2,3},{3,2},{4,5},{5,4},{6,7},{7,6},{8,9},{9,8},{10,11... | collective-permute-start | bytes 1572872 | tf_op jit(solution)/shard_map/ppermute | solution.py:61
  122.7 0.8 copy-start.1
  126.0 20.2 %copy-start.6 = (bf16[32,256]{1,0:T(8,128)(2,1)S(1)}, bf16[32,256]{1,0:T(8,128)(2,1)}, u32[]{:S(2)}) copy-start(bf16[32,256]{1,0:T(8,128)(2,1)} %w_query.1) | copy-start | bytes 49156
  126.0 38.5 %copy-start.2 = (bf16[512,32]{0,1:T(8,128)(2,1)S(1)}, bf16[512,32]{0,1:T(8,128)(2,1)}, u32[]{:S(2)}) copy-start(bf16[512,32]{0,1:T(8,128)(2,1)} %param.7) | copy-start | bytes 98308
  126.0 10.2 %collective-permute-start.1 = (bf16[256,256]{1,0:T(8,128)(2,1)}, bf16[256,256]{1,0:T(8,128)(2,1)S(1)}, u32[]{:S(2)}, u32[]{:S(2)}) collective-permute-start(bf16[256,256]{1,0:T(8,128)(2,1)} %get-tuple-element.48), channel_id=1, source_target_pairs={{0,4},{2,6},{4,0},{6,2},{1,5},{3,7},{5,1},{7,3},{8,12},{10,14},{12... | collective-permute-start | bytes 393224 | tf_op jit(solution)/shard_map/ppermute | solution.py:61
  130.2 8.3 %collective-permute-start.2 = (bf16[256,256]{1,0:T(8,128)(2,1)}, bf16[256,256]{1,0:T(8,128)(2,1)S(1)}, u32[]{:S(2)}, u32[]{:S(2)}) collective-permute-start(bf16[256,256]{1,0:T(8,128)(2,1)} %get-tuple-element.49), channel_id=1, source_target_pairs={{0,6},{2,4},{4,2},{6,0},{1,7},{3,5},{5,3},{7,1},{8,14},{10,12},{12... | collective-permute-start | bytes 393224 | tf_op jit(solution)/shard_map/ppermute | solution.py:61
  134.3 8.5 %collective-permute-start.3 = (bf16[256,256]{1,0:T(8,128)(2,1)}, bf16[256,256]{1,0:T(8,128)(2,1)S(1)}, u32[]{:S(2)}, u32[]{:S(2)}) collective-permute-start(bf16[256,256]{1,0:T(8,128)(2,1)} %get-tuple-element.50), channel_id=1, source_target_pairs={{0,2},{2,0},{4,6},{6,4},{1,3},{3,1},{5,7},{7,5},{8,10},{10,8},{12,... | collective-permute-start | bytes 393224 | tf_op jit(solution)/shard_map/ppermute | solution.py:61
  136.2 6.6 %copy-start.3 = (bf16[256,256]{1,0:T(8,128)(2,1)}, bf16[256,256]{1,0:T(8,128)(2,1)S(1)}, u32[]{:S(2)}) copy-start(bf16[256,256]{1,0:T(8,128)(2,1)S(1)} %collective-permute-done.1.one) | copy-start | bytes 393220
  138.5 4.3 %copy-start.4 = (bf16[256,256]{1,0:T(8,128)(2,1)}, bf16[256,256]{1,0:T(8,128)(2,1)S(1)}, u32[]{:S(2)}) copy-start(bf16[256,256]{1,0:T(8,128)(2,1)S(1)} %collective-permute-done.2.two) | copy-start | bytes 393220
  142.8 0.7 copy-start.5
  143.5 25.6 %copy-start = (s32[5]{0:T(128)S(1)}, s32[5]{0:T(128)}, u32[]{:S(2)}) copy-start(s32[5]{0:T(128)} %stack.19.place) | copy-start | bytes 64
  146.4 9.7 %collective-permute-start.4 = (bf16[32,512]{1,0:T(8,128)(2,1)S(1)}, bf16[32,512]{1,0:T(8,128)(2,1)S(1)}, u32[]{:S(2)}, u32[]{:S(2)}) collective-permute-start(bf16[32,512]{1,0:T(8,128)(2,1)S(1)} %fusion), channel_id=1, source_target_pairs={{0,1},{1,0},{2,3},{3,2},{4,5},{5,4},{6,7},{7,6},{8,9},{9,8},{10,11... | collective-permute-start | bytes 98312 | tf_op jit(solution)/shard_map/ppermute | solution.py:61
  149.1 21.2 %all-to-all-start.6 = ((bf16[4,32,512]{2,1,0:T(8,128)(2,1)}), bf16[4,32,512]{2,1,0:T(8,128)(2,1)S(1)}, u32[]{:S(2)}, u32[]{:S(2)}) async-start(bf16[4,32,512]{2,1,0:T(8,128)(2,1)} %shard_map.110), calls=%async_computation.6 | async-start | bytes 262144 | tf_op jit(solution)/shard_map/all_to_all | solution.py:56
  156.1 9.2 %collective-permute-start.7 = (bf16[32,512]{1,0:T(8,128)(2,1)S(1)}, bf16[32,512]{1,0:T(8,128)(2,1)S(1)}, u32[]{:S(2)}, u32[]{:S(2)}) collective-permute-start(bf16[32,512]{1,0:T(8,128)(2,1)S(1)} %add_convert_fusion.own), channel_id=1, source_target_pairs={{0,2},{2,0},{4,6},{6,4},{1,3},{3,1},{5,7},{7,5},{8,10},{10,8},{12,... | collective-permute-start | bytes 98312 | tf_op jit(solution)/shard_map/ppermute | solution.py:61
  158.3 9.3 %collective-permute-start.6 = (bf16[32,512]{1,0:T(8,128)(2,1)S(1)}, bf16[32,512]{1,0:T(8,128)(2,1)S(1)}, u32[]{:S(2)}, u32[]{:S(2)}) collective-permute-start(bf16[32,512]{1,0:T(8,128)(2,1)S(1)} %add_convert_fusion.own), channel_id=1, source_target_pairs={{0,6},{2,4},{4,2},{6,0},{1,7},{3,5},{5,3},{7,1},{8,14},{10,12},{12... | collective-permute-start | bytes 98312 | tf_op jit(solution)/shard_map/ppermute | solution.py:61
  161.8 7.3 %collective-permute-start.5 = (bf16[32,512]{1,0:T(8,128)(2,1)S(1)}, bf16[32,512]{1,0:T(8,128)(2,1)S(1)}, u32[]{:S(2)}, u32[]{:S(2)}) collective-permute-start(bf16[32,512]{1,0:T(8,128)(2,1)S(1)} %add_convert_fusion.own), channel_id=1, source_target_pairs={{0,4},{2,6},{4,0},{6,2},{1,5},{3,7},{5,1},{7,3},{8,12},{10,14},{12... | collective-permute-start | bytes 98312 | tf_op jit(solution)/shard_map/ppermute | solution.py:61

commit v5 on v4

--- a/solution.py
+++ b/solution.py
@@ -137,6 +137,27 @@
     return dot(a, high) + dot(a, low)
 
 
+def pack_sums(sums):
+    high = sums.astype(BF16).astype(F32)
+    middle = (sums - high).astype(BF16).astype(F32)
+    low = sums - high - middle
+    return jnp.concatenate([high, middle, low, jnp.zeros_like(sums)], axis=0).astype(BF16)
+
+
+def unpack_sums(rows):
+    rows = rows.astype(F32)
+    return rows[0:4] + rows[4:8] + rows[8:12]
+
+
+def mean_of(numer, denom):
+    return jnp.where(denom > 0, numer / jnp.where(denom > 0, denom, 1.0), 0.0)
+
+
+def mine_of(sums, place):
+    first = place[4] < 8
+    return jnp.where(first, sums[0:1], sums[2:3]), jnp.where(first, sums[1:2], sums[3:4])
+
+
 def expo_kernel(place, query_t, keys, keys_t, values, cot, spread):
     heads = keys.shape[1] // HEAD_DIM
     n = spread.shape[0]
@@ -147,17 +168,46 @@
         cols = slice(h * HEAD_DIM, (h + 1) * HEAD_DIM)
         expo = expo_of(place, h, query_t, keys)
         weighted = expo * (dprob_of(h, values, cot) * SHRINK)
-        sums.append(jnp.sum(expo, axis=0, keepdims=True))
-        sums.append(jnp.sum(weighted, axis=0, keepdims=True))
-        first = dot_split(keys_t[cols, :], weighted)
+        denom = jnp.sum(expo, axis=0, keepdims=True)
+        numer = jnp.sum(weighted, axis=0, keepdims=True)
+        sums += [denom, numer]
         second = dot_split(keys_t[cols, :], expo)
+        first = dot_split(keys_t[cols, :], weighted) - mean_of(numer, denom) * second
+        first, second = first.astype(BF16), second.astype(BF16)
         for j in range(per_head):
             rows = slice(j * each, (j + 1) * each)
             spread[h * per_head + j, :each, :] = first[rows, :]
             spread[h * per_head + j, each : 2 * each, :] = second[rows, :]
-    packed = jnp.concatenate(sums + sums, axis=0)
+    packed = pack_sums(jnp.concatenate(sums, axis=0))
     for j in range(n):
         spread[j, 2 * each :, :] = packed
+
+
+def gathered(blocks, place):
+    each = (blocks.shape[1] - 16) // 2
+    sent = [unpack_sums(blocks[d, 2 * each :, :]) for d in range(blocks.shape[0])]
+    sums = sent[0]
+    for part in sent[1:]:
+        sums = sums + part
+    denom, numer = mine_of(sums, place)
+    mean = mean_of(numer, denom)
+    first = second = 0.0
+    for d, part in enumerate(sent):
+        denom_d, numer_d = mine_of(part, place)
+        rows = blocks[d, each : 2 * each, :].astype(F32)
+        first = first + blocks[d, :each, :].astype(F32) + (mean_of(numer_d, denom_d) - mean) * rows
+        second = second + rows
+    return sums, first, second
+
+
+def sums_kernel(place, blocks, out):
+    sums, first, second = gathered(blocks, place)
+    each = first.shape[0]
+    first, second, packed = first.astype(BF16), second.astype(BF16), pack_sums(sums)
+    for j in range(out.shape[0]):
+        out[j, :each, :] = first
+        out[j, each : 2 * each, :] = second
+        out[j, 2 * each :, :] = packed
 
 
 def grad_kernel(
@@ -168,29 +218,20 @@
     fetch.start()
     fetch_other.start()
     heads = keys.shape[1] // HEAD_DIM
-    sums = summed(sums4)
+    sums, centred, _ = gathered(sums4, place)
     n, held, _ = blocks.shape
     depth = tokens_t.shape[1]
     each = held - depth
-    denoms, deltas = [], []
     for h in range(heads):
         cols = slice(h * HEAD_DIM, (h + 1) * HEAD_DIM)
-        at = 2 * each + 2 * h
-        denom = sums[at : at + 1, :]
-        shrunk = sums[at + 1 : at + 2, :] / denom
-        delta = shrunk * (1.0 / SHRINK)
-        denoms.append(denom)
-        deltas.append(shrunk)
+        denom = sums[2 * h : 2 * h + 1, :]
+        delta = sums[2 * h + 1 : 2 * h + 2, :] / denom * (1.0 / SHRINK)
         probs = expo_of(place, h, query_t, keys) / denom
         grad = (probs * (dprob_of(h, values, cot) - delta) * SCALE).astype(BF16)
         both[:, cols] = dot_nt(grad, query_t[cols, :]).astype(BF16)
         value_cols = slice((heads + h) * HEAD_DIM, (heads + h + 1) * HEAD_DIM)
         both[:, value_cols] = dot(probs.astype(BF16), cot[:, cols]).astype(BF16)
-    first_head = place[4] * heads < n
-    denom = jnp.where(first_head, denoms[0], denoms[1])
-    shrunk = jnp.where(first_head, deltas[0], deltas[1])
-    query_grad = (sums[:each] - shrunk * sums[each : 2 * each]) / denom * (SCALE / SHRINK)
-    query_grad = query_grad.astype(BF16)
+    query_grad = (centred / mine_of(sums, place)[0] * (SCALE / SHRINK)).astype(BF16)
     fetch.wait()
     tall = 4
     for j in range(0, n, tall):
@@ -280,13 +321,19 @@
 
     (spread,) = local(
         expo_kernel,
-        [shape((near, 2 * each + 4 * heads, lats), F32)],
+        [shape((near, 2 * each + 16, lats), BF16)],
         [place, query_t, keys, keys_t, values, cotangent],
         12 * rows * width * lats,
         specs=scalars,
         limit=60,
     )
-    sums = exchange(sum_copies(exchange(spread, NEAR), far, F32), "w")
+    (spread,) = local(
+        sums_kernel,
+        [shape((far,) + spread.shape[1:], BF16)],
+        [place, exchange(spread, NEAR)],
+        specs=scalars,
+    )
+    sums = exchange(spread, "w")
 
     blocks, both, other = local(
         grad_kernel,

time: 173 us -> 162 us (0.936)
  blocking collectives: 67.8 us -> 59.1 us
  starting transfers between devices: 57.8 us -> 53.6 us
    all_to_all x4, blocking collectives: 67.8 us -> 59.1 us  [exchange(): return lax.all_to_all(blocks, axes, split_axis=0, concat_axis=0, tiled=True)]
    all_to_all x3, starting transfers between devices: 28.3 us -> 23.5 us  [exchange(): return lax.all_to_all(blocks, axes, split_axis=0, concat_axis=0, tiled=True)]
  transfers between devices with their start and end apart: 11 -> 11, of which waited for: 6 -> 7; matrix products, arithmetic and copies ran while one was open for 1% -> 1% of each run, Pallas kernels for 6% -> 6%
where the time goes in v5:
time: 162 us; the launch traced here: 159 us
  blocking collectives  59.1 us (36%)
  starting transfers between devices  53.6 us (33%)
  Pallas kernels  23 us (14%)
  waiting for transfers between devices  19.9 us (12%)
  local copies, waits for them, and re-layouts  2.14 us (1%)
    all_to_all x4, blocking collectives, exchange(): return lax.all_to_all(blocks, axes, split_axis=0, concat_axis=0, tiled=True)  59.1 us
    ppermute x8, starting transfers between devices, partner(): return lax.ppermute(value, axis, [(i, i ^ flip) for i in range(size)])  30.1 us
    all_to_all x3, starting transfers between devices, exchange(): return lax.all_to_all(blocks, axes, split_axis=0, concat_axis=0, tiled=True)  23.5 us
    pallas_call x12, Pallas kernels, local(): pl.pallas_call(body, out_shape=outs, grid=(grid,), in_specs=[specs.get(i)...  23 us
    ppermute x8, waiting for transfers between devices, partner(): return lax.ppermute(value, axis, [(i, i ^ flip) for i in range(size)])  12.6 us
    all_to_all x3, waiting for transfers between devices, exchange(): return lax.all_to_all(blocks, axes, split_axis=0, concat_axis=0, tiled=True)  7.28 us
  transfers between devices with their start and end apart: 11, of which 7 were waited for; matrix products, arithmetic and copies ran while one was open for 1% of the time, Pallas kernels for 6%

profile of v5, /device:TPU:1, one launch (start us, length us, event | category | flops | bytes accessed | tf_op | source)
XLA Modules:
  0.0 159.5 jit_solution(16952304327587512754)
XLA Ops:
  0.6 1.8 %shard_map.101 = f32[16,16,512]{2,1,0:T(8,128)} custom-call(bf16[32,256]{1,0:T(8,128)(2,1)} %w_query.1, bf16[32,512]{1,0:T(8,128)(2,1)} %bitcast.20), custom_call_target="tpu_custom_call" | custom-call | flops 8388608 | bytes 573440 | tf_op jit(solution)/shard_map/pallas_call | solution.py:43
  2.5 16.7 %all_to_all.35.blocks = f32[16,16,512]{2,1,0:T(8,128)S(1)} all-to-all(f32[16,16,512]{2,1,0:T(8,128)} %shard_map.101), channel_id=1, replica_groups=mesh['x'=4,'w'=4,'y'=4,'z'=4,'c'=2] {'x','y'}, dimensions={0} | all-to-all | bytes 1048576 | tf_op jit(solution)/shard_map/all_to_all | solution.py:56
  19.1 0.7 shard_map.102
  19.8 16.0 %all-to-all-start.1 = ((f32[4,16,512]{2,1,0:T(8,128)}), f32[4,16,512]{2,1,0:T(8,128)S(1)}, u32[]{:S(2)}, u32[]{:S(2)}) async-start(f32[4,16,512]{2,1,0:T(8,128)} %shard_map.102), calls=%async_computation.1 | async-start | bytes 262144 | tf_op jit(solution)/shard_map/all_to_all | solution.py:56
  35.8 0.7 stack.19.place
  36.5 4.3 %shard_map.103 = (bf16[256,256]{1,0:T(8,128)(2,1)}, bf16[256,256]{1,0:T(8,128)(2,1)}, bf16[256,256]{1,0:T(8,128)(2,1)}, bf16[16,128,256]{2,1,0:T(8,128)(2,1)}, b...) custom-call(s32[5]{0:T(128)} %stack.19.place, bf16[256,2048]{1,0:T(8,128)(2,1)} %tokens.1, ...), custom_call_target="tpu_custom_call" | custom-call | flops 536870912 | bytes 6684692 | tf_op jit(solution)/shard_map/pallas_call | solution.py:43
  40.8 0.0 copy-start
  40.8 7.3 %all-to-all-done.1.blocks = f32[4,16,512]{2,1,0:T(8,128)S(1)} async-done(((f32[4,16,512]{2,1,0:T(8,128)}), f32[4,16,512]{2,1,0:T(8,128)S(1)}, u32[]{:S(2)}, u32[]{:S(2)}) %all-to-all-start.1) | async-done | bytes 131104 | tf_op jit(solution)/shard_map/all_to_all | solution.py:56
  48.1 10.7 %all_to_all.36 = bf16[16,16,512]{2,1,0:T(8,128)(2,1)} all-to-all(bf16[16,16,512]{2,1,0:T(8,128)(2,1)S(1)} %shard_map.104), channel_id=1, replica_groups=mesh['x'=4,'w'=4,'y'=4,'z'=4,'c'=2] {'x','y'}, dimensions={0} | all-to-all | bytes 524288 | tf_op jit(solution)/shard_map/all_to_all | solution.py:56
  58.8 3.3 %shard_map.105 = bf16[16,48,512]{2,1,0:T(8,128)(2,1)} custom-call(s32[5]{0:T(128)} %stack.19.place, bf16[256,512]{1,0:T(8,128)(2,1)} %bitcast.18, bf16[256,256]{1,0:T(8,128)(2,1)} %get-tuple-element.38.keys, bf16[256,256]{1,0:T(8,128)(2,1)} %get-tuple-element.39.keys_t, bf16[256,256]{1,0:T(8,128)(2,1)} %get-tuple-element.40.values, bf16[512,256]{1,0:T(8,128)(2,1)} %cot.3), custom_call_target="tpu_custom_call" | custom-call | flops 402653184 | bytes 1703956 | tf_op jit(solution)/shard_map/pallas_call | solution.py:43
  62.1 13.7 %all_to_all.37.blocks = bf16[16,48,512]{2,1,0:T(8,128)(2,1)S(1)} all-to-all(bf16[16,48,512]{2,1,0:T(8,128)(2,1)} %shard_map.105), channel_id=1, replica_groups=mesh['x'=4,'w'=4,'y'=4,'z'=4,'c'=2] {'x','y'}, dimensions={0} | all-to-all | bytes 1572864 | tf_op jit(solution)/shard_map/all_to_all | solution.py:56
  75.8 0.0 copy-done
  75.8 0.8 shard_map.106
  76.7 18.0 %all_to_all.38.sums4 = bf16[4,48,512]{2,1,0:T(8,128)(2,1)} all-to-all(bf16[4,48,512]{2,1,0:T(8,128)(2,1)S(1)} %shard_map.106), channel_id=1, replica_groups=mesh['x'=4,'w'=4,'y'=4,'z'=4,'c'=2] {'w'}, dimensions={0} | all-to-all | bytes 393216 | tf_op jit(solution)/shard_map/all_to_all | solution.py:56
  94.6 4.9 %shard_map.107 = (bf16[16,144,512]{2,1,0:T(8,128)(2,1)}, bf16[256,512]{1,0:T(8,128)(2,1)}, bf16[4,256,256]{2,1,0:T(8,128)(2,1)}) custom-call(s32[5]{0:T(128)} %stack.19.place, bf16[4,48,512]{2,1,0:T(8,128)(2,1)} %all_to_all.38.sums4, bf16[256,512]{1,0:T(8,128)(2,1)} %bitcast.19, bf16[256,256]{1,0:T(8,128)(2,1)} %get-tuple-element.38.keys, ...), custom_call_target="tpu_custom_call" | custom-call | flops 1073741824 | bytes 6225940 | tf_op jit(solution)/shard_map/pallas_call | solution.py:43
  99.5 0.0 copy-start.8
  99.5 4.1 %all-to-all-start.5 = ((bf16[16,144,512]{2,1,0:T(8,128)(2,1)}), bf16[16,144,512]{2,1,0:T(8,128)(2,1)S(1)}, u32[]{:S(2)}, u32[]{:S(2)}) async-start(bf16[16,144,512]{2,1,0:T(8,128)(2,1)} %get-tuple-element.43), calls=%async_computation.5 | async-start | bytes 4718592 | tf_op jit(solution)/shard_map/all_to_all | solution.py:56
  103.7 0.0 copy-done.8
  103.7 9.5 %collective-permute-start = (bf16[4,256,256]{2,1,0:T(8,128)(2,1)S(1)}, bf16[4,256,256]{2,1,0:T(8,128)(2,1)S(1)}, u32[]{:S(2)}, u32[]{:S(2)}) collective-permute-start(bf16[4,256,256]{2,1,0:T(8,128)(2,1)S(1)} %copy-done.8), channel_id=1, source_target_pairs={{0,1},{1,0},{2,3},{3,2},{4,5},{5,4},{6,7},{7,6},{8,9},{9,8},{10,11... | collective-permute-start | bytes 1572872 | tf_op jit(solution)/shard_map/ppermute | solution.py:61
  113.2 1.5 collective-permute-done.other
  114.7 0.0 copy-start.2
  114.7 0.8 copy-done.2
  115.5 2.6 %shard_map.108 = (f32[256,256]{1,0:T(8,128)}, bf16[256,256]{1,0:T(8,128)(2,1)}, bf16[256,256]{1,0:T(8,128)(2,1)}, bf16[256,256]{1,0:T(8,128)(2,1)}) custom-call(bf16[256,512]{1,0:T(8,128)(2,1)} %get-tuple-element.44.both, bf16[4,512,256]{2,1,0:T(8,128)(2,1)} %get-tuple-element.45.weights, bf16[4,256,256]{2,1,0:T(8,128)(2,1)} %copy-done.2), custom_call_target="tpu_custom_call" | custom-call | flops 268435456 | bytes 2490368 | tf_op jit(solution)/shard_map/pallas_call | solution.py:43
  118.1 0.0 copy-start.7
  118.1 0.0 copy-start.3
  118.1 4.7 %collective-permute-start.1 = (bf16[256,256]{1,0:T(8,128)(2,1)}, bf16[256,256]{1,0:T(8,128)(2,1)S(1)}, u32[]{:S(2)}, u32[]{:S(2)}) collective-permute-start(bf16[256,256]{1,0:T(8,128)(2,1)} %get-tuple-element.48), channel_id=1, source_target_pairs={{0,4},{2,6},{4,0},{6,2},{1,5},{3,7},{5,1},{7,3},{8,12},{10,14},{12... | collective-permute-start | bytes 393224 | tf_op jit(solution)/shard_map/ppermute | solution.py:61
  122.7 3.2 %collective-permute-start.2 = (bf16[256,256]{1,0:T(8,128)(2,1)}, bf16[256,256]{1,0:T(8,128)(2,1)S(1)}, u32[]{:S(2)}, u32[]{:S(2)}) collective-permute-start(bf16[256,256]{1,0:T(8,128)(2,1)} %get-tuple-element.49), channel_id=1, source_target_pairs={{0,6},{2,4},{4,2},{6,0},{1,7},{3,5},{5,3},{7,1},{8,14},{10,12},{12... | collective-permute-start | bytes 393224 | tf_op jit(solution)/shard_map/ppermute | solution.py:61
  125.9 1.9 %collective-permute-start.3 = (bf16[256,256]{1,0:T(8,128)(2,1)}, bf16[256,256]{1,0:T(8,128)(2,1)S(1)}, u32[]{:S(2)}, u32[]{:S(2)}) collective-permute-start(bf16[256,256]{1,0:T(8,128)(2,1)} %get-tuple-element.50), channel_id=1, source_target_pairs={{0,2},{2,0},{4,6},{6,4},{1,3},{3,1},{5,7},{7,5},{8,10},{10,8},{12,... | collective-permute-start | bytes 393224 | tf_op jit(solution)/shard_map/ppermute | solution.py:61
  127.8 1.5 collective-permute-done.1.one
  129.3 0.0 copy-start.4
  129.3 1.8 %collective-permute-done.2.two = bf16[256,256]{1,0:T(8,128)(2,1)S(1)} collective-permute-done((bf16[256,256]{1,0:T(8,128)(2,1)}, bf16[256,256]{1,0:T(8,128)(2,1)S(1)}, u32[]{:S(2)}, u32[]{:S(2)}) %collective-permute-start.2) | collective-permute-done | bytes 131104 | tf_op jit(solution)/shard_map/ppermute | solution.py:61
  131.1 0.0 copy-start.5
  131.1 4.2 %collective-permute-done.3.three = bf16[256,256]{1,0:T(8,128)(2,1)S(1)} collective-permute-done((bf16[256,256]{1,0:T(8,128)(2,1)}, bf16[256,256]{1,0:T(8,128)(2,1)S(1)}, u32[]{:S(2)}, u32[]{:S(2)}) %collective-permute-start.3) | collective-permute-done | bytes 131104 | tf_op jit(solution)/shard_map/ppermute | solution.py:61
  135.3 0.0 copy-start.6
  135.3 0.0 copy-done.4
  135.3 0.0 copy-done.5
  135.3 0.7 copy-done.6
  135.9 0.0 copy-start.1
  136.0 1.8 %shard_map.109 = bf16[256,256]{1,0:T(8,128)(2,1)} custom-call(f32[256,256]{1,0:T(8,128)} %get-tuple-element.47.here, bf16[256,256]{1,0:T(8,128)(2,1)} %copy-done.4, bf16[256,256]{1,0:T(8,128)(2,1)} %copy-done.5, bf16[256,256]{1,0:T(8,128)(2,1)} %copy-done.6), custom_call_target="tpu_custom_call" | custom-call | bytes 786432 | tf_op jit(solution)/shard_map/pallas_call | solution.py:43
  137.8 0.0 all-to-all-done.5.arrived
  137.8 0.9 shard_map.110
  138.7 0.0 copy-done.7
  138.7 0.1 fusion
  138.9 2.5 %collective-permute-start.4 = (bf16[32,512]{1,0:T(8,128)(2,1)S(1)}, bf16[32,512]{1,0:T(8,128)(2,1)S(1)}, u32[]{:S(2)}, u32[]{:S(2)}) collective-permute-start(bf16[32,512]{1,0:T(8,128)(2,1)S(1)} %fusion), channel_id=1, source_target_pairs={{0,1},{1,0},{2,3},{3,2},{4,5},{5,4},{6,7},{7,6},{8,9},{9,8},{10,11... | collective-permute-start | bytes 98312 | tf_op jit(solution)/shard_map/ppermute | solution.py:61
  141.4 3.3 %all-to-all-start.6 = ((bf16[4,32,512]{2,1,0:T(8,128)(2,1)}), bf16[4,32,512]{2,1,0:T(8,128)(2,1)S(1)}, u32[]{:S(2)}, u32[]{:S(2)}) async-start(bf16[4,32,512]{2,1,0:T(8,128)(2,1)} %shard_map.110), calls=%async_computation.6 | async-start | bytes 262144 | tf_op jit(solution)/shard_map/all_to_all | solution.py:56
  144.7 0.0 collective-permute-done.4
  144.8 2.2 %collective-permute-start.7 = (bf16[32,512]{1,0:T(8,128)(2,1)S(1)}, bf16[32,512]{1,0:T(8,128)(2,1)S(1)}, u32[]{:S(2)}, u32[]{:S(2)}) collective-permute-start(bf16[32,512]{1,0:T(8,128)(2,1)S(1)} %add_convert_fusion.own), channel_id=1, source_target_pairs={{0,2},{2,0},{4,6},{6,4},{1,3},{3,1},{5,7},{7,5},{8,10},{10,8},{12,... | collective-permute-start | bytes 98312 | tf_op jit(solution)/shard_map/ppermute | solution.py:61
  147.0 3.2 %collective-permute-start.6 = (bf16[32,512]{1,0:T(8,128)(2,1)S(1)}, bf16[32,512]{1,0:T(8,128)(2,1)S(1)}, u32[]{:S(2)}, u32[]{:S(2)}) collective-permute-start(bf16[32,512]{1,0:T(8,128)(2,1)S(1)} %add_convert_fusion.own), channel_id=1, source_target_pairs={{0,6},{2,4},{4,2},{6,0},{1,7},{3,5},{5,3},{7,1},{8,14},{10,12},{12... | collective-permute-start | bytes 98312 | tf_op jit(solution)/shard_map/ppermute | solution.py:61
  150.1 3.0 %collective-permute-start.5 = (bf16[32,512]{1,0:T(8,128)(2,1)S(1)}, bf16[32,512]{1,0:T(8,128)(2,1)S(1)}, u32[]{:S(2)}, u32[]{:S(2)}) collective-permute-start(bf16[32,512]{1,0:T(8,128)(2,1)S(1)} %add_convert_fusion.own), channel_id=1, source_target_pairs={{0,4},{2,6},{4,0},{6,2},{1,5},{3,7},{5,1},{7,3},{8,12},{10,14},{12... | collective-permute-start | bytes 98312 | tf_op jit(solution)/shard_map/ppermute | solution.py:61
  153.2 0.0 copy-done.3
  153.2 0.8 convolution_bitcast_fusion
  154.0 0.0 collective-permute-done.7.one
  154.0 1.9 %collective-permute-done.6.three = bf16[32,512]{1,0:T(8,128)(2,1)S(1)} collective-permute-done((bf16[32,512]{1,0:T(8,128)(2,1)S(1)}, bf16[32,512]{1,0:T(8,128)(2,1)S(1)}, u32[]{:S(2)}, u32[]{:S(2)}) %collective-permute-start.6) | collective-permute-done | bytes 32800 | tf_op jit(solution)/shard_map/ppermute | solution.py:61
  155.9 1.8 %collective-permute-done.5.two = bf16[32,512]{1,0:T(8,128)(2,1)S(1)} collective-permute-done((bf16[32,512]{1,0:T(8,128)(2,1)S(1)}, bf16[32,512]{1,0:T(8,128)(2,1)S(1)}, u32[]{:S(2)}, u32[]{:S(2)}) %collective-permute-start.5) | collective-permute-done | bytes 32800 | tf_op jit(solution)/shard_map/ppermute | solution.py:61
  157.6 0.0 copy-done.1
  157.6 1.2 shard_map.111
  158.9 0.0 all-to-all-done.6.arrived
  158.9 0.6 shard_map.112
  (3 shorter events, 0.1 us)
Async XLA Ops:
  19.8 28.2 %all-to-all-start.1 = ((f32[4,16,512]{2,1,0:T(8,128)}), f32[4,16,512]{2,1,0:T(8,128)S(1)}, u32[]{:S(2)}, u32[]{:S(2)}) async-start(f32[4,16,512]{2,1,0:T(8,128)} %shard_map.102), calls=%async_computation.1 | async-start | bytes 262144 | tf_op jit(solution)/shard_map/all_to_all | solution.py:56
  40.8 35.1 %copy-start = (s32[5]{0:T(128)S(1)}, s32[5]{0:T(128)}, u32[]{:S(2)}) copy-start(s32[5]{0:T(128)} %stack.19.place) | copy-start | bytes 64
  99.5 4.1 %copy-start.8 = (bf16[4,256,256]{2,1,0:T(8,128)(2,1)S(1)}, bf16[4,256,256]{2,1,0:T(8,128)(2,1)}, u32[]{:S(2)}) copy-start(bf16[4,256,256]{2,1,0:T(8,128)(2,1)} %get-tuple-element.46) | copy-start | bytes 1572868
  99.5 38.3 %all-to-all-start.5 = ((bf16[16,144,512]{2,1,0:T(8,128)(2,1)}), bf16[16,144,512]{2,1,0:T(8,128)(2,1)S(1)}, u32[]{:S(2)}, u32[]{:S(2)}) async-start(bf16[16,144,512]{2,1,0:T(8,128)(2,1)} %get-tuple-element.43), calls=%async_computation.5 | async-start | bytes 4718592 | tf_op jit(solution)/shard_map/all_to_all | solution.py:56
  103.7 11.0 %collective-permute-start = (bf16[4,256,256]{2,1,0:T(8,128)(2,1)S(1)}, bf16[4,256,256]{2,1,0:T(8,128)(2,1)S(1)}, u32[]{:S(2)}, u32[]{:S(2)}) collective-permute-start(bf16[4,256,256]{2,1,0:T(8,128)(2,1)S(1)} %copy-done.8), channel_id=1, source_target_pairs={{0,1},{1,0},{2,3},{3,2},{4,5},{5,4},{6,7},{7,6},{8,9},{9,8},{10,11... | collective-permute-start | bytes 1572872 | tf_op jit(solution)/shard_map/ppermute | solution.py:61
  114.7 0.8 copy-start.2
  118.1 20.7 %copy-start.7 = (bf16[32,256]{1,0:T(8,128)(2,1)S(1)}, bf16[32,256]{1,0:T(8,128)(2,1)}, u32[]{:S(2)}) copy-start(bf16[32,256]{1,0:T(8,128)(2,1)} %w_query.1) | copy-start | bytes 49156
  118.1 35.1 %copy-start.3 = (bf16[512,32]{0,1:T(8,128)(2,1)S(1)}, bf16[512,32]{0,1:T(8,128)(2,1)}, u32[]{:S(2)}) copy-start(bf16[512,32]{0,1:T(8,128)(2,1)} %param.7) | copy-start | bytes 98308
  118.1 11.2 %collective-permute-start.1 = (bf16[256,256]{1,0:T(8,128)(2,1)}, bf16[256,256]{1,0:T(8,128)(2,1)S(1)}, u32[]{:S(2)}, u32[]{:S(2)}) collective-permute-start(bf16[256,256]{1,0:T(8,128)(2,1)} %get-tuple-element.48), channel_id=1, source_target_pairs={{0,4},{2,6},{4,0},{6,2},{1,5},{3,7},{5,1},{7,3},{8,12},{10,14},{12... | collective-permute-start | bytes 393224 | tf_op jit(solution)/shard_map/ppermute | solution.py:61
  122.7 8.4 %collective-permute-start.2 = (bf16[256,256]{1,0:T(8,128)(2,1)}, bf16[256,256]{1,0:T(8,128)(2,1)S(1)}, u32[]{:S(2)}, u32[]{:S(2)}) collective-permute-start(bf16[256,256]{1,0:T(8,128)(2,1)} %get-tuple-element.49), channel_id=1, source_target_pairs={{0,6},{2,4},{4,2},{6,0},{1,7},{3,5},{5,3},{7,1},{8,14},{10,12},{12... | collective-permute-start | bytes 393224 | tf_op jit(solution)/shard_map/ppermute | solution.py:61
  125.9 9.4 %collective-permute-start.3 = (bf16[256,256]{1,0:T(8,128)(2,1)}, bf16[256,256]{1,0:T(8,128)(2,1)S(1)}, u32[]{:S(2)}, u32[]{:S(2)}) collective-permute-start(bf16[256,256]{1,0:T(8,128)(2,1)} %get-tuple-element.50), channel_id=1, source_target_pairs={{0,2},{2,0},{4,6},{6,4},{1,3},{3,1},{5,7},{7,5},{8,10},{10,8},{12,... | collective-permute-start | bytes 393224 | tf_op jit(solution)/shard_map/ppermute | solution.py:61
  129.3 6.0 %copy-start.4 = (bf16[256,256]{1,0:T(8,128)(2,1)}, bf16[256,256]{1,0:T(8,128)(2,1)S(1)}, u32[]{:S(2)}) copy-start(bf16[256,256]{1,0:T(8,128)(2,1)S(1)} %collective-permute-done.1.one) | copy-start | bytes 393220
  131.1 4.2 %copy-start.5 = (bf16[256,256]{1,0:T(8,128)(2,1)}, bf16[256,256]{1,0:T(8,128)(2,1)S(1)}, u32[]{:S(2)}) copy-start(bf16[256,256]{1,0:T(8,128)(2,1)S(1)} %collective-permute-done.2.two) | copy-start | bytes 393220
  135.3 0.7 copy-start.6
  135.9 21.7 %copy-start.1 = (s32[5]{0:T(128)S(1)}, s32[5]{0:T(128)}, u32[]{:S(2)}) copy-start(s32[5]{0:T(128)} %stack.19.place) | copy-start | bytes 64
  138.9 5.9 %collective-permute-start.4 = (bf16[32,512]{1,0:T(8,128)(2,1)S(1)}, bf16[32,512]{1,0:T(8,128)(2,1)S(1)}, u32[]{:S(2)}, u32[]{:S(2)}) collective-permute-start(bf16[32,512]{1,0:T(8,128)(2,1)S(1)} %fusion), channel_id=1, source_target_pairs={{0,1},{1,0},{2,3},{3,2},{4,5},{5,4},{6,7},{7,6},{8,9},{9,8},{10,11... | collective-permute-start | bytes 98312 | tf_op jit(solution)/shard_map/ppermute | solution.py:61
  141.4 17.5 %all-to-all-start.6 = ((bf16[4,32,512]{2,1,0:T(8,128)(2,1)}), bf16[4,32,512]{2,1,0:T(8,128)(2,1)S(1)}, u32[]{:S(2)}, u32[]{:S(2)}) async-start(bf16[4,32,512]{2,1,0:T(8,128)(2,1)} %shard_map.110), calls=%async_computation.6 | async-start | bytes 262144 | tf_op jit(solution)/shard_map/all_to_all | solution.py:56
  144.8 9.2 %collective-permute-start.7 = (bf16[32,512]{1,0:T(8,128)(2,1)S(1)}, bf16[32,512]{1,0:T(8,128)(2,1)S(1)}, u32[]{:S(2)}, u32[]{:S(2)}) collective-permute-start(bf16[32,512]{1,0:T(8,128)(2,1)S(1)} %add_convert_fusion.own), channel_id=1, source_target_pairs={{0,2},{2,0},{4,6},{6,4},{1,3},{3,1},{5,7},{7,5},{8,10},{10,8},{12,... | collective-permute-start | bytes 98312 | tf_op jit(solution)/shard_map/ppermute | solution.py:61
  147.0 8.9 %collective-permute-start.6 = (bf16[32,512]{1,0:T(8,128)(2,1)S(1)}, bf16[32,512]{1,0:T(8,128)(2,1)S(1)}, u32[]{:S(2)}, u32[]{:S(2)}) collective-permute-start(bf16[32,512]{1,0:T(8,128)(2,1)S(1)} %add_convert_fusion.own), channel_id=1, source_target_pairs={{0,6},{2,4},{4,2},{6,0},{1,7},{3,5},{5,3},{7,1},{8,14},{10,12},{12... | collective-permute-start | bytes 98312 | tf_op jit(solution)/shard_map/ppermute | solution.py:61
  150.1 7.5 %collective-permute-start.5 = (bf16[32,512]{1,0:T(8,128)(2,1)S(1)}, bf16[32,512]{1,0:T(8,128)(2,1)S(1)}, u32[]{:S(2)}, u32[]{:S(2)}) collective-permute-start(bf16[32,512]{1,0:T(8,128)(2,1)S(1)} %add_convert_fusion.own), channel_id=1, source_target_pairs={{0,4},{2,6},{4,0},{6,2},{1,5},{3,7},{5,1},{7,3},{8,12},{10,14},{12... | collective-permute-start | bytes 98312 | tf_op jit(solution)/shard_map/ppermute | solution.py:61

commit v6 on v5

--- a/solution.py
+++ b/solution.py
@@ -313,7 +313,7 @@
         limit=60,
     )
 
-    query_part = exchange(sum_copies(query_part, far, F32), "w")
+    query_part = exchange(sum_copies(query_part, far, BF16), "w")
     query_part, keys, keys_t, values, tokens_t, other_t, own_t = lax.optimization_barrier(
         (query_part, keys, keys_t, values, tokens_t, other_t, own_t)
     )
@@ -362,8 +362,8 @@
         limit=60,
     )
     parts = [partner(away[k - 1], "z", k) for k in (2, 3, 1)]
+    arrived, here, *parts = lax.optimization_barrier((arrived, here, *parts))
     (token_grad,) = local(token_sum_kernel, [shape((rows, block), BF16)], [here, *parts], limit=60)
-    arrived, token_grad = lax.optimization_barrier((arrived, token_grad))
 
     (sent,) = local(
         near_sum_kernel,

time: 162 us -> 159 us (0.981)
  waiting for transfers between devices: 19.9 us -> 17.7 us
    ppermute x8, waiting for transfers between devices: 12.6 us -> 10.7 us  [partner(): return lax.ppermute(value, axis, [(i, i ^ flip) for i in range(size)])]
  transfers between devices with their start and end apart: 11 -> 11, of which waited for: 7 -> 5; matrix products, arithmetic and copies ran while one was open for 1% -> 1% of each run, Pallas kernels for 6% -> 6%
where the time goes in v6:
time: 159 us; the launch traced here: 158 us
  blocking collectives  59.1 us (37%)
  starting transfers between devices  55 us (35%)
  Pallas kernels  23 us (14%)
  waiting for transfers between devices  17.7 us (11%)
    all_to_all x4, blocking collectives, exchange(): return lax.all_to_all(blocks, axes, split_axis=0, concat_axis=0, tiled=True)  59.1 us
    ppermute x8, starting transfers between devices, partner(): return lax.ppermute(value, axis, [(i, i ^ flip) for i in range(size)])  31.7 us
    all_to_all x3, starting transfers between devices, exchange(): return lax.all_to_all(blocks, axes, split_axis=0, concat_axis=0, tiled=True)  23.2 us
    pallas_call x12, Pallas kernels, local(): pl.pallas_call(body, out_shape=outs, grid=(grid,), in_specs=[specs.get(i)...  23 us
    ppermute x8, waiting for transfers between devices, partner(): return lax.ppermute(value, axis, [(i, i ^ flip) for i in range(size)])  10.7 us
    all_to_all x3, waiting for transfers between devices, exchange(): return lax.all_to_all(blocks, axes, split_axis=0, concat_axis=0, tiled=True)  7.02 us
  transfers between devices with their start and end apart: 11, of which 5 were waited for; matrix products, arithmetic and copies ran while one was open for 1% of the time, Pallas kernels for 6%

profile of v6, /device:TPU:1, one launch (start us, length us, event | category | flops | bytes accessed | tf_op | source)
XLA Modules:
  0.0 157.9 jit_solution(6061458080465332214)
XLA Ops:
  0.6 1.8 %shard_map.101 = f32[16,16,512]{2,1,0:T(8,128)} custom-call(bf16[32,256]{1,0:T(8,128)(2,1)} %w_query.1, bf16[32,512]{1,0:T(8,128)(2,1)} %bitcast.20), custom_call_target="tpu_custom_call" | custom-call | flops 8388608 | bytes 573440 | tf_op jit(solution)/shard_map/pallas_call | solution.py:43
  2.5 16.7 %all_to_all.35.blocks = f32[16,16,512]{2,1,0:T(8,128)S(1)} all-to-all(f32[16,16,512]{2,1,0:T(8,128)} %shard_map.101), channel_id=1, replica_groups=mesh['x'=4,'w'=4,'y'=4,'z'=4,'c'=2] {'x','y'}, dimensions={0} | all-to-all | bytes 1048576 | tf_op jit(solution)/shard_map/all_to_all | solution.py:56
  19.1 0.7 shard_map.102
  19.8 16.0 %all-to-all-start.1 = ((bf16[4,16,512]{2,1,0:T(8,128)(2,1)}), bf16[4,16,512]{2,1,0:T(8,128)(2,1)S(1)}, u32[]{:S(2)}, u32[]{:S(2)}) async-start(bf16[4,16,512]{2,1,0:T(8,128)(2,1)} %shard_map.102), calls=%async_computation.1 | async-start | bytes 131072 | tf_op jit(solution)/shard_map/all_to_all | solution.py:56
  35.8 0.6 stack.19.place
  36.4 4.3 %shard_map.103 = (bf16[256,256]{1,0:T(8,128)(2,1)}, bf16[256,256]{1,0:T(8,128)(2,1)}, bf16[256,256]{1,0:T(8,128)(2,1)}, bf16[16,128,256]{2,1,0:T(8,128)(2,1)}, b...) custom-call(s32[5]{0:T(128)} %stack.19.place, bf16[256,2048]{1,0:T(8,128)(2,1)} %tokens.1, ...), custom_call_target="tpu_custom_call" | custom-call | flops 536870912 | bytes 6684692 | tf_op jit(solution)/shard_map/pallas_call | solution.py:43
  40.7 0.0 copy-start
  40.7 7.0 %all-to-all-done.1.blocks = bf16[4,16,512]{2,1,0:T(8,128)(2,1)S(1)} async-done(((bf16[4,16,512]{2,1,0:T(8,128)(2,1)}), bf16[4,16,512]{2,1,0:T(8,128)(2,1)S(1)}, u32[]{:S(2)}, u32[]{:S(2)}) %all-to-all-start.1) | async-done | bytes 65568 | tf_op jit(solution)/shard_map/all_to_all | solution.py:56
  47.7 10.7 %all_to_all.36 = bf16[16,16,512]{2,1,0:T(8,128)(2,1)} all-to-all(bf16[16,16,512]{2,1,0:T(8,128)(2,1)S(1)} %shard_map.104), channel_id=1, replica_groups=mesh['x'=4,'w'=4,'y'=4,'z'=4,'c'=2] {'x','y'}, dimensions={0} | all-to-all | bytes 524288 | tf_op jit(solution)/shard_map/all_to_all | solution.py:56
  58.4 3.3 %shard_map.105 = bf16[16,48,512]{2,1,0:T(8,128)(2,1)} custom-call(s32[5]{0:T(128)} %stack.19.place, bf16[256,512]{1,0:T(8,128)(2,1)} %bitcast.18, bf16[256,256]{1,0:T(8,128)(2,1)} %get-tuple-element.41.keys, bf16[256,256]{1,0:T(8,128)(2,1)} %get-tuple-element.42.keys_t, bf16[256,256]{1,0:T(8,128)(2,1)} %get-tuple-element.43.values, bf16[512,256]{1,0:T(8,128)(2,1)} %cot.3), custom_call_target="tpu_custom_call" | custom-call | flops 402653184 | bytes 1703956 | tf_op jit(solution)/shard_map/pallas_call | solution.py:43
  61.8 13.7 %all_to_all.37.blocks = bf16[16,48,512]{2,1,0:T(8,128)(2,1)S(1)} all-to-all(bf16[16,48,512]{2,1,0:T(8,128)(2,1)} %shard_map.105), channel_id=1, replica_groups=mesh['x'=4,'w'=4,'y'=4,'z'=4,'c'=2] {'x','y'}, dimensions={0} | all-to-all | bytes 1572864 | tf_op jit(solution)/shard_map/all_to_all | solution.py:56
  75.5 0.0 copy-done
  75.5 0.8 shard_map.106
  76.3 18.0 %all_to_all.38.sums4 = bf16[4,48,512]{2,1,0:T(8,128)(2,1)} all-to-all(bf16[4,48,512]{2,1,0:T(8,128)(2,1)S(1)} %shard_map.106), channel_id=1, replica_groups=mesh['x'=4,'w'=4,'y'=4,'z'=4,'c'=2] {'w'}, dimensions={0} | all-to-all | bytes 393216 | tf_op jit(solution)/shard_map/all_to_all | solution.py:56
  94.3 4.9 %shard_map.107 = (bf16[16,144,512]{2,1,0:T(8,128)(2,1)}, bf16[256,512]{1,0:T(8,128)(2,1)}, bf16[4,256,256]{2,1,0:T(8,128)(2,1)}) custom-call(s32[5]{0:T(128)} %stack.19.place, bf16[4,48,512]{2,1,0:T(8,128)(2,1)} %all_to_all.38.sums4, bf16[256,512]{1,0:T(8,128)(2,1)} %bitcast.19, bf16[256,256]{1,0:T(8,128)(2,1)} %get-tuple-element.41.keys, ...), custom_call_target="tpu_custom_call" | custom-call | flops 1073741824 | bytes 6225940 | tf_op jit(solution)/shard_map/pallas_call | solution.py:43
  99.2 0.0 copy-start.8
  99.2 3.9 %all-to-all-start.5 = ((bf16[16,144,512]{2,1,0:T(8,128)(2,1)}), bf16[16,144,512]{2,1,0:T(8,128)(2,1)S(1)}, u32[]{:S(2)}, u32[]{:S(2)}) async-start(bf16[16,144,512]{2,1,0:T(8,128)(2,1)} %get-tuple-element.46), calls=%async_computation.5 | async-start | bytes 4718592 | tf_op jit(solution)/shard_map/all_to_all | solution.py:56
  103.1 0.0 copy-done.8
  103.1 8.8 %collective-permute-start = (bf16[4,256,256]{2,1,0:T(8,128)(2,1)S(1)}, bf16[4,256,256]{2,1,0:T(8,128)(2,1)S(1)}, u32[]{:S(2)}, u32[]{:S(2)}) collective-permute-start(bf16[4,256,256]{2,1,0:T(8,128)(2,1)S(1)} %copy-done.8), channel_id=1, source_target_pairs={{0,1},{1,0},{2,3},{3,2},{4,5},{5,4},{6,7},{7,6},{8,9},{9,8},{10,11... | collective-permute-start | bytes 1572872 | tf_op jit(solution)/shard_map/ppermute | solution.py:61
  111.9 1.5 collective-permute-done.other
  113.4 0.0 copy-start.2
  113.4 0.8 copy-done.2
  114.2 0.0 copy-start.7
  114.2 0.0 copy-start.3
  114.2 2.6 %shard_map.108 = (f32[256,256]{1,0:T(8,128)}, bf16[256,256]{1,0:T(8,128)(2,1)}, bf16[256,256]{1,0:T(8,128)(2,1)}, bf16[256,256]{1,0:T(8,128)(2,1)}) custom-call(bf16[256,512]{1,0:T(8,128)(2,1)} %get-tuple-element.47.both, bf16[4,512,256]{2,1,0:T(8,128)(2,1)} %get-tuple-element.48.weights, bf16[4,256,256]{2,1,0:T(8,128)(2,1)} %copy-done.2), custom_call_target="tpu_custom_call" | custom-call | flops 268435456 | bytes 2490368 | tf_op jit(solution)/shard_map/pallas_call | solution.py:43
  116.8 3.7 %collective-permute-start.1 = (bf16[256,256]{1,0:T(8,128)(2,1)}, bf16[256,256]{1,0:T(8,128)(2,1)S(1)}, u32[]{:S(2)}, u32[]{:S(2)}) collective-permute-start(bf16[256,256]{1,0:T(8,128)(2,1)} %get-tuple-element.51), channel_id=1, source_target_pairs={{0,4},{2,6},{4,0},{6,2},{1,5},{3,7},{5,1},{7,3},{8,12},{10,14},{12... | collective-permute-start | bytes 393224 | tf_op jit(solution)/shard_map/ppermute | solution.py:61
  120.6 3.5 %collective-permute-start.2 = (bf16[256,256]{1,0:T(8,128)(2,1)}, bf16[256,256]{1,0:T(8,128)(2,1)S(1)}, u32[]{:S(2)}, u32[]{:S(2)}) collective-permute-start(bf16[256,256]{1,0:T(8,128)(2,1)} %get-tuple-element.52), channel_id=1, source_target_pairs={{0,6},{2,4},{4,2},{6,0},{1,7},{3,5},{5,3},{7,1},{8,14},{10,12},{12... | collective-permute-start | bytes 393224 | tf_op jit(solution)/shard_map/ppermute | solution.py:61
  124.1 1.9 %collective-permute-start.3 = (bf16[256,256]{1,0:T(8,128)(2,1)}, bf16[256,256]{1,0:T(8,128)(2,1)S(1)}, u32[]{:S(2)}, u32[]{:S(2)}) collective-permute-start(bf16[256,256]{1,0:T(8,128)(2,1)} %get-tuple-element.53), channel_id=1, source_target_pairs={{0,2},{2,0},{4,6},{6,4},{1,3},{3,1},{5,7},{7,5},{8,10},{10,8},{12,... | collective-permute-start | bytes 393224 | tf_op jit(solution)/shard_map/ppermute | solution.py:61
  126.0 3.4 %collective-permute-done.1.one = bf16[256,256]{1,0:T(8,128)(2,1)S(1)} collective-permute-done((bf16[256,256]{1,0:T(8,128)(2,1)}, bf16[256,256]{1,0:T(8,128)(2,1)S(1)}, u32[]{:S(2)}, u32[]{:S(2)}) %collective-permute-start.1) | collective-permute-done | bytes 131104 | tf_op jit(solution)/shard_map/ppermute | solution.py:61
  129.3 0.0 copy-start.4
  129.3 0.0 collective-permute-done.2.two
  129.3 0.0 copy-start.5
  129.3 4.2 %collective-permute-done.3.three = bf16[256,256]{1,0:T(8,128)(2,1)S(1)} collective-permute-done((bf16[256,256]{1,0:T(8,128)(2,1)}, bf16[256,256]{1,0:T(8,128)(2,1)S(1)}, u32[]{:S(2)}, u32[]{:S(2)}) %collective-permute-start.3) | collective-permute-done | bytes 131104 | tf_op jit(solution)/shard_map/ppermute | solution.py:61
  133.5 0.0 copy-start.6
  133.5 0.0 all-to-all-done.5.arrived
  133.5 0.0 copy-start.1
  133.5 0.9 shard_map.110
  134.5 0.0 copy-done.7
  134.5 0.1 fusion
  134.6 3.8 %collective-permute-start.4 = (bf16[32,512]{1,0:T(8,128)(2,1)S(1)}, bf16[32,512]{1,0:T(8,128)(2,1)S(1)}, u32[]{:S(2)}, u32[]{:S(2)}) collective-permute-start(bf16[32,512]{1,0:T(8,128)(2,1)S(1)} %fusion), channel_id=1, source_target_pairs={{0,1},{1,0},{2,3},{3,2},{4,5},{5,4},{6,7},{7,6},{8,9},{9,8},{10,11... | collective-permute-start | bytes 98312 | tf_op jit(solution)/shard_map/ppermute | solution.py:61
  138.4 3.3 %all-to-all-start.6 = ((bf16[4,32,512]{2,1,0:T(8,128)(2,1)}), bf16[4,32,512]{2,1,0:T(8,128)(2,1)S(1)}, u32[]{:S(2)}, u32[]{:S(2)}) async-start(bf16[4,32,512]{2,1,0:T(8,128)(2,1)} %shard_map.110), calls=%async_computation.6 | async-start | bytes 262144 | tf_op jit(solution)/shard_map/all_to_all | solution.py:56
  141.7 0.0 collective-permute-done.4
  141.8 4.5 %collective-permute-start.7 = (bf16[32,512]{1,0:T(8,128)(2,1)S(1)}, bf16[32,512]{1,0:T(8,128)(2,1)S(1)}, u32[]{:S(2)}, u32[]{:S(2)}) collective-permute-start(bf16[32,512]{1,0:T(8,128)(2,1)S(1)} %add_convert_fusion.own), channel_id=1, source_target_pairs={{0,2},{2,0},{4,6},{6,4},{1,3},{3,1},{5,7},{7,5},{8,10},{10,8},{12,... | collective-permute-start | bytes 98312 | tf_op jit(solution)/shard_map/ppermute | solution.py:61
  146.3 3.6 %collective-permute-start.6 = (bf16[32,512]{1,0:T(8,128)(2,1)S(1)}, bf16[32,512]{1,0:T(8,128)(2,1)S(1)}, u32[]{:S(2)}, u32[]{:S(2)}) collective-permute-start(bf16[32,512]{1,0:T(8,128)(2,1)S(1)} %add_convert_fusion.own), channel_id=1, source_target_pairs={{0,6},{2,4},{4,2},{6,0},{1,7},{3,5},{5,3},{7,1},{8,14},{10,12},{12... | collective-permute-start | bytes 98312 | tf_op jit(solution)/shard_map/ppermute | solution.py:61
  149.9 1.9 %collective-permute-start.5 = (bf16[32,512]{1,0:T(8,128)(2,1)S(1)}, bf16[32,512]{1,0:T(8,128)(2,1)S(1)}, u32[]{:S(2)}, u32[]{:S(2)}) collective-permute-start(bf16[32,512]{1,0:T(8,128)(2,1)S(1)} %add_convert_fusion.own), channel_id=1, source_target_pairs={{0,4},{2,6},{4,0},{6,2},{1,5},{3,7},{5,1},{7,3},{8,12},{10,14},{12... | collective-permute-start | bytes 98312 | tf_op jit(solution)/shard_map/ppermute | solution.py:61
  151.8 0.0 copy-done.3
  151.8 0.8 convolution_bitcast_fusion
  152.6 0.0 copy-done.4
  152.6 0.0 copy-done.5
  152.6 0.0 copy-done.6
  152.6 1.8 %shard_map.109 = bf16[256,256]{1,0:T(8,128)(2,1)} custom-call(f32[256,256]{1,0:T(8,128)} %get-tuple-element.54.here, bf16[256,256]{1,0:T(8,128)(2,1)} %copy-done.4, bf16[256,256]{1,0:T(8,128)(2,1)} %copy-done.5, bf16[256,256]{1,0:T(8,128)(2,1)} %copy-done.6), custom_call_target="tpu_custom_call" | custom-call | bytes 786432 | tf_op jit(solution)/shard_map/pallas_call | solution.py:43
  154.5 0.0 collective-permute-done.7.one
  154.5 0.0 collective-permute-done.6.three
  154.5 1.6 %collective-permute-done.5.two = bf16[32,512]{1,0:T(8,128)(2,1)S(1)} collective-permute-done((bf16[32,512]{1,0:T(8,128)(2,1)S(1)}, bf16[32,512]{1,0:T(8,128)(2,1)S(1)}, u32[]{:S(2)}, u32[]{:S(2)}) %collective-permute-start.5) | collective-permute-done | bytes 32800 | tf_op jit(solution)/shard_map/ppermute | solution.py:61
  156.1 0.0 copy-done.1
  156.1 1.2 shard_map.111
  157.3 0.0 all-to-all-done.6.arrived
  157.3 0.6 shard_map.112
  (3 shorter events, 0.1 us)
Async XLA Ops:
  19.8 27.9 %all-to-all-start.1 = ((bf16[4,16,512]{2,1,0:T(8,128)(2,1)}), bf16[4,16,512]{2,1,0:T(8,128)(2,1)S(1)}, u32[]{:S(2)}, u32[]{:S(2)}) async-start(bf16[4,16,512]{2,1,0:T(8,128)(2,1)} %shard_map.102), calls=%async_computation.1 | async-start | bytes 131072 | tf_op jit(solution)/shard_map/all_to_all | solution.py:56
  40.7 34.8 %copy-start = (s32[5]{0:T(128)S(1)}, s32[5]{0:T(128)}, u32[]{:S(2)}) copy-start(s32[5]{0:T(128)} %stack.19.place) | copy-start | bytes 64
  99.2 3.9 %copy-start.8 = (bf16[4,256,256]{2,1,0:T(8,128)(2,1)S(1)}, bf16[4,256,256]{2,1,0:T(8,128)(2,1)}, u32[]{:S(2)}) copy-start(bf16[4,256,256]{2,1,0:T(8,128)(2,1)} %get-tuple-element.49) | copy-start | bytes 1572868
  99.2 34.3 %all-to-all-start.5 = ((bf16[16,144,512]{2,1,0:T(8,128)(2,1)}), bf16[16,144,512]{2,1,0:T(8,128)(2,1)S(1)}, u32[]{:S(2)}, u32[]{:S(2)}) async-start(bf16[16,144,512]{2,1,0:T(8,128)(2,1)} %get-tuple-element.46), calls=%async_computation.5 | async-start | bytes 4718592 | tf_op jit(solution)/shard_map/all_to_all | solution.py:56
  103.1 10.4 %collective-permute-start = (bf16[4,256,256]{2,1,0:T(8,128)(2,1)S(1)}, bf16[4,256,256]{2,1,0:T(8,128)(2,1)S(1)}, u32[]{:S(2)}, u32[]{:S(2)}) collective-permute-start(bf16[4,256,256]{2,1,0:T(8,128)(2,1)S(1)} %copy-done.8), channel_id=1, source_target_pairs={{0,1},{1,0},{2,3},{3,2},{4,5},{5,4},{6,7},{7,6},{8,9},{9,8},{10,11... | collective-permute-start | bytes 1572872 | tf_op jit(solution)/shard_map/ppermute | solution.py:61
  113.4 0.8 copy-start.2
  114.2 20.3 %copy-start.7 = (bf16[32,256]{1,0:T(8,128)(2,1)S(1)}, bf16[32,256]{1,0:T(8,128)(2,1)}, u32[]{:S(2)}) copy-start(bf16[32,256]{1,0:T(8,128)(2,1)} %w_query.1) | copy-start | bytes 49156
  114.2 37.6 %copy-start.3 = (bf16[512,32]{0,1:T(8,128)(2,1)S(1)}, bf16[512,32]{0,1:T(8,128)(2,1)}, u32[]{:S(2)}) copy-start(bf16[512,32]{0,1:T(8,128)(2,1)} %param.7) | copy-start | bytes 98308
  116.8 12.5 %collective-permute-start.1 = (bf16[256,256]{1,0:T(8,128)(2,1)}, bf16[256,256]{1,0:T(8,128)(2,1)S(1)}, u32[]{:S(2)}, u32[]{:S(2)}) collective-permute-start(bf16[256,256]{1,0:T(8,128)(2,1)} %get-tuple-element.51), channel_id=1, source_target_pairs={{0,4},{2,6},{4,0},{6,2},{1,5},{3,7},{5,1},{7,3},{8,12},{10,14},{12... | collective-permute-start | bytes 393224 | tf_op jit(solution)/shard_map/ppermute | solution.py:61
  120.6 8.8 %collective-permute-start.2 = (bf16[256,256]{1,0:T(8,128)(2,1)}, bf16[256,256]{1,0:T(8,128)(2,1)S(1)}, u32[]{:S(2)}, u32[]{:S(2)}) collective-permute-start(bf16[256,256]{1,0:T(8,128)(2,1)} %get-tuple-element.52), channel_id=1, source_target_pairs={{0,6},{2,4},{4,2},{6,0},{1,7},{3,5},{5,3},{7,1},{8,14},{10,12},{12... | collective-permute-start | bytes 393224 | tf_op jit(solution)/shard_map/ppermute | solution.py:61
  124.1 9.5 %collective-permute-start.3 = (bf16[256,256]{1,0:T(8,128)(2,1)}, bf16[256,256]{1,0:T(8,128)(2,1)S(1)}, u32[]{:S(2)}, u32[]{:S(2)}) collective-permute-start(bf16[256,256]{1,0:T(8,128)(2,1)} %get-tuple-element.53), channel_id=1, source_target_pairs={{0,2},{2,0},{4,6},{6,4},{1,3},{3,1},{5,7},{7,5},{8,10},{10,8},{12,... | collective-permute-start | bytes 393224 | tf_op jit(solution)/shard_map/ppermute | solution.py:61
  129.3 23.3 %copy-start.4 = (bf16[256,256]{1,0:T(8,128)(2,1)}, bf16[256,256]{1,0:T(8,128)(2,1)S(1)}, u32[]{:S(2)}) copy-start(bf16[256,256]{1,0:T(8,128)(2,1)S(1)} %collective-permute-done.1.one) | copy-start | bytes 393220
  129.3 23.3 %copy-start.5 = (bf16[256,256]{1,0:T(8,128)(2,1)}, bf16[256,256]{1,0:T(8,128)(2,1)S(1)}, u32[]{:S(2)}) copy-start(bf16[256,256]{1,0:T(8,128)(2,1)S(1)} %collective-permute-done.2.two) | copy-start | bytes 393220
  133.5 19.1 %copy-start.6 = (bf16[256,256]{1,0:T(8,128)(2,1)}, bf16[256,256]{1,0:T(8,128)(2,1)S(1)}, u32[]{:S(2)}) copy-start(bf16[256,256]{1,0:T(8,128)(2,1)S(1)} %collective-permute-done.3.three) | copy-start | bytes 393220
  133.5 22.5 %copy-start.1 = (s32[5]{0:T(128)S(1)}, s32[5]{0:T(128)}, u32[]{:S(2)}) copy-start(s32[5]{0:T(128)} %stack.19.place) | copy-start | bytes 64
  134.6 7.1 %collective-permute-start.4 = (bf16[32,512]{1,0:T(8,128)(2,1)S(1)}, bf16[32,512]{1,0:T(8,128)(2,1)S(1)}, u32[]{:S(2)}, u32[]{:S(2)}) collective-permute-start(bf16[32,512]{1,0:T(8,128)(2,1)S(1)} %fusion), channel_id=1, source_target_pairs={{0,1},{1,0},{2,3},{3,2},{4,5},{5,4},{6,7},{7,6},{8,9},{9,8},{10,11... | collective-permute-start | bytes 98312 | tf_op jit(solution)/shard_map/ppermute | solution.py:61
  138.4 18.9 %all-to-all-start.6 = ((bf16[4,32,512]{2,1,0:T(8,128)(2,1)}), bf16[4,32,512]{2,1,0:T(8,128)(2,1)S(1)}, u32[]{:S(2)}, u32[]{:S(2)}) async-start(bf16[4,32,512]{2,1,0:T(8,128)(2,1)} %shard_map.110), calls=%async_computation.6 | async-start | bytes 262144 | tf_op jit(solution)/shard_map/all_to_all | solution.py:56
  141.8 12.7 %collective-permute-start.7 = (bf16[32,512]{1,0:T(8,128)(2,1)S(1)}, bf16[32,512]{1,0:T(8,128)(2,1)S(1)}, u32[]{:S(2)}, u32[]{:S(2)}) collective-permute-start(bf16[32,512]{1,0:T(8,128)(2,1)S(1)} %add_convert_fusion.own), channel_id=1, source_target_pairs={{0,2},{2,0},{4,6},{6,4},{1,3},{3,1},{5,7},{7,5},{8,10},{10,8},{12,... | collective-permute-start | bytes 98312 | tf_op jit(solution)/shard_map/ppermute | solution.py:61
  146.3 8.2 %collective-permute-start.6 = (bf16[32,512]{1,0:T(8,128)(2,1)S(1)}, bf16[32,512]{1,0:T(8,128)(2,1)S(1)}, u32[]{:S(2)}, u32[]{:S(2)}) collective-permute-start(bf16[32,512]{1,0:T(8,128)(2,1)S(1)} %add_convert_fusion.own), channel_id=1, source_target_pairs={{0,6},{2,4},{4,2},{6,0},{1,7},{3,5},{5,3},{7,1},{8,14},{10,12},{12... | collective-permute-start | bytes 98312 | tf_op jit(solution)/shard_map/ppermute | solution.py:61
  149.9 6.2 %collective-permute-start.5 = (bf16[32,512]{1,0:T(8,128)(2,1)S(1)}, bf16[32,512]{1,0:T(8,128)(2,1)S(1)}, u32[]{:S(2)}, u32[]{:S(2)}) collective-permute-start(bf16[32,512]{1,0:T(8,128)(2,1)S(1)} %add_convert_fusion.own), channel_id=1, source_target_pairs={{0,4},{2,6},{4,0},{6,2},{1,5},{3,7},{5,1},{7,3},{8,12},{10,14},{12... | collective-permute-start | bytes 98312 | tf_op jit(solution)/shard_map/ppermute | solution.py:61

commit v7 on v6

--- a/solution.py
+++ b/solution.py
@@ -262,11 +262,18 @@
     out[...] = ((terms[z] + terms[z ^ 1]) + terms[z ^ 2]) + terms[z ^ 3]
 
 
-def near_sum_kernel(arrived, out):
-    acc = summed(arrived)
-    share = out.shape[1]
-    for w in range(out.shape[0]):
+def near_sum_kernel(arrived, w_query, latents_t, out, latent, query_weight):
+    far, share, _ = out.shape
+    depth = far * share
+    n, held, lats = arrived.shape
+    acc = arrived[0, :depth, :].astype(F32)
+    for j in range(1, n):
+        acc = acc + arrived[j, :depth, :].astype(F32)
+    for w in range(far):
         out[w] = acc[w * share : (w + 1) * share].astype(BF16)
+    query_grad_t = arrived[:, depth:, :].reshape(n * (held - depth), lats)
+    latent[...] = dot(w_query[...], query_grad_t).astype(BF16)
+    query_weight[...] = dot_nt(latents_t[...], query_grad_t)
 
 
 def far_sum_kernel(arrived, key_weight, value_weight):
@@ -313,7 +320,7 @@
         limit=60,
     )
 
-    query_part = exchange(sum_copies(query_part, far, BF16), "w")
+    query_part = exchange(sum_copies(query_part, far, F32), "w")
     query_part, keys, keys_t, values, tokens_t, other_t, own_t = lax.optimization_barrier(
         (query_part, keys, keys_t, values, tokens_t, other_t, own_t)
     )
@@ -365,22 +372,19 @@
     arrived, here, *parts = lax.optimization_barrier((arrived, here, *parts))
     (token_grad,) = local(token_sum_kernel, [shape((rows, block), BF16)], [here, *parts], limit=60)
 
-    (sent,) = local(
+    sent, held, query_weight_grad = local(
         near_sum_kernel,
-        [shape((far, share, 2 * width), BF16)],
-        [arrived],
-        specs={0: pl.BlockSpec((near, depth // near, 2 * width), lambda i: (0, 0, 0))},
-    )
-    query_grad_t = arrived[:, depth // near :, :].reshape(width, lats)
-    sent, query_grad_t = lax.optimization_barrier((sent, query_grad_t))
+        [
+            shape((far, share, 2 * width), BF16),
+            shape((share, lats), BF16),
+            shape((share, width), F32),
+        ],
+        [arrived, w_query, latents.T],
+        4 * share * width * lats,
+    )
     key_weight_grad, value_weight_grad = local(
         far_sum_kernel, [shape((share, width), F32)] * 2, [exchange(sent, "w")]
     )
-    latent_grad_t = dot(w_query, query_grad_t)
-    query_weight_grad = lax.dot_general(
-        latents, query_grad_t, (((0,), (1,)), ((), ())), preferred_element_type=F32
-    )
-    held = latent_grad_t.astype(BF16)
     held = (held.astype(F32) + partner(held, "c", 1).astype(F32)).astype(BF16)
     (latent_grad_t,) = local(
         latent_sum_kernel,

time: 159 us -> 160 us (level)
  transfers between devices with their start and end apart: 11 -> 11, of which waited for: 5 -> 7; matrix products, arithmetic and copies ran while one was open for 1% -> 0% of each run, Pallas kernels for 6% -> 6%
where the time goes in v7:
time: 160 us; the launch traced here: 158 us
  blocking collectives  59.1 us (37%)
  starting transfers between devices  55.6 us (35%)
  Pallas kernels  23.2 us (14%)
  waiting for transfers between devices  17.9 us (11%)
    all_to_all x4, blocking collectives, exchange(): return lax.all_to_all(blocks, axes, split_axis=0, concat_axis=0, tiled=True)  59.1 us
    ppermute x8, starting transfers between devices, partner(): return lax.ppermute(value, axis, [(i, i ^ flip) for i in range(size)])  32.1 us
    all_to_all x3, starting transfers between devices, exchange(): return lax.all_to_all(blocks, axes, split_axis=0, concat_axis=0, tiled=True)  23.5 us
    pallas_call x12, Pallas kernels, local(): pl.pallas_call(body, out_shape=outs, grid=(grid,), in_specs=[specs.get(i)...  23.2 us
    ppermute x8, waiting for transfers between devices, partner(): return lax.ppermute(value, axis, [(i, i ^ flip) for i in range(size)])  10.6 us
    all_to_all x3, waiting for transfers between devices, exchange(): return lax.all_to_all(blocks, axes, split_axis=0, concat_axis=0, tiled=True)  7.28 us
  transfers between devices with their start and end apart: 11, of which 7 were waited for; matrix products, arithmetic and copies ran while one was open for 0% of the time, Pallas kernels for 6%

profile of v7, /device:TPU:1, one launch (start us, length us, event | category | flops | bytes accessed | tf_op | source)
XLA Modules:
  0.0 158.1 jit_solution(6044575923994088260)
XLA Ops:
  0.6 1.8 %shard_map.101 = f32[16,16,512]{2,1,0:T(8,128)} custom-call(bf16[32,256]{1,0:T(8,128)(2,1)} %w_query.3, bf16[32,512]{1,0:T(8,128)(2,1)} %bitcast.7), custom_call_target="tpu_custom_call" | custom-call | flops 8388608 | bytes 573440 | tf_op jit(solution)/shard_map/pallas_call | solution.py:43
  2.5 16.7 %all_to_all.35.blocks = f32[16,16,512]{2,1,0:T(8,128)S(1)} all-to-all(f32[16,16,512]{2,1,0:T(8,128)} %shard_map.101), channel_id=1, replica_groups=mesh['x'=4,'w'=4,'y'=4,'z'=4,'c'=2] {'x','y'}, dimensions={0} | all-to-all | bytes 1048576 | tf_op jit(solution)/shard_map/all_to_all | solution.py:56
  19.1 0.7 shard_map.102
  19.8 16.0 %all-to-all-start.1 = ((f32[4,16,512]{2,1,0:T(8,128)}), f32[4,16,512]{2,1,0:T(8,128)S(1)}, u32[]{:S(2)}, u32[]{:S(2)}) async-start(f32[4,16,512]{2,1,0:T(8,128)} %shard_map.102), calls=%async_computation.1 | async-start | bytes 262144 | tf_op jit(solution)/shard_map/all_to_all | solution.py:56
  35.8 0.7 stack.19.place
  36.5 4.3 %shard_map.103 = (bf16[256,256]{1,0:T(8,128)(2,1)}, bf16[256,256]{1,0:T(8,128)(2,1)}, bf16[256,256]{1,0:T(8,128)(2,1)}, bf16[16,128,256]{2,1,0:T(8,128)(2,1)}, b...) custom-call(s32[5]{0:T(128)} %stack.19.place, bf16[256,2048]{1,0:T(8,128)(2,1)} %tokens.1, ...), custom_call_target="tpu_custom_call" | custom-call | flops 536870912 | bytes 6684692 | tf_op jit(solution)/shard_map/pallas_call | solution.py:43
  40.8 0.0 copy-start.2
  40.8 7.3 %all-to-all-done.1.blocks = f32[4,16,512]{2,1,0:T(8,128)S(1)} async-done(((f32[4,16,512]{2,1,0:T(8,128)}), f32[4,16,512]{2,1,0:T(8,128)S(1)}, u32[]{:S(2)}, u32[]{:S(2)}) %all-to-all-start.1) | async-done | bytes 131104 | tf_op jit(solution)/shard_map/all_to_all | solution.py:56
  48.1 10.7 %all_to_all.36 = bf16[16,16,512]{2,1,0:T(8,128)(2,1)} all-to-all(bf16[16,16,512]{2,1,0:T(8,128)(2,1)S(1)} %shard_map.104), channel_id=1, replica_groups=mesh['x'=4,'w'=4,'y'=4,'z'=4,'c'=2] {'x','y'}, dimensions={0} | all-to-all | bytes 524288 | tf_op jit(solution)/shard_map/all_to_all | solution.py:56
  58.8 3.3 %shard_map.105 = bf16[16,48,512]{2,1,0:T(8,128)(2,1)} custom-call(s32[5]{0:T(128)} %stack.19.place, bf16[256,512]{1,0:T(8,128)(2,1)} %bitcast.9, bf16[256,256]{1,0:T(8,128)(2,1)} %get-tuple-element.42.keys, bf16[256,256]{1,0:T(8,128)(2,1)} %get-tuple-element.43.keys_t, bf16[256,256]{1,0:T(8,128)(2,1)} %get-tuple-element.44.values, bf16[512,256]{1,0:T(8,128)(2,1)} %cot.3), custom_call_target="tpu_custom_call" | custom-call | flops 402653184 | bytes 1703956 | tf_op jit(solution)/shard_map/pallas_call | solution.py:43
  62.1 13.7 %all_to_all.37.blocks = bf16[16,48,512]{2,1,0:T(8,128)(2,1)S(1)} all-to-all(bf16[16,48,512]{2,1,0:T(8,128)(2,1)} %shard_map.105), channel_id=1, replica_groups=mesh['x'=4,'w'=4,'y'=4,'z'=4,'c'=2] {'x','y'}, dimensions={0} | all-to-all | bytes 1572864 | tf_op jit(solution)/shard_map/all_to_all | solution.py:56
  75.8 0.0 copy-done.2
  75.9 0.8 shard_map.106
  76.7 18.0 %all_to_all.38.sums4 = bf16[4,48,512]{2,1,0:T(8,128)(2,1)} all-to-all(bf16[4,48,512]{2,1,0:T(8,128)(2,1)S(1)} %shard_map.106), channel_id=1, replica_groups=mesh['x'=4,'w'=4,'y'=4,'z'=4,'c'=2] {'w'}, dimensions={0} | all-to-all | bytes 393216 | tf_op jit(solution)/shard_map/all_to_all | solution.py:56
  94.7 4.8 %shard_map.107 = (bf16[16,144,512]{2,1,0:T(8,128)(2,1)}, bf16[256,512]{1,0:T(8,128)(2,1)}, bf16[4,256,256]{2,1,0:T(8,128)(2,1)}) custom-call(s32[5]{0:T(128)} %stack.19.place, bf16[4,48,512]{2,1,0:T(8,128)(2,1)} %all_to_all.38.sums4, bf16[256,512]{1,0:T(8,128)(2,1)} %bitcast.10, bf16[256,256]{1,0:T(8,128)(2,1)} %get-tuple-element.42.keys, ...), custom_call_target="tpu_custom_call" | custom-call | flops 1073741824 | bytes 6225940 | tf_op jit(solution)/shard_map/pallas_call | solution.py:43
  99.5 0.0 copy-start.8
  99.5 0.0 copy-start
  99.5 0.0 copy-start.1
  99.6 4.1 %all-to-all-start.5 = ((bf16[16,144,512]{2,1,0:T(8,128)(2,1)}), bf16[16,144,512]{2,1,0:T(8,128)(2,1)S(1)}, u32[]{:S(2)}, u32[]{:S(2)}) async-start(bf16[16,144,512]{2,1,0:T(8,128)(2,1)} %get-tuple-element.47), calls=%async_computation.5 | async-start | bytes 4718592 | tf_op jit(solution)/shard_map/all_to_all | solution.py:56
  103.7 0.0 copy-done.8
  103.7 9.5 %collective-permute-start = (bf16[4,256,256]{2,1,0:T(8,128)(2,1)S(1)}, bf16[4,256,256]{2,1,0:T(8,128)(2,1)S(1)}, u32[]{:S(2)}, u32[]{:S(2)}) collective-permute-start(bf16[4,256,256]{2,1,0:T(8,128)(2,1)S(1)} %copy-done.8), channel_id=1, source_target_pairs={{0,1},{1,0},{2,3},{3,2},{4,5},{5,4},{6,7},{7,6},{8,9},{9,8},{10,11... | collective-permute-start | bytes 1572872 | tf_op jit(solution)/shard_map/ppermute | solution.py:61
  113.2 1.5 collective-permute-done.other
  114.7 0.0 copy-start.4
  114.7 0.8 copy-done.4
  115.5 0.0 copy-start.3
  115.5 2.6 %shard_map.108 = (f32[256,256]{1,0:T(8,128)}, bf16[256,256]{1,0:T(8,128)(2,1)}, bf16[256,256]{1,0:T(8,128)(2,1)}, bf16[256,256]{1,0:T(8,128)(2,1)}) custom-call(bf16[256,512]{1,0:T(8,128)(2,1)} %get-tuple-element.48.both, bf16[4,512,256]{2,1,0:T(8,128)(2,1)} %get-tuple-element.49.weights, bf16[4,256,256]{2,1,0:T(8,128)(2,1)} %copy-done.4), custom_call_target="tpu_custom_call" | custom-call | flops 268435456 | bytes 2490368 | tf_op jit(solution)/shard_map/pallas_call | solution.py:43
  118.1 4.5 %collective-permute-start.1 = (bf16[256,256]{1,0:T(8,128)(2,1)}, bf16[256,256]{1,0:T(8,128)(2,1)S(1)}, u32[]{:S(2)}, u32[]{:S(2)}) collective-permute-start(bf16[256,256]{1,0:T(8,128)(2,1)} %get-tuple-element.52), channel_id=1, source_target_pairs={{0,4},{2,6},{4,0},{6,2},{1,5},{3,7},{5,1},{7,3},{8,12},{10,14},{12... | collective-permute-start | bytes 393224 | tf_op jit(solution)/shard_map/ppermute | solution.py:61
  122.6 3.2 %collective-permute-start.2 = (bf16[256,256]{1,0:T(8,128)(2,1)}, bf16[256,256]{1,0:T(8,128)(2,1)S(1)}, u32[]{:S(2)}, u32[]{:S(2)}) collective-permute-start(bf16[256,256]{1,0:T(8,128)(2,1)} %get-tuple-element.53), channel_id=1, source_target_pairs={{0,6},{2,4},{4,2},{6,0},{1,7},{3,5},{5,3},{7,1},{8,14},{10,12},{12... | collective-permute-start | bytes 393224 | tf_op jit(solution)/shard_map/ppermute | solution.py:61
  125.8 1.9 %collective-permute-start.3 = (bf16[256,256]{1,0:T(8,128)(2,1)}, bf16[256,256]{1,0:T(8,128)(2,1)S(1)}, u32[]{:S(2)}, u32[]{:S(2)}) collective-permute-start(bf16[256,256]{1,0:T(8,128)(2,1)} %get-tuple-element.54), channel_id=1, source_target_pairs={{0,2},{2,0},{4,6},{6,4},{1,3},{3,1},{5,7},{7,5},{8,10},{10,8},{12,... | collective-permute-start | bytes 393224 | tf_op jit(solution)/shard_map/ppermute | solution.py:61
  127.8 1.5 collective-permute-done.1.one
  129.2 0.0 copy-start.5
  129.2 1.8 %collective-permute-done.2.two = bf16[256,256]{1,0:T(8,128)(2,1)S(1)} collective-permute-done((bf16[256,256]{1,0:T(8,128)(2,1)}, bf16[256,256]{1,0:T(8,128)(2,1)S(1)}, u32[]{:S(2)}, u32[]{:S(2)}) %collective-permute-start.2) | collective-permute-done | bytes 131104 | tf_op jit(solution)/shard_map/ppermute | solution.py:61
  131.0 0.0 copy-start.6
  131.0 4.2 %collective-permute-done.3.three = bf16[256,256]{1,0:T(8,128)(2,1)S(1)} collective-permute-done((bf16[256,256]{1,0:T(8,128)(2,1)}, bf16[256,256]{1,0:T(8,128)(2,1)S(1)}, u32[]{:S(2)}, u32[]{:S(2)}) %collective-permute-start.3) | collective-permute-done | bytes 131104 | tf_op jit(solution)/shard_map/ppermute | solution.py:61
  135.2 0.0 copy-start.7
  135.2 0.0 all-to-all-done.5.arrived
  135.2 0.0 copy-done
  135.2 0.0 copy-done.1
  135.2 1.2 shard_map.110
  136.4 3.3 %all-to-all-start.6 = ((bf16[4,32,512]{2,1,0:T(8,128)(2,1)}), bf16[4,32,512]{2,1,0:T(8,128)(2,1)S(1)}, u32[]{:S(2)}, u32[]{:S(2)}) async-start(bf16[4,32,512]{2,1,0:T(8,128)(2,1)} %get-tuple-element.62), calls=%async_computation.6 | async-start | bytes 262144 | tf_op jit(solution)/shard_map/all_to_all | solution.py:56
  139.7 4.6 %collective-permute-start.4 = (bf16[32,512]{1,0:T(8,128)(2,1)S(1)}, bf16[32,512]{1,0:T(8,128)(2,1)S(1)}, u32[]{:S(2)}, u32[]{:S(2)}) collective-permute-start(bf16[32,512]{1,0:T(8,128)(2,1)S(1)} %get-tuple-element.60), channel_id=1, source_target_pairs={{0,1},{1,0},{2,3},{3,2},{4,5},{5,4},{6,7},{7,6},{8,9},{9,8},{10,11... | collective-permute-start | bytes 98312 | tf_op jit(solution)/shard_map/ppermute | solution.py:61
  144.3 0.8 collective-permute-done.4
  145.1 1.9 %collective-permute-start.7 = (bf16[32,512]{1,0:T(8,128)(2,1)S(1)}, bf16[32,512]{1,0:T(8,128)(2,1)S(1)}, u32[]{:S(2)}, u32[]{:S(2)}) collective-permute-start(bf16[32,512]{1,0:T(8,128)(2,1)S(1)} %add_convert_fusion.own), channel_id=1, source_target_pairs={{0,2},{2,0},{4,6},{6,4},{1,3},{3,1},{5,7},{7,5},{8,10},{10,8},{12,... | collective-permute-start | bytes 98312 | tf_op jit(solution)/shard_map/ppermute | solution.py:61
  147.1 3.6 %collective-permute-start.6 = (bf16[32,512]{1,0:T(8,128)(2,1)S(1)}, bf16[32,512]{1,0:T(8,128)(2,1)S(1)}, u32[]{:S(2)}, u32[]{:S(2)}) collective-permute-start(bf16[32,512]{1,0:T(8,128)(2,1)S(1)} %add_convert_fusion.own), channel_id=1, source_target_pairs={{0,6},{2,4},{4,2},{6,0},{1,7},{3,5},{5,3},{7,1},{8,14},{10,12},{12... | collective-permute-start | bytes 98312 | tf_op jit(solution)/shard_map/ppermute | solution.py:61
  150.7 2.9 %collective-permute-start.5 = (bf16[32,512]{1,0:T(8,128)(2,1)S(1)}, bf16[32,512]{1,0:T(8,128)(2,1)S(1)}, u32[]{:S(2)}, u32[]{:S(2)}) collective-permute-start(bf16[32,512]{1,0:T(8,128)(2,1)S(1)} %add_convert_fusion.own), channel_id=1, source_target_pairs={{0,4},{2,6},{4,0},{6,2},{1,5},{3,7},{5,1},{7,3},{8,12},{10,14},{12... | collective-permute-start | bytes 98312 | tf_op jit(solution)/shard_map/ppermute | solution.py:61
  153.5 0.0 copy-done.5
  153.5 0.0 copy-done.6
  153.6 0.0 copy-done.7
  153.6 1.8 %shard_map.109 = bf16[256,256]{1,0:T(8,128)(2,1)} custom-call(f32[256,256]{1,0:T(8,128)} %get-tuple-element.55.here, bf16[256,256]{1,0:T(8,128)(2,1)} %copy-done.5, bf16[256,256]{1,0:T(8,128)(2,1)} %copy-done.6, bf16[256,256]{1,0:T(8,128)(2,1)} %copy-done.7), custom_call_target="tpu_custom_call" | custom-call | bytes 786432 | tf_op jit(solution)/shard_map/pallas_call | solution.py:43
  155.4 0.0 collective-permute-done.7.one
  155.4 0.0 collective-permute-done.6.three
  155.4 0.8 collective-permute-done.5.two
  156.2 0.0 copy-done.3
  156.2 1.2 shard_map.111
  157.4 0.0 all-to-all-done.6.arrived
  157.4 0.6 shard_map.112
  (2 shorter events, 0.0 us)
Async XLA Ops:
  19.8 28.2 %all-to-all-start.1 = ((f32[4,16,512]{2,1,0:T(8,128)}), f32[4,16,512]{2,1,0:T(8,128)S(1)}, u32[]{:S(2)}, u32[]{:S(2)}) async-start(f32[4,16,512]{2,1,0:T(8,128)} %shard_map.102), calls=%async_computation.1 | async-start | bytes 262144 | tf_op jit(solution)/shard_map/all_to_all | solution.py:56
  40.8 35.1 %copy-start.2 = (s32[5]{0:T(128)S(1)}, s32[5]{0:T(128)}, u32[]{:S(2)}) copy-start(s32[5]{0:T(128)} %stack.19.place) | copy-start | bytes 64
  99.5 4.2 %copy-start.8 = (bf16[4,256,256]{2,1,0:T(8,128)(2,1)S(1)}, bf16[4,256,256]{2,1,0:T(8,128)(2,1)}, u32[]{:S(2)}) copy-start(bf16[4,256,256]{2,1,0:T(8,128)(2,1)} %get-tuple-element.50) | copy-start | bytes 1572868
  99.5 35.7 %copy-start = (bf16[512,32]{0,1:T(8,128)(2,1)S(1)}, bf16[512,32]{0,1:T(8,128)(2,1)}, u32[]{:S(2)}) copy-start(bf16[512,32]{0,1:T(8,128)(2,1)} %param.7) | copy-start | bytes 98308
  99.5 35.7 %copy-start.1 = (bf16[32,256]{1,0:T(8,128)(2,1)S(1)}, bf16[32,256]{1,0:T(8,128)(2,1)}, u32[]{:S(2)}) copy-start(bf16[32,256]{1,0:T(8,128)(2,1)} %w_query.3) | copy-start | bytes 49156
  99.6 35.6 %all-to-all-start.5 = ((bf16[16,144,512]{2,1,0:T(8,128)(2,1)}), bf16[16,144,512]{2,1,0:T(8,128)(2,1)S(1)}, u32[]{:S(2)}, u32[]{:S(2)}) async-start(bf16[16,144,512]{2,1,0:T(8,128)(2,1)} %get-tuple-element.47), calls=%async_computation.5 | async-start | bytes 4718592 | tf_op jit(solution)/shard_map/all_to_all | solution.py:56
  103.7 11.0 %collective-permute-start = (bf16[4,256,256]{2,1,0:T(8,128)(2,1)S(1)}, bf16[4,256,256]{2,1,0:T(8,128)(2,1)S(1)}, u32[]{:S(2)}, u32[]{:S(2)}) collective-permute-start(bf16[4,256,256]{2,1,0:T(8,128)(2,1)S(1)} %copy-done.8), channel_id=1, source_target_pairs={{0,1},{1,0},{2,3},{3,2},{4,5},{5,4},{6,7},{7,6},{8,9},{9,8},{10,11... | collective-permute-start | bytes 1572872 | tf_op jit(solution)/shard_map/ppermute | solution.py:61
  114.7 0.8 copy-start.4
  115.5 40.7 %copy-start.3 = (s32[5]{0:T(128)S(1)}, s32[5]{0:T(128)}, u32[]{:S(2)}) copy-start(s32[5]{0:T(128)} %stack.19.place) | copy-start | bytes 64
  118.1 11.1 %collective-permute-start.1 = (bf16[256,256]{1,0:T(8,128)(2,1)}, bf16[256,256]{1,0:T(8,128)(2,1)S(1)}, u32[]{:S(2)}, u32[]{:S(2)}) collective-permute-start(bf16[256,256]{1,0:T(8,128)(2,1)} %get-tuple-element.52), channel_id=1, source_target_pairs={{0,4},{2,6},{4,0},{6,2},{1,5},{3,7},{5,1},{7,3},{8,12},{10,14},{12... | collective-permute-start | bytes 393224 | tf_op jit(solution)/shard_map/ppermute | solution.py:61
  122.6 8.4 %collective-permute-start.2 = (bf16[256,256]{1,0:T(8,128)(2,1)}, bf16[256,256]{1,0:T(8,128)(2,1)S(1)}, u32[]{:S(2)}, u32[]{:S(2)}) collective-permute-start(bf16[256,256]{1,0:T(8,128)(2,1)} %get-tuple-element.53), channel_id=1, source_target_pairs={{0,6},{2,4},{4,2},{6,0},{1,7},{3,5},{5,3},{7,1},{8,14},{10,12},{12... | collective-permute-start | bytes 393224 | tf_op jit(solution)/shard_map/ppermute | solution.py:61
  125.8 9.4 %collective-permute-start.3 = (bf16[256,256]{1,0:T(8,128)(2,1)}, bf16[256,256]{1,0:T(8,128)(2,1)S(1)}, u32[]{:S(2)}, u32[]{:S(2)}) collective-permute-start(bf16[256,256]{1,0:T(8,128)(2,1)} %get-tuple-element.54), channel_id=1, source_target_pairs={{0,2},{2,0},{4,6},{6,4},{1,3},{3,1},{5,7},{7,5},{8,10},{10,8},{12,... | collective-permute-start | bytes 393224 | tf_op jit(solution)/shard_map/ppermute | solution.py:61
  129.2 24.3 %copy-start.5 = (bf16[256,256]{1,0:T(8,128)(2,1)}, bf16[256,256]{1,0:T(8,128)(2,1)S(1)}, u32[]{:S(2)}) copy-start(bf16[256,256]{1,0:T(8,128)(2,1)S(1)} %collective-permute-done.1.one) | copy-start | bytes 393220
  131.0 22.5 %copy-start.6 = (bf16[256,256]{1,0:T(8,128)(2,1)}, bf16[256,256]{1,0:T(8,128)(2,1)S(1)}, u32[]{:S(2)}) copy-start(bf16[256,256]{1,0:T(8,128)(2,1)S(1)} %collective-permute-done.2.two) | copy-start | bytes 393220
  135.2 18.4 %copy-start.7 = (bf16[256,256]{1,0:T(8,128)(2,1)}, bf16[256,256]{1,0:T(8,128)(2,1)S(1)}, u32[]{:S(2)}) copy-start(bf16[256,256]{1,0:T(8,128)(2,1)S(1)} %collective-permute-done.3.three) | copy-start | bytes 393220
  136.4 21.1 %all-to-all-start.6 = ((bf16[4,32,512]{2,1,0:T(8,128)(2,1)}), bf16[4,32,512]{2,1,0:T(8,128)(2,1)S(1)}, u32[]{:S(2)}, u32[]{:S(2)}) async-start(bf16[4,32,512]{2,1,0:T(8,128)(2,1)} %get-tuple-element.62), calls=%async_computation.6 | async-start | bytes 262144 | tf_op jit(solution)/shard_map/all_to_all | solution.py:56
  139.7 5.4 %collective-permute-start.4 = (bf16[32,512]{1,0:T(8,128)(2,1)S(1)}, bf16[32,512]{1,0:T(8,128)(2,1)S(1)}, u32[]{:S(2)}, u32[]{:S(2)}) collective-permute-start(bf16[32,512]{1,0:T(8,128)(2,1)S(1)} %get-tuple-element.60), channel_id=1, source_target_pairs={{0,1},{1,0},{2,3},{3,2},{4,5},{5,4},{6,7},{7,6},{8,9},{9,8},{10,11... | collective-permute-start | bytes 98312 | tf_op jit(solution)/shard_map/ppermute | solution.py:61
  145.1 10.3 %collective-permute-start.7 = (bf16[32,512]{1,0:T(8,128)(2,1)S(1)}, bf16[32,512]{1,0:T(8,128)(2,1)S(1)}, u32[]{:S(2)}, u32[]{:S(2)}) collective-permute-start(bf16[32,512]{1,0:T(8,128)(2,1)S(1)} %add_convert_fusion.own), channel_id=1, source_target_pairs={{0,2},{2,0},{4,6},{6,4},{1,3},{3,1},{5,7},{7,5},{8,10},{10,8},{12,... | collective-permute-start | bytes 98312 | tf_op jit(solution)/shard_map/ppermute | solution.py:61
  147.1 8.3 %collective-permute-start.6 = (bf16[32,512]{1,0:T(8,128)(2,1)S(1)}, bf16[32,512]{1,0:T(8,128)(2,1)S(1)}, u32[]{:S(2)}, u32[]{:S(2)}) collective-permute-start(bf16[32,512]{1,0:T(8,128)(2,1)S(1)} %add_convert_fusion.own), channel_id=1, source_target_pairs={{0,6},{2,4},{4,2},{6,0},{1,7},{3,5},{5,3},{7,1},{8,14},{10,12},{12... | collective-permute-start | bytes 98312 | tf_op jit(solution)/shard_map/ppermute | solution.py:61
  150.7 5.6 %collective-permute-start.5 = (bf16[32,512]{1,0:T(8,128)(2,1)S(1)}, bf16[32,512]{1,0:T(8,128)(2,1)S(1)}, u32[]{:S(2)}, u32[]{:S(2)}) collective-permute-start(bf16[32,512]{1,0:T(8,128)(2,1)S(1)} %add_convert_fusion.own), channel_id=1, source_target_pairs={{0,4},{2,6},{4,0},{6,2},{1,5},{3,7},{5,1},{7,3},{8,12},{10,14},{12... | collective-permute-start | bytes 98312 | tf_op jit(solution)/shard_map/ppermute | solution.py:61
